TPU v7x, 32 devices: a whole 2x2x4 slice. The times are simulated.
32 devices in a mesh: expert: 8 (over y, x, core), hidden: 4 (over z).
Axes of the slice: x: 2, y: 2, z: 4, core: 2. Of those that a mesh axis runs over, the one named last changes fastest.
Arguments:
- tokens: bfloat16 [16384, 1024], P(('expert', 'hidden')), may hold values from -6 to 6
- gain_one: float32 [1024], replicated, may hold values from 0.5 to 1.5
- w_query: bfloat16 [1024, 1024], replicated, may hold values from -0.1875 to 0.1875
- w_key: bfloat16 [1024, 1024], replicated, may hold values from -0.1875 to 0.1875
- w_value: bfloat16 [1024, 1024], replicated, may hold values from -0.1875 to 0.1875
- w_out: bfloat16 [1024, 1024], replicated, may hold values from -1.5 to 1.5
- bias_table: float32 [32, 16], replicated, may hold values from -4 to 4
- gain_two: float32 [1024], replicated, may hold values from 0.5 to 1.5
- w_router: float32 [1024, 16], replicated, may hold values from -0.1875 to 0.1875
- w_gate: bfloat16 [16, 1024, 2816], P('expert', None, 'hidden'), may hold values from -0.1875 to 0.1875
- w_up: bfloat16 [16, 1024, 2816], P('expert', None, 'hidden'), may hold values from -0.1875 to 0.1875
- w_down: bfloat16 [16, 2816, 1024], P('expert', 'hidden'), may hold values from -0.109375 to 0.109375
- routes: int32 [16384, 2], P(('expert', 'hidden')), may hold values from 0 to 15, all different within a row; in each aligned block of 256 rows (0 to 255, 256 to 511, ...) at most 40 rows name the same one
- cotangent: bfloat16 [16384, 1024], P(('expert', 'hidden')), may hold values from -6 to 6
Outputs:
- block_out: bfloat16 [16384, 1024], P(('expert', 'hidden'))
- tokens_grad: float32 [16384, 1024], P(('expert', 'hidden'))
- gain_one_grad: float32 [1024], replicated
- query_grad: float32 [1024, 1024], replicated
- key_grad: float32 [1024, 1024], replicated
- value_grad: float32 [1024, 1024], replicated
- w_out_grad: float32 [1024, 1024], replicated
- bias_table_grad: float32 [32, 16], replicated
- gain_two_grad: float32 [1024], replicated
- router_grad: float32 [1024, 16], replicated
- gate_grad: float32 [16, 1024, 2816], P('expert', None, 'hidden')
- up_grad: float32 [16, 1024, 2816], P('expert', None, 'hidden')
- down_grad: float32 [16, 2816, 1024], P('expert', 'hidden')
Inputs may be any that keep to these rules, and one draw needn't show every extreme that they name: `routes`: each row names two different experts; in each aligned block of 256 rows (one micro-batch of one device) no expert is named by more than 40 rows, a bound that some block reaches.
All inputs are finite; a program needn't handle non-finite values.
Results may differ from a plain program's by a relative error of at most 0.015.
Values may be sent and summed in bfloat16 or wider, within the bound.
A program may use at most 384 MiB of HBM per device.

v0:
```python
import jax
import jax.numpy as jnp
from jax import lax
from jax.sharding import PartitionSpec as P

D = 1024
HEADS = 16
HEAD_DIM = 64
BUCKETS = 32
LEN = 512
MICRO = 2
MB_TOK = 256


eps = 1e-06
precise = lax.Precision.HIGHEST
thresholds = (12, 16, 23, 32, 46, 64, 91)


def bucket_ids(length):
    position = jnp.arange(length, dtype=jnp.int32)
    offset = position[None, :] - position[:, None]
    distance = jnp.abs(offset)
    far_bucket = 8 + sum(((distance >= threshold).astype(jnp.int32) for threshold in thresholds))
    near_bucket = jnp.where(distance < 8, distance, far_bucket)
    return near_bucket + 16 * (offset > 0).astype(jnp.int32)


def contract_last(matrix_a, matrix_b, mode=None):
    return lax.dot_general(
        matrix_a,
        matrix_b,
        (((1,), (1,)), ((), ())),
        precision=mode,
        preferred_element_type=jnp.float32,
    )


def contract_first(matrix_a, matrix_b, mode=None):
    return lax.dot_general(
        matrix_a,
        matrix_b,
        (((0,), (0,)), ((), ())),
        precision=mode,
        preferred_element_type=jnp.float32,
    )


def slot_table(route_block, experts_all, capacity):
    flat_routes = route_block.reshape(-1)
    route_hits = (flat_routes[:, None] == jnp.arange(experts_all, dtype=jnp.int32)[None, :]).astype(
        jnp.int32
    )
    slot_rank = jnp.sum((jnp.cumsum(route_hits, axis=0) - 1) * route_hits, axis=1)
    target = slot_rank * experts_all + flat_routes
    return (target[:, None] == jnp.arange(capacity * experts_all, dtype=jnp.int32)[None, :]).astype(
        jnp.bfloat16
    )


def glu_product(gate_in, up_in):
    return jax.nn.gelu(gate_in, approximate=True) * up_in


def glu_back(gate_pre, up_pre, grad_act):
    _, pullback = jax.vjp(glu_product, gate_pre, up_pre)
    grad_gate, grad_up = pullback(grad_act)
    return (grad_gate.astype(jnp.bfloat16), grad_up.astype(jnp.bfloat16))


def per_device(
    tokens,
    gain_one,
    w_query,
    w_key,
    w_value,
    w_out,
    bias_table,
    gain_two,
    w_router,
    w_gate,
    w_up,
    w_down,
    routes,
    cotangent,
):
    experts_all = w_router.shape[1]
    capacity = 10 * MB_TOK // (4 * experts_all)
    scaling = HEAD_DIM ** (-0.5)
    bucket_hot = (bucket_ids(LEN)[:, :, None] == jnp.arange(BUCKETS, dtype=jnp.int32)).astype(
        jnp.float32
    )
    inputs = tokens.astype(jnp.float32)
    inv_one = lax.rsqrt(jnp.mean(inputs * inputs, axis=-1, keepdims=True) + eps)
    normed_one = (inputs * inv_one * gain_one).astype(jnp.bfloat16)
    query_rows = jnp.dot(normed_one, w_query, preferred_element_type=jnp.float32).astype(
        jnp.bfloat16
    )
    key_rows = jnp.dot(normed_one, w_key, preferred_element_type=jnp.float32).astype(jnp.bfloat16)
    value_rows = jnp.dot(normed_one, w_value, preferred_element_type=jnp.float32).astype(
        jnp.bfloat16
    )
    query_heads = query_rows.reshape(LEN, HEADS, HEAD_DIM)
    key_heads = key_rows.reshape(LEN, HEADS, HEAD_DIM)
    value_heads = value_rows.reshape(LEN, HEADS, HEAD_DIM)
    bias_rows = jnp.einsum("ijb,bh->hij", bucket_hot, bias_table, precision=precise)

    def score_of():
        raw = jnp.einsum("qhd,khd->hqk", query_heads, key_heads, preferred_element_type=jnp.float32)
        return raw * scaling + bias_rows

    scores = score_of()
    row_peak = jnp.max(scores, axis=-1, keepdims=True)
    exp_terms = jnp.exp(scores - row_peak)
    row_total = jnp.sum(exp_terms, axis=-1, keepdims=True)
    log_total = row_peak + jnp.log(row_total)
    soft_low = (exp_terms / row_total).astype(jnp.bfloat16)
    mixed_rows = jnp.einsum(
        "hqk,khd->qhd", soft_low, value_heads, preferred_element_type=jnp.float32
    )
    mixed_rows = mixed_rows.reshape(LEN, D).astype(jnp.bfloat16)
    hidden = inputs + jnp.dot(mixed_rows, w_out, preferred_element_type=jnp.float32)
    inv_two = lax.rsqrt(jnp.mean(hidden * hidden, axis=-1, keepdims=True) + eps)
    normed_two = hidden * inv_two * gain_two
    sent = normed_two.astype(jnp.bfloat16)
    logits = jnp.dot(normed_two, w_router, precision=precise)
    route_hot = (routes[:, :, None] == jnp.arange(experts_all, dtype=jnp.int32)).astype(jnp.float32)
    chosen = jnp.sum(route_hot * logits[:, None, :], axis=-1)
    gate_values = jax.nn.softmax(chosen, axis=-1)
    tables = []
    kept_state = []
    picked_all = []
    for micro_index in range(MICRO):
        row_start = micro_index * MB_TOK
        slot_hot = slot_table(routes[row_start : row_start + MB_TOK], experts_all, capacity)
        copies = jnp.repeat(sent[row_start : row_start + MB_TOK], 2, axis=0)
        outgoing = jnp.einsum("rs,rd->sd", slot_hot, copies, preferred_element_type=jnp.float32)
        outgoing = outgoing.astype(jnp.bfloat16).reshape(capacity, experts_all, D)
        received = lax.all_to_all(outgoing, "expert", split_axis=1, concat_axis=0, tiled=True)
        everyone = lax.all_gather(received, "hidden", axis=0, tiled=True)
        gate_pre = jnp.einsum("rxd,xdf->rxf", everyone, w_gate, preferred_element_type=jnp.float32)
        up_pre = jnp.einsum("rxd,xdf->rxf", everyone, w_up, preferred_element_type=jnp.float32)
        activation = glu_product(gate_pre, up_pre).astype(jnp.bfloat16)
        partial_sum = jnp.einsum(
            "rxf,xfd->rxd", activation, w_down, preferred_element_type=jnp.float32
        )
        result = lax.psum_scatter(
            partial_sum.astype(jnp.bfloat16), "hidden", scatter_dimension=0, tiled=True
        )
        kept_state.append((everyone, gate_pre, up_pre, activation))
        came_back = lax.all_to_all(
            result, "expert", split_axis=0, concat_axis=1, tiled=True
        ).reshape(capacity * experts_all, D)
        picked_all.append(
            jnp.einsum(
                "rs,sd->rd", slot_hot, came_back, preferred_element_type=jnp.float32
            ).reshape(MB_TOK, 2, D)
        )
        tables.append(slot_hot)
    picked = jnp.concatenate(picked_all, axis=0)
    block_out = (hidden + jnp.sum(gate_values[:, :, None] * picked, axis=1)).astype(jnp.bfloat16)
    grad_out = cotangent.astype(jnp.float32)
    grad_gates = jnp.sum(grad_out[:, None, :] * picked, axis=-1)
    grad_chosen = gate_values * (
        grad_gates - jnp.sum(gate_values * grad_gates, axis=-1, keepdims=True)
    )
    grad_logits = jnp.sum(route_hot * grad_chosen[:, :, None], axis=1)
    router_grad = contract_first(normed_two, grad_logits, precise)
    grad_normed_two = contract_last(grad_logits, w_router, precise)
    grad_returned = (
        (gate_values[:, :, None] * grad_out[:, None, :]).astype(jnp.bfloat16).reshape(LEN * 2, D)
    )
    acc_gate = jnp.zeros(w_gate.shape, jnp.float32)
    acc_up = jnp.zeros(w_up.shape, jnp.float32)
    acc_down = jnp.zeros(w_down.shape, jnp.float32)
    grad_sent_parts = []
    for micro_index in range(MICRO):
        row_start = micro_index * MB_TOK
        slot_hot = tables[micro_index]
        rows_in = grad_returned[2 * row_start : 2 * (row_start + MB_TOK)]
        outgoing_grad = jnp.einsum(
            "rs,rd->sd", slot_hot, rows_in, preferred_element_type=jnp.float32
        )
        outgoing_grad = outgoing_grad.astype(jnp.bfloat16).reshape(capacity, experts_all, D)
        arrived = lax.all_to_all(outgoing_grad, "expert", split_axis=1, concat_axis=0, tiled=True)
        source_rows, gate_pre, up_pre, activation = kept_state[micro_index]
        grad_all = lax.all_gather(arrived, "hidden", axis=0, tiled=True)
        grad_act = jnp.einsum("rxd,xfd->rxf", grad_all, w_down, preferred_element_type=jnp.float32)
        grad_gate, grad_up = glu_back(gate_pre, up_pre, grad_act)
        acc_down = acc_down + jnp.einsum(
            "rxf,rxd->xfd", activation, grad_all, preferred_element_type=jnp.float32
        )
        acc_gate = acc_gate + jnp.einsum(
            "rxd,rxf->xdf", source_rows, grad_gate, preferred_element_type=jnp.float32
        )
        acc_up = acc_up + jnp.einsum(
            "rxd,rxf->xdf", source_rows, grad_up, preferred_element_type=jnp.float32
        )
        input_parts = jnp.einsum(
            "rxf,xdf->rxd", grad_gate, w_gate, preferred_element_type=jnp.float32
        )
        input_parts = input_parts + jnp.einsum(
            "rxf,xdf->rxd", grad_up, w_up, preferred_element_type=jnp.float32
        )
        returned = lax.psum_scatter(
            input_parts.astype(jnp.bfloat16), "hidden", scatter_dimension=0, tiled=True
        )
        gone_home = lax.all_to_all(
            returned, "expert", split_axis=0, concat_axis=1, tiled=True
        ).reshape(capacity * experts_all, D)
        token_rows = jnp.einsum(
            "rs,sd->rd", slot_hot, gone_home, preferred_element_type=jnp.float32
        )
        grad_sent_parts.append(jnp.sum(token_rows.reshape(MB_TOK, 2, D), axis=1))
    gate_grad, up_grad, down_grad = (acc_gate, acc_up, acc_down)
    grad_normed_two = grad_normed_two + jnp.concatenate(grad_sent_parts, axis=0)
    gain_two_grad = jnp.sum(grad_normed_two * hidden * inv_two, axis=0)
    scaled_two = grad_normed_two * gain_two
    grad_hidden = (
        grad_out
        + inv_two * scaled_two
        - hidden * inv_two**3 * jnp.mean(scaled_two * hidden, axis=-1, keepdims=True)
    )
    grad_branch = grad_hidden.astype(jnp.bfloat16)
    w_out_grad = contract_first(mixed_rows, grad_branch)
    grad_mixed = (
        contract_last(grad_branch, w_out).astype(jnp.bfloat16).reshape(LEN, HEADS, HEAD_DIM)
    )
    soft_again = jnp.exp(score_of() - log_total)
    soft_again_low = soft_again.astype(jnp.bfloat16)
    grad_value_heads = jnp.einsum(
        "hqk,qhd->khd", soft_again_low, grad_mixed, preferred_element_type=jnp.float32
    )
    grad_value_rows = grad_value_heads.astype(jnp.bfloat16).reshape(LEN, D)
    grad_soft = jnp.einsum(
        "qhd,khd->hqk", grad_mixed, value_heads, preferred_element_type=jnp.float32
    )
    grad_scores = soft_again * (grad_soft - jnp.sum(soft_again * grad_soft, axis=-1, keepdims=True))
    grad_scores = grad_scores.astype(jnp.bfloat16)
    bias_table_grad = jnp.einsum(
        "hij,ijb->bh", grad_scores.astype(jnp.float32), bucket_hot, precision=precise
    )
    grad_query_rows = (
        jnp.einsum("hqk,khd->qhd", grad_scores, key_heads, preferred_element_type=jnp.float32)
        * scaling
    )
    grad_query_rows = grad_query_rows.astype(jnp.bfloat16).reshape(LEN, D)
    grad_key_rows = (
        jnp.einsum("hqk,qhd->khd", grad_scores, query_heads, preferred_element_type=jnp.float32)
        * scaling
    )
    grad_key_rows = grad_key_rows.astype(jnp.bfloat16).reshape(LEN, D)
    query_grad = contract_first(normed_one, grad_query_rows)
    key_grad = contract_first(normed_one, grad_key_rows)
    value_grad = contract_first(normed_one, grad_value_rows)
    grad_normed_one = (
        contract_last(grad_query_rows, w_query)
        + contract_last(grad_key_rows, w_key)
        + contract_last(grad_value_rows, w_value)
    )
    gain_one_grad = jnp.sum(grad_normed_one * inputs * inv_one, axis=0)
    scaled_one = grad_normed_one * gain_one
    tokens_grad = (
        grad_hidden
        + inv_one * scaled_one
        - inputs * inv_one**3 * jnp.mean(scaled_one * inputs, axis=-1, keepdims=True)
    )
    summed = lax.psum(
        (
            query_grad,
            key_grad,
            value_grad,
            w_out_grad,
            bias_table_grad,
            gain_one_grad,
            gain_two_grad,
            router_grad,
        ),
        ("expert", "hidden"),
    )
    return (
        block_out,
        tokens_grad,
        summed[5],
        summed[0],
        summed[1],
        summed[2],
        summed[3],
        summed[4],
        summed[6],
        summed[7],
        gate_grad,
        up_grad,
        down_grad,
    )


def solution(mesh):
    in_specs = (
        P(("expert", "hidden"), None),
        P(),
        P(),
        P(),
        P(),
        P(),
        P(),
        P(),
        P(),
        P("expert", None, "hidden"),
        P("expert", None, "hidden"),
        P("expert", "hidden", None),
        P(("expert", "hidden"), None),
        P(("expert", "hidden"), None),
    )
    out_specs = (
        P(("expert", "hidden"), None),
        P(("expert", "hidden"), None),
        P(),
        P(),
        P(),
        P(),
        P(),
        P(),
        P(),
        P(),
        P("expert", None, "hidden"),
        P("expert", None, "hidden"),
        P("expert", "hidden", None),
    )
    return jax.shard_map(
        per_device, mesh=mesh, in_specs=in_specs, out_specs=out_specs, check_vma=False
    )
```

profile of v0, /device:TPU:1, one launch (start us, length us, event | category | flops | bytes accessed | tf_op | source)
XLA Modules:
  0.0 1342.0 jit_solution(17821647731350769313)
XLA Ops:
  25.5 14.8 %fusion.1 = f32[512,512,16]{1,2,0:T(8,128)} fusion(s32[512,512]{1,0:T(8,128)} %fusion.60, f32[32,16]{0,1:T(8,128)S(1)} %copy-done.53), kind=kOutput, calls=%fused_computation.2 | convolution fusion | flops 1619001344 | bytes 17827840 | tf_op jit(solution)/shard_map/ijb,bh->hij/dot_general | solution.py:106
  40.3 19.3 %copy.121 = f32[512,512,16]{0,1,2:T(8,128)} copy(f32[512,512,16]{1,2,0:T(8,128)} %fusion.1) | data formatting | bytes 33554432 | tf_op jit(solution)/shard_map/ijb,bh->hij/dot_general | solution.py:106
  66.0 14.6 %fusion.108 = (f32[16,512]{1,0:T(8,128)S(1)}, f32[16,512,512]{1,2,0:T(8,128)}) fusion(f32[512,512,16]{0,1,2:T(8,128)} %copy.121, bf16[512,16,64]{0,2,1:T(8,128)(2,1)} %bitcast.248, bf16[512,16,64]{0,2,1:T(8,128)(2,1)} %bitcast.246), kind=kOutput, calls=%fused_computation.188 | convolution fusion | flops 549445632 | bytes 35684352 | tf_op jit(solution)/shard_map/qhd,khd->hqk/dot_general | solution.py:109
  80.6 8.4 fusion.4
  89.0 16.2 %fusion.47 = bf16[16,64,512]{2,1,0:T(8,128)(2,1)S(1)} fusion(bf16[512,16,64]{0,2,1:T(8,128)(2,1)S(1)} %bitcast.270, f32[16,512,512]{1,2,0:T(8,128)} %get-tuple-element.50, f32[16,512]{1,0:T(8,128)S(1)} %fusion.4, f32[16,512]{1,0:T(8,128)S(1)} %get-tuple-element.49), kind=kOutput, calls=%fused_computation.99 | convolution fusion | flops 549978112 | bytes 18939904 | tf_op jit(solution)/shard_map/hqk,khd->qhd/dot_general | solution.py:118
  119.2 21.9 %all_to_all.132 = bf16[40,16,1024]{2,0,1:T(8,128)(2,1)S(1)} all-to-all(bf16[40,16,1024]{2,0,1:T(8,128)(2,1)S(1)} %copy.126), channel_id=1, replica_groups=mesh['expert'=8,'hidden'=4] {'expert'}, dimensions={1} | all-to-all | bytes 2621440 | tf_op jit(solution)/shard_map/all_to_all | solution.py:139
  159.9 20.7 %all_to_all.133 = bf16[40,16,1024]{2,0,1:T(8,128)(2,1)S(1)} all-to-all(bf16[40,16,1024]{2,0,1:T(8,128)(2,1)S(1)} %copy.138), channel_id=1, replica_groups=mesh['expert'=8,'hidden'=4] {'expert'}, dimensions={1} | all-to-all | bytes 2621440 | tf_op jit(solution)/shard_map/all_to_all | solution.py:185
  201.1 20.6 %all_to_all.134 = bf16[40,16,1024]{2,0,1:T(8,128)(2,1)S(1)} all-to-all(bf16[40,16,1024]{2,0,1:T(8,128)(2,1)S(1)} %copy.133), channel_id=1, replica_groups=mesh['expert'=8,'hidden'=4] {'expert'}, dimensions={1} | all-to-all | bytes 2621440 | tf_op jit(solution)/shard_map/all_to_all | solution.py:139
  231.4 20.5 %all_to_all.135 = bf16[40,16,1024]{2,0,1:T(8,128)(2,1)S(1)} all-to-all(bf16[40,16,1024]{2,0,1:T(8,128)(2,1)S(1)} %copy.143), channel_id=1, replica_groups=mesh['expert'=8,'hidden'=4] {'expert'}, dimensions={1} | all-to-all | bytes 2621440 | tf_op jit(solution)/shard_map/all_to_all | solution.py:185
  253.2 10.3 fusion.109
  269.9 69.4 %all-gather.9.cloned.1.call-done = bf16[1280,2,1024]{2,0,1:T(8,128)(2,1)} async-done(((bf16[320,2,1024]{2,0,1:T(8,128)(2,1)}), bf16[1280,2,1024]{2,0,1:T(8,128)(2,1)}) %all-gather.9.cloned.1.call-update) | async-done | bytes 5242896 | tf_op jit(solution)/shard_map/all_gather | solution.py:187
  339.3 15.5 %fusion.25 = (bf16[1280,2,704]{0,2,1:T(8,128)(2,1)}, bf16[1280,2,704]{0,2,1:T(8,128)(2,1)}, bf16[1280,2,704]{0,2,1:T(8,128)(2,1)S(1)}) fusion(f32[2,1280,704]{1,2,0:T(8,128)} %fusion.109, f32[2,1280,704]{1,2,0:T(8,128)} %fusion.110, bf16[1280,2,1024]{2,0,1:T(8,128)(2,1)} %all-gather.9.cloned.1.call-done, bf16[2,704,1024]{2,1,0:T(8,128)(2,1)S(1)} %copy-done), kind=kOutput, calls=%fused_computation.41 | convolution fusion | flops 3737845760 | bytes 33357824 | tf_op jit(solution)/shard_map/rxd,xfd->rxf/dot_general | solution.py:188
  362.7 75.2 %all-gather.7.cloned.1.call-done = bf16[1280,2,1024]{2,0,1:T(8,128)(2,1)} async-done(((bf16[320,2,1024]{2,0,1:T(8,128)(2,1)}), bf16[1280,2,1024]{2,0,1:T(8,128)(2,1)}) %all-gather.7.cloned.1.call-update) | async-done | bytes 5242896 | tf_op jit(solution)/shard_map/all_gather | solution.py:140
  437.9 10.6 fusion.111
  454.7 81.7 %all-gather.11.cloned.1.call-done = bf16[1280,2,1024]{2,0,1:T(8,128)(2,1)} async-done(((bf16[320,2,1024]{2,0,1:T(8,128)(2,1)}), bf16[1280,2,1024]{2,0,1:T(8,128)(2,1)}) %all-gather.11.cloned.1.call-update) | async-done | bytes 5242896 | tf_op jit(solution)/shard_map/all_gather | solution.py:187
  536.3 15.5 %fusion.24 = (bf16[1280,2,704]{0,2,1:T(8,128)(2,1)}, bf16[1280,2,704]{0,2,1:T(8,128)(2,1)}, bf16[1280,2,704]{0,2,1:T(8,128)(2,1)S(1)}) fusion(f32[2,1280,704]{1,2,0:T(8,128)} %fusion.111, f32[2,1280,704]{1,2,0:T(8,128)} %fusion.112, bf16[1280,2,1024]{2,0,1:T(8,128)(2,1)} %all-gather.11.cloned.1.call-done, bf16[2,704,1024]{2,1,0:T(8,128)(2,1)S(1)} %copy-done), kind=kOutput, calls=%fused_computation.38 | convolution fusion | flops 3737845760 | bytes 33357824 | tf_op jit(solution)/shard_map/rxd,xfd->rxf/dot_general | solution.py:188
  561.7 9.4 fusion.113
  571.0 8.5 fusion.34
  579.7 9.2 fusion.114
  588.8 8.5 fusion.35
  597.4 33.2 %reduce-scatter.5.cloned.1.call-done = bf16[320,2,1024]{2,0,1:T(8,128)(2,1)} async-done(((bf16[1280,2,1024]{2,0,1:T(8,128)(2,1)}), bf16[320,2,1024]{2,0,1:T(8,128)(2,1)}) %reduce-scatter.5.cloned.1.call-update) | async-done | bytes 1310736 | tf_op jit(solution)/shard_map/reduce_scatter | solution.py:147
  639.0 88.6 %reduce-scatter.7.cloned.1.call-done = bf16[320,2,1024]{2,0,1:T(8,128)(2,1)} async-done(((bf16[1280,2,1024]{2,0,1:T(8,128)(2,1)}), bf16[320,2,1024]{2,0,1:T(8,128)(2,1)}) %reduce-scatter.7.cloned.1.call-update) | async-done | bytes 1310736 | tf_op jit(solution)/shard_map/reduce_scatter | solution.py:147
  735.7 89.0 %reduce-scatter.9.cloned.1.call-done = bf16[320,2,1024]{2,0,1:T(8,128)(2,1)} async-done(((bf16[1280,2,1024]{2,0,1:T(8,128)(2,1)}), bf16[320,2,1024]{2,0,1:T(8,128)(2,1)}) %reduce-scatter.9.cloned.1.call-update) | async-done | bytes 1310736 | tf_op jit(solution)/shard_map/reduce_scatter | solution.py:205
  833.8 88.1 %reduce-scatter.11.cloned.1.call-done = bf16[320,2,1024]{2,0,1:T(8,128)(2,1)} async-done(((bf16[1280,2,1024]{2,0,1:T(8,128)(2,1)}), bf16[320,2,1024]{2,0,1:T(8,128)(2,1)}) %reduce-scatter.11.cloned.1.call-update) | async-done | bytes 1310736 | tf_op jit(solution)/shard_map/reduce_scatter | solution.py:205
  986.9 11.4 multiply_reduce_fusion
  998.3 11.8 multiply_convert_fusion
  1015.0 8.9 fusion.48
  1042.0 8.4 fusion.119
  1054.5 8.0 convolution_add_fusion.2
  1075.9 15.6 %copy.151 = bf16[16,512,512]{2,0,1:T(8,128)(2,1)} copy(bf16[16,512,512]{1,2,0:T(8,128)(2,1)} %copy-done.2) | data formatting | bytes 16777216 | tf_op jit(solution)/shard_map/convert_element_type | solution.py:239
  1104.9 42.2 %all-reduce = (f32[1024]{0:T(1024)}, f32[32,16]{0,1:T(8,128)}, f32[1024]{0:T(1024)}) all-reduce(f32[1024]{0:T(1024)S(1)} %get-tuple-element.17, f32[32,16]{0,1:T(8,128)S(1)} %fusion.59, f32[1024]{0:T(1024)S(1)} %get-tuple-element.13), channel_id=1, replica_groups=mesh['expert'=8,'hidden'=4] {'expert','hidden'}, use_global_device_ids=true, to_apply=%region_27.28 | all-reduce | flops 2560 | bytes 20480 | tf_op jit(solution)/shard_map/psum | solution.py:268
  1151.0 169.3 %all-reduce.4.cloned.1.call-done = (f32[1024,1024]{1,0:T(8,128)}, f32[1024,1024]{1,0:T(8,128)}, f32[1024,1024]{1,0:T(8,128)}, f32[1024,1024]{1,0:T(8,128)}, f32[1024,16]{0,1:T(8,128)}) async-done(((f32[1024,1024]{1,0:T(8,128)}, f32[1024,1024]{1,0:T(8,128)}, f32[1024,1024]{1,0:T(8,128)}, f32[1024,1024]{1,0:T(8,128)}, f32[1024,16]{0,1:T(8,128)}), (f32[1024,1024]{1,0:T(8,128)}, f32[1024,1024]{1,0:T(8,128)}, ...) | async-done | bytes 16842768 | tf_op jit(solution)/shard_map/psum | solution.py:268
  (313 shorter events, 281.9 us)
Async XLA Ops:
  7.2 332.1 %copy-start = (bf16[2,704,1024]{2,1,0:T(8,128)(2,1)S(1)}, bf16[2,704,1024]{2,1,0:T(8,128)(2,1)}, u32[]{:S(2)}) copy-start(bf16[2,704,1024]{2,1,0:T(8,128)(2,1)} %param.25) | copy-start | bytes 8650756
  7.2 246.0 %all-gather.5.cloned.1.call-start = ((), (), s32[]{:S(2)}) async-start(), calls=%async_computation.12 | async-start | bytes 6553600 | tf_op jit(solution)/shard_map/all_gather | solution.py:140
  12.5 47.1 %copy-start.49 = (f32[512]{0:T(512)}, f32[512]{0:T(512)S(1)}, u32[]{:S(2)}) copy-start(f32[512]{0:T(512)S(1)} %get-tuple-element.42) | copy-start | bytes 6148
  89.0 16.3 %copy-start.39 = (f32[16,512]{1,0:T(8,128)}, f32[16,512]{1,0:T(8,128)S(1)}, u32[]{:S(2)}) copy-start(f32[16,512]{1,0:T(8,128)S(1)} %fusion.4) | copy-start | bytes 98308
  89.0 16.3 %copy-start.7 = (bf16[512,1024]{1,0:T(8,128)(2,1)S(1)}, bf16[512,1024]{1,0:T(8,128)(2,1)}, u32[]{:S(2)}) copy-start(bf16[512,1024]{1,0:T(8,128)(2,1)} %param.14) | copy-start | bytes 3145732
  89.0 16.3 %copy-start.29 = (bf16[1024,1024]{1,0:T(8,128)(2,1)S(1)}, bf16[1024,1024]{1,0:T(8,128)(2,1)}, u32[]{:S(2)}) copy-start(bf16[1024,1024]{1,0:T(8,128)(2,1)} %param.19) | copy-start | bytes 6291460
  142.2 197.0 %all-gather.9.cloned.1.call-start = ((), (), s32[]{:S(2)}) async-start(), calls=%async_computation.16 | async-start | bytes 6553600 | tf_op jit(solution)/shard_map/all_gather | solution.py:187
  181.8 256.1 %all-gather.7.cloned.1.call-start = ((), (), s32[]{:S(2)}) async-start(), calls=%async_computation.14 | async-start | bytes 6553600 | tf_op jit(solution)/shard_map/all_gather | solution.py:140
  222.9 313.4 %all-gather.11.cloned.1.call-start = ((), (), s32[]{:S(2)}) async-start(), calls=%async_computation.18 | async-start | bytes 6553600 | tf_op jit(solution)/shard_map/all_gather | solution.py:187
  253.1 377.5 %reduce-scatter.5.cloned.1.call-start = ((), (), s32[]{:S(2)}) async-start(), calls=%async_computation.13 | async-start | bytes 6553600 | tf_op jit(solution)/shard_map/reduce_scatter | solution.py:147
  362.7 364.9 %reduce-scatter.7.cloned.1.call-start = ((), (), s32[]{:S(2)}) async-start(), calls=%async_computation.15 | async-start | bytes 6553600 | tf_op jit(solution)/shard_map/reduce_scatter | solution.py:147
  437.9 10.6 copy-start.61
  559.8 265.0 %reduce-scatter.9.cloned.1.call-start = ((), (), s32[]{:S(2)}) async-start(), calls=%async_computation.17 | async-start | bytes 6553600 | tf_op jit(solution)/shard_map/reduce_scatter | solution.py:205
  579.6 342.4 %reduce-scatter.11.cloned.1.call-start = ((), (), s32[]{:S(2)}) async-start(), calls=%async_computation.19 | async-start | bytes 6553600 | tf_op jit(solution)/shard_map/reduce_scatter | solution.py:205
  634.3 97.0 %all-to-all-start.1 = ((bf16[320,2,1024]{2,1,0:T(2,128)(2,1)}), bf16[320,2,1024]{2,1,0:T(2,128)(2,1)S(1)}, u32[]{:S(2)}, u32[]{:S(2)}) async-start(bf16[320,2,1024]{2,1,0:T(2,128)(2,1)} %copy.128), calls=%async_computation.2 | async-start | bytes 2621440 | tf_op jit(solution)/shard_map/all_to_all | solution.py:151
  731.3 101.9 %copy-start.56 = (s32[512]{0:T(512)S(1)}, s32[512]{0:T(512)}, u32[]{:S(2)}) copy-start(s32[512]{0:T(512)} %get-tuple-element.45) | copy-start | bytes 6148
  731.3 102.1 %copy-start.28 = (s32[256,2]{1,0:T(8,128)S(1)}, s32[256,2]{1,0:T(8,128)}, u32[]{:S(2)}) copy-start(s32[256,2]{1,0:T(8,128)} %copy-done.27) | copy-start | bytes 6148
  731.3 97.2 %all-to-all-start.3 = ((bf16[320,2,1024]{2,1,0:T(2,128)(2,1)}), bf16[320,2,1024]{2,1,0:T(2,128)(2,1)S(1)}, u32[]{:S(2)}, u32[]{:S(2)}) async-start(bf16[320,2,1024]{2,1,0:T(2,128)(2,1)} %copy.135), calls=%async_computation.5 | async-start | bytes 2621440 | tf_op jit(solution)/shard_map/all_to_all | solution.py:151
  735.7 98.0 %copy-start.36 = (f32[16,512]{1,0:T(8,128)S(1)}, f32[16,512]{1,0:T(8,128)}, u32[]{:S(2)}) copy-start(f32[16,512]{1,0:T(8,128)} %copy-done.35) | copy-start | bytes 98308
  735.7 98.0 %copy-start.40 = (f32[16,512]{1,0:T(8,128)S(1)}, f32[16,512]{1,0:T(8,128)}, u32[]{:S(2)}) copy-start(f32[16,512]{1,0:T(8,128)} %copy-done.39) | copy-start | bytes 98308
  828.5 112.6 %all-to-all-start.5 = ((bf16[320,2,1024]{2,1,0:T(2,128)(2,1)}), bf16[320,2,1024]{2,1,0:T(2,128)(2,1)}, u32[]{:S(2)}, u32[]{:S(2)}) async-start(bf16[320,2,1024]{2,1,0:T(2,128)(2,1)} %copy.140), calls=%async_computation.8 | async-start | bytes 2621440 | tf_op jit(solution)/shard_map/all_to_all | solution.py:208
  941.1 22.9 %all-to-all-start.7 = ((bf16[320,2,1024]{2,1,0:T(2,128)(2,1)}), bf16[320,2,1024]{2,1,0:T(2,128)(2,1)}, u32[]{:S(2)}, u32[]{:S(2)}) async-start(bf16[320,2,1024]{2,1,0:T(2,128)(2,1)} %copy.145), calls=%async_computation.11 | async-start | bytes 2621440 | tf_op jit(solution)/shard_map/all_to_all | solution.py:208
  945.8 374.5 %all-reduce.4.cloned.1.call-start = ((), (), s32[]{:S(2)}) async-start(), calls=%async_computation.20 | async-start | bytes 33685504 | tf_op jit(solution)/shard_map/psum | solution.py:268
  986.9 11.4 copy-start.11
  998.3 11.8 copy-start.10
  1015.0 12.4 copy-start.25
  1034.4 16.0 %slice-start.2 = ((s8[5242880]{0:T(1024)(128)(4,1)}), s8[4194304]{0:T(1024)(128)(4,1)S(1)}, s32[]{:S(2)}) async-start(s8[5242880]{0:T(1024)(128)(4,1)} %bitcast.282), calls=%async_computation.23 | async-start | bytes 8388608
  1042.0 12.4 slice-start.6
  1050.5 12.0 slice-start.4
  1075.9 15.6 %copy-start.34 = (bf16[16,64,512]{2,1,0:T(8,128)(2,1)S(1)}, bf16[16,64,512]{2,1,0:T(8,128)(2,1)}, u32[]{:S(2)}) copy-start(bf16[16,64,512]{2,1,0:T(8,128)(2,1)} %copy-done.33) | copy-start | bytes 3145732
  1099.9 47.2 %copy-start.5 = (f32[512,1024]{1,0:T(8,128)S(1)}, f32[512,1024]{1,0:T(8,128)}, u32[]{:S(2)}) copy-start(f32[512,1024]{1,0:T(8,128)} %copy-done.4) | copy-start | bytes 6291460
  1100.0 47.2 %copy-start.54 = (f32[512]{0:T(512)S(1)}, f32[512]{0:T(512)}, u32[]{:S(2)}) copy-start(f32[512]{0:T(512)} %get-tuple-element.41) | copy-start | bytes 6148
  (62 other events, 351.7 us)
Sparse Core Ops, SparseCore 0:
  142.4 98.2 all-gather.4
  242.8 96.4 all-gather.8
  341.4 96.4 all-gather.6
  439.9 96.4 all-gather.10
  538.5 92.0 reduce-scatter.4
  633.3 94.2 reduce-scatter.6
  730.5 94.2 reduce-scatter.8
  827.6 94.2 reduce-scatter.10
  1034.5 285.7 all-reduce.3
where the time goes:
time: 1350 us; the launch traced here: 1340 us
  waiting for transfers between devices  695 us (51%)
  matrix products  297 us (22%)
  local copies, waits for them, and re-layouts  140 us (10%)
  blocking collectives  126 us (9%)
  other arithmetic  50.5 us (4%)
  starting transfers between devices  18.9 us (1%)
  between operations  15 us (1%)
    reduce_scatter x2, waiting for transfers between devices, per_device(): lax.psum_scatter(input_parts.astype(jnp.bfloat16), 'hidden', scatter_dime...  177 us
    psum x1, waiting for transfers between devices, per_device(): lax.psum((query_grad, key_grad, value_grad, w_out_grad, bias_table_grad,...  169 us
    all_gather x2, waiting for transfers between devices, per_device(): grad_all = lax.all_gather(arrived, 'hidden', axis=0, tiled=True)  151 us
    reduce_scatter x2, waiting for transfers between devices, per_device(): lax.psum_scatter(partial_sum.astype(jnp.bfloat16), 'hidden', scatter_dime...  122 us
    all_gather x2, waiting for transfers between devices, per_device(): everyone = lax.all_gather(received, 'hidden', axis=0, tiled=True)  75.2 us
    all_to_all x2, blocking collectives, per_device(): lax.all_to_all(outgoing, 'expert', split_axis=1, concat_axis=0, tiled=True)  42.5 us
    psum x1, blocking collectives, per_device(): lax.psum((query_grad, key_grad, value_grad, w_out_grad, bias_table_grad,...  42.2 us
    all_to_all x2, blocking collectives, per_device(): lax.all_to_all(outgoing_grad, 'expert', split_axis=1, concat_axis=0, tile...  41.2 us
  transfers between devices with their start and end apart: 13, of which 8 were waited for; matrix products, arithmetic and copies ran while one was open for 21% of the time, Pallas kernels for 0%

commit v1 on v0

v1 whole, which is shorter than its diff:
```python
import functools

import jax
import jax.numpy as jnp
from jax import lax
from jax.experimental import pallas as pl
from jax.experimental.pallas import tpu as pltpu
from jax.sharding import PartitionSpec as P

D = 1024
HEADS = 16
HEAD_DIM = 64
BUCKETS = 32
LEN = 512
MICRO = 2
MB_TOK = 256
VMEM = 62 * 1024 * 1024
MESH = pl.DeviceIdType.MESH


eps = 1e-06
precise = lax.Precision.HIGHEST
thresholds = (12, 16, 23, 32, 46, 64, 91)


def bucket_ids(length):
    position = jnp.arange(length, dtype=jnp.int32)
    offset = position[None, :] - position[:, None]
    distance = jnp.abs(offset)
    far_bucket = 8 + sum(((distance >= threshold).astype(jnp.int32) for threshold in thresholds))
    near_bucket = jnp.where(distance < 8, distance, far_bucket)
    return near_bucket + 16 * (offset > 0).astype(jnp.int32)


def contract_last(matrix_a, matrix_b, mode=None):
    return lax.dot_general(
        matrix_a,
        matrix_b,
        (((1,), (1,)), ((), ())),
        precision=mode,
        preferred_element_type=jnp.float32,
    )


def contract_first(matrix_a, matrix_b, mode=None):
    return lax.dot_general(
        matrix_a,
        matrix_b,
        (((0,), (0,)), ((), ())),
        precision=mode,
        preferred_element_type=jnp.float32,
    )


def dot(matrix_a, matrix_b):
    return jnp.dot(matrix_a, matrix_b, preferred_element_type=jnp.float32)


def slot_targets(routes, experts_all, capacity, stride):
    pairs = 2 * MB_TOK
    flat = routes.reshape(-1, pairs)
    hits = (flat[:, :, None] == jnp.arange(experts_all, dtype=jnp.int32)).astype(jnp.bfloat16)
    lower = (
        jnp.arange(pairs, dtype=jnp.int32)[:, None] > jnp.arange(pairs, dtype=jnp.int32)[None, :]
    ).astype(jnp.bfloat16)
    earlier = jnp.einsum("pq,bqe->bpe", lower, hits, preferred_element_type=jnp.float32)
    rank = jnp.sum(earlier * hits.astype(jnp.float32), axis=-1).astype(jnp.int32)
    block = jnp.arange(flat.shape[0], dtype=jnp.int32)[:, None]
    target = flat * stride + block * capacity + rank
    return target.reshape(-1, 2).T


class Plan:
    def __init__(self, n_e, n_h, experts_all, width):
        self.n_e, self.n_h, self.width = n_e, n_h, width
        self.capacity = 10 * MB_TOK // (4 * experts_all)
        self.stride = -(-MICRO * self.capacity // 16) * 16
        self.span = 2 * self.stride
        self.rows = n_e * self.stride
        self.total = n_h * self.rows

    def place(self):
        return lax.axis_index("expert"), lax.axis_index("hidden")


def across(here, mask):
    there, bit = here, 1
    while bit <= mask:
        if mask & bit:
            there = there + bit * (1 - 2 * lax.rem(lax.div(here, bit), 2))
        bit *= 2
    return there


def remote(src, dst, send_sem, recv_sem, device):
    return pltpu.make_async_remote_copy(
        src_ref=src,
        dst_ref=dst,
        send_sem=send_sem,
        recv_sem=recv_sem,
        device_id=device,
        device_id_type=MESH,
    )


def greet(plan):
    e, z = plan.place()
    barrier = pltpu.get_barrier_semaphore()
    for mask in range(1, plan.n_e):
        pl.semaphore_signal(barrier, inc=1, device_id=(across(e, mask), z), device_id_type=MESH)
    for shift in range(1, plan.n_h):
        pl.semaphore_signal(
            barrier, inc=1, device_id=(e, lax.rem(z + shift, plan.n_h)), device_id_type=MESH
        )
    pl.semaphore_wait(barrier, plan.n_e + plan.n_h - 2)


def slot_hits(plan, base, target):
    slots = lax.broadcasted_iota(jnp.int32, (plan.stride, LEN), 0).astype(jnp.float32) + base
    return jnp.where((slots == target[0:1, :]) | (slots == target[1:2, :]), 1.0, 0.0).astype(
        jnp.bfloat16
    )


def slot_base(plan, device, j):
    return (device * plan.span + j * plan.stride).astype(jnp.float32)


class Dispatch:
    def __init__(self, plan, rows, meta, land, out, meta_out, rows_v, meta_v, stage, sems):
        self.plan = plan
        self.rows, self.meta, self.land = rows, meta, land
        self.out, self.meta_out = out, meta_out
        self.rows_v, self.meta_v, self.stage = rows_v, meta_v, stage
        (
            self.z_send,
            self.z_recv,
            self.zm_send,
            self.zm_recv,
            self.a_send,
            self.a_recv,
            self.m_send,
            self.m_recv,
            self.local,
        ) = sems

    @staticmethod
    def sem_shapes(plan):
        dma = pltpu.SemaphoreType.DMA
        n_h, n_e = plan.n_h, plan.n_e
        return [
            dma((n_h,)),
            dma((n_h,)),
            dma((n_h,)),
            dma((n_h,)),
            dma((2, n_e)),
            dma((n_h, n_e)),
            dma((n_h, n_e)),
            dma((n_h, n_e)),
            dma((3,)),
        ]

    def along_z(self, shift):
        e, z = self.plan.place()
        peer = (e, lax.rem(z + self.plan.n_h - shift, self.plan.n_h))
        return (
            remote(
                self.meta,
                self.meta_v.at[shift],
                self.zm_send.at[shift],
                self.zm_recv.at[shift],
                peer,
            ),
            remote(
                self.rows,
                self.land.at[shift],
                self.z_send.at[shift],
                self.z_recv.at[shift],
                peer,
            ),
        )

    def begin(self):
        for shift in range(1, self.plan.n_h):
            for copy in self.along_z(shift):
                copy.start()
        copy = pltpu.make_async_copy(self.meta, self.meta_v.at[0], self.local.at[1])
        copy.start()
        copy.wait()

    def in_plane(self, chunk, mask):
        plan = self.plan
        e, z = plan.place()
        buffer = lax.rem(chunk, 2)
        at = pl.multiple_of((chunk * plan.n_e + mask) * plan.stride, 16)
        return remote(
            self.stage.at[buffer, :, pl.ds(mask * plan.stride, plan.stride), :],
            self.out.at[:, pl.ds(at, plan.stride), :],
            self.a_send.at[buffer, mask],
            self.a_recv.at[chunk, mask],
            (across(e, mask), z),
        )

    def meta_copy(self, chunk, mask):
        e, z = self.plan.place()
        return remote(
            self.meta_v.at[chunk],
            self.meta_out.at[chunk, mask],
            self.m_send.at[chunk, mask],
            self.m_recv.at[chunk, mask],
            (across(e, mask), z),
        )

    def chunk(self, chunk, target_of):
        plan = self.plan
        e, _ = plan.place()
        buffer = lax.rem(chunk, 2)

        @pl.when(chunk == 0)
        def _():
            copy = pltpu.make_async_copy(self.rows, self.rows_v.at[buffer], self.local.at[0])
            copy.start()
            copy.wait()

        @pl.when(chunk > 0)
        def _():
            for copy in self.along_z(chunk):
                copy.wait_recv()
            copy = pltpu.make_async_copy(
                self.land.at[chunk], self.rows_v.at[buffer], self.local.at[0]
            )
            copy.start()
            copy.wait()

        for mask in range(1, plan.n_e):
            self.meta_copy(chunk, mask).start()
        own_meta = pltpu.make_async_copy(
            self.meta_v.at[chunk], self.meta_out.at[chunk, 0], self.local.at[1]
        )
        own_meta.start()

        @pl.when(chunk >= 2)
        def _():
            for mask in range(1, plan.n_e):
                self.in_plane(chunk - 2, mask).wait_send()

        target = target_of(chunk)
        group = min(4, plan.n_e)
        for start in range(0, plan.n_e, group):
            for j in range(2):
                hot = jnp.concatenate(
                    [
                        slot_hits(plan, slot_base(plan, across(e, start + i), j), target)
                        for i in range(group)
                    ],
                    axis=0,
                )
                picked = dot(hot, self.rows_v[buffer]).astype(jnp.bfloat16)
                self.stage[
                    buffer, j, start * plan.stride : (start + group) * plan.stride, :
                ] = picked
            for mask in range(max(start, 1), start + group):
                self.in_plane(chunk, mask).start()
        at = pl.multiple_of(chunk * plan.rows, 16)
        own = pltpu.make_async_copy(
            self.stage.at[buffer, :, pl.ds(0, plan.stride), :],
            self.out.at[:, pl.ds(at, plan.stride), :],
            self.local.at[2],
        )
        own.start()
        own.wait()
        own_meta.wait()

    def arrived(self, chunk):
        for mask in range(1, self.plan.n_e):
            self.meta_copy(chunk, mask).wait_recv()
            self.in_plane(chunk, mask).wait_recv()

    def finish(self):
        plan = self.plan
        for chunk in range(max(0, plan.n_h - 2), plan.n_h):
            for mask in range(1, plan.n_e):
                self.in_plane(chunk, mask).wait_send()
        for shift in range(1, plan.n_h):
            for copy in self.along_z(shift):
                copy.wait_send()
        for chunk in range(plan.n_h):
            for mask in range(1, plan.n_e):
                self.meta_copy(chunk, mask).wait_send()


class Return:
    def __init__(self, plan, back, land, out, stage, rows_v, total, sems):
        self.plan = plan
        self.back, self.land, self.out = back, land, out
        self.stage, self.rows_v, self.total = stage, rows_v, total
        (self.b_send, self.b_recv, self.s_send, self.s_recv, self.local, self.own) = sems

    @staticmethod
    def sem_shapes(plan):
        dma = pltpu.SemaphoreType.DMA
        n_h, n_e = plan.n_h, plan.n_e
        return [
            dma((n_h, n_e)),
            dma((n_h, n_e)),
            dma((n_h,)),
            dma((n_h,)),
            dma((2,)),
            dma((n_h,)),
        ]

    def source(self, chunk, mask):
        raise NotImplementedError

    def in_plane(self, chunk, mask):
        plan = self.plan
        e, z = plan.place()
        return remote(
            self.source(chunk, mask),
            self.back.at[chunk, :, pl.ds(mask * plan.stride, plan.stride), :],
            self.b_send.at[chunk, mask],
            self.b_recv.at[chunk, mask],
            (across(e, mask), z),
        )

    def own_copy(self, chunk):
        plan = self.plan
        return pltpu.make_async_copy(
            self.source(chunk, 0),
            self.back.at[chunk, :, pl.ds(0, plan.stride), :],
            self.own.at[chunk],
        )

    def send(self, chunk):
        for mask in range(1, self.plan.n_e):
            self.in_plane(chunk, mask).start()
        self.own_copy(chunk).start()

    def along_z(self, chunk):
        e, z = self.plan.place()
        return remote(
            self.rows_v.at[lax.rem(chunk, 2)],
            self.land.at[chunk],
            self.s_send.at[chunk],
            self.s_recv.at[chunk],
            (e, lax.rem(z + chunk, self.plan.n_h)),
        )

    def combine(self, chunk, target):
        plan = self.plan
        e, _ = plan.place()
        buffer = lax.rem(chunk, 2)
        for mask in range(1, plan.n_e):
            self.in_plane(chunk, mask).wait_recv()
        self.own_copy(chunk).wait()
        copy = pltpu.make_async_copy(self.back.at[chunk], self.stage.at[buffer], self.local.at[0])
        copy.start()
        hot = [
            jnp.concatenate(
                [
                    slot_hits(plan, slot_base(plan, across(e, mask), j), target)
                    for mask in range(plan.n_e)
                ],
                axis=0,
            )
            for j in range(2)
        ]
        copy.wait()

        @pl.when(chunk >= 3)
        def _():
            self.along_z(chunk - 2).wait_send()

        part = contract_first(hot[0], self.stage[buffer, 0]) + contract_first(
            hot[1], self.stage[buffer, 1]
        )

        @pl.when(chunk == 0)
        def _():
            self.total[...] = part

        @pl.when(chunk > 0)
        def _():
            self.rows_v[buffer] = part.astype(jnp.bfloat16)
            self.along_z(chunk).start()

    def finish(self):
        plan = self.plan
        for chunk in range(max(1, plan.n_h - 2), plan.n_h):
            self.along_z(chunk).wait_send()
        for chunk in range(1, plan.n_h):
            self.along_z(chunk).wait_recv()
            copy = pltpu.make_async_copy(
                self.land.at[chunk], self.rows_v.at[chunk % 2], self.local.at[0]
            )
            copy.start()
            copy.wait()
            self.total[...] += self.rows_v[chunk % 2].astype(jnp.float32)
        copy = pltpu.make_async_copy(self.total, self.out, self.local.at[0])
        copy.start()
        copy.wait()


class ReturnHeld(Return):
    def __init__(self, plan, given, *rest):
        super().__init__(plan, *rest)
        self.given = given

    def source(self, chunk, mask):
        plan = self.plan
        at = pl.multiple_of((chunk * plan.n_e + mask) * plan.stride, 16)
        return self.given.at[:, pl.ds(at, plan.stride), :]

    def sent(self):
        for chunk in range(self.plan.n_h):
            for mask in range(1, self.plan.n_e):
                self.in_plane(chunk, mask).wait_send()


class ReturnMade(Return):
    def __init__(self, plan, made, *rest):
        super().__init__(plan, *rest)
        self.made = made
        self.ring = made.shape[0]

    def source(self, chunk, mask):
        plan = self.plan
        return self.made.at[
            lax.rem(chunk, self.ring), :, pl.ds(mask * plan.stride, plan.stride), :
        ]

    def free(self, chunk):
        if self.plan.n_h > self.ring:

            @pl.when(chunk >= self.ring)
            def _():
                self.wait_sent(chunk - self.ring)
                self.own_copy(chunk - self.ring).wait()

    def wait_sent(self, chunk):
        for mask in range(1, self.plan.n_e):
            self.in_plane(chunk, mask).wait_send()

    def sent(self):
        for chunk in range(max(0, self.plan.n_h - self.ring), self.plan.n_h):
            self.wait_sent(chunk)


ANY = pl.BlockSpec(memory_space=pl.ANY)


def send_body(plan, rows, meta, out, meta_out, land, rows_v, meta_v, stage, *sems):
    greet(plan)
    work = Dispatch(plan, rows, meta, land, out, meta_out, rows_v, meta_v, stage, sems)
    work.begin()
    pl.loop(0, plan.n_h)(lambda chunk: work.chunk(chunk, lambda at: meta_v[at]))
    for chunk in range(plan.n_h):
        work.arrived(chunk)
    work.finish()


def send_rows(plan, rows, meta):
    n_h, n_e = plan.n_h, plan.n_e
    out = pl.pallas_call(
        functools.partial(send_body, plan),
        in_specs=[ANY, ANY],
        out_specs=[ANY, ANY, ANY],
        out_shape=[
            jax.ShapeDtypeStruct((2, plan.total, D), jnp.bfloat16),
            jax.ShapeDtypeStruct((n_h, n_e, 8, LEN), jnp.float32),
            jax.ShapeDtypeStruct((n_h, LEN, D), jnp.bfloat16),
        ],
        scratch_shapes=[
            pltpu.VMEM((2, LEN, D), jnp.bfloat16),
            pltpu.VMEM((n_h, 8, LEN), jnp.float32),
            pltpu.VMEM((2, 2, plan.rows, D), jnp.bfloat16),
        ]
        + Dispatch.sem_shapes(plan),
        compiler_params=pltpu.CompilerParams(
            collective_id=1, has_side_effects=True, vmem_limit_bytes=VMEM
        ),
        name="send_rows",
    )(rows, meta)
    return out[0], out[1]


def expert_body(plan, halves, n_d, *refs):
    (
        sent,
        gates,
        grads,
        targets,
        w_gate,
        w_up,
        w_down,
        total_out,
        gg_out,
        rows_out,
        y_out,
        dgate_out,
        dup_out,
        act_out,
        meta_out,
        land,
        back,
        land_back,
        rows_v,
        meta_v,
        stage,
        wg_v,
        wu_v,
        wd_v,
        target_v,
        gate_v,
        x_v,
        g_v,
        dx_v,
        y_v,
        dgate_v,
        dup_v,
        act_v,
        gg_v,
        gg_back,
        gg_part,
        gg_land,
        total,
        w_sem,
        t_sem,
        x_sem,
        o_sem,
        gg_send,
        gg_recv,
        ggs_send,
        ggs_recv,
        *sems,
    ) = refs
    n_e, n_h = plan.n_e, plan.n_h
    e, z = plan.place()
    loads = [
        pltpu.make_async_copy(source, held, w_sem.at[i])
        for i, (source, held) in enumerate(((w_gate, wg_v), (w_up, wu_v), (w_down, wd_v)))
    ]
    for load in loads:
        load.start()
    targets_in = pltpu.make_async_copy(targets, target_v, t_sem.at[0])
    targets_in.start()
    greet(plan)
    work = Dispatch(
        plan, sent, gates, land, rows_out, meta_out, rows_v, meta_v, stage, sems[:n_d]
    )
    give = ReturnMade(
        plan, dx_v, back, land_back, total_out, stage, rows_v, total, sems[n_d:]
    )
    work.begin()
    targets_in.wait()
    ahead = min(3, n_h)
    pl.loop(0, ahead)(lambda chunk: work.chunk(chunk, lambda at: target_v[at, 0]))
    for load in loads:
        load.wait()

    def gg_copy(chunk, mask):
        return remote(
            gg_v.at[chunk, mask],
            gg_back.at[chunk, mask],
            gg_send.at[chunk, mask],
            gg_recv.at[chunk, mask],
            (across(e, mask), z),
        )

    def gg_along(chunk):
        return remote(
            gg_part.at[chunk],
            gg_land.at[chunk],
            ggs_send.at[chunk],
            ggs_recv.at[chunk],
            (e, lax.rem(z + chunk, n_h)),
        )

    def outs(chunk, j):
        at = pl.multiple_of(chunk * plan.rows, 16)
        return [
            pltpu.make_async_copy(held.at[j], out.at[j, pl.ds(at, plan.rows), :], o_sem.at[i, j])
            for i, (held, out) in enumerate(
                ((y_v, y_out), (dgate_v, dgate_out), (dup_v, dup_out), (act_v, act_out))
            )
        ]

    masks = n_e // halves
    piece = masks * plan.stride

    def step(chunk, index):
        j, half = lax.div(index, halves), lax.rem(index, halves)
        at = pl.ds(pl.multiple_of(half * piece, 16), piece)
        rows, grads_in = x_v[j, at, :], g_v[j, at, :]
        gate_pre = dot(rows, wg_v[j])
        up_pre = dot(rows, wu_v[j])
        raw = contract_last(grads_in, wd_v[j])
        slots = lax.broadcasted_iota(jnp.int32, (plan.stride, LEN), 0).astype(
            jnp.float32
        ) + slot_base(plan, e, j)
        columns = []
        for i in range(masks):
            mask = half * masks + i
            aim, weight = target_v[chunk, mask], gate_v[mask]
            hit = jnp.where(slots == aim[0:1, :], weight[0:1, :], 0.0)
            hit = hit + jnp.where(slots == aim[1:2, :], weight[1:2, :], 0.0)
            columns.append(jnp.sum(hit, axis=1, keepdims=True))
        gate = jnp.concatenate(columns, axis=0)
        square = gate_pre * gate_pre
        tanh = jnp.tanh(0.7978845608028654 * gate_pre * (1.0 + 0.044715 * square))
        side = 0.5 * (1.0 + tanh)
        gelu = gate_pre * side
        slope = side + 0.5 * gate_pre * (1.0 - tanh * tanh) * (
            0.7978845608028654 * (1.0 + 0.134145 * square)
        )
        act = gelu * up_pre
        act_low = act.astype(jnp.bfloat16)
        dots = jnp.sum(act_low.astype(jnp.float32) * raw, axis=1, keepdims=True)
        for i in range(masks):
            mask = half * masks + i
            aim, part = target_v[chunk, mask], dots[i * plan.stride : (i + 1) * plan.stride]
            for k in range(2):
                line = jnp.sum(
                    jnp.where(slots == aim[k : k + 1, :], part, 0.0), axis=0, keepdims=True
                )
                gg_v[chunk, mask, k : k + 1, :] += line
        grad_act = gate * raw
        grad_gate = (grad_act * up_pre * slope).astype(jnp.bfloat16)
        grad_up = (grad_act * gelu).astype(jnp.bfloat16)
        dgate_v[j, at, :] = grad_gate
        dup_v[j, at, :] = grad_up
        act_v[j, at, :] = (act * gate).astype(jnp.bfloat16)
        dx_v[lax.rem(chunk, dx_v.shape[0]), j, at, :] = (
            contract_last(grad_gate, wg_v[j]) + contract_last(grad_up, wu_v[j])
        ).astype(jnp.bfloat16)
        y_v[j, at, :] = (dot(act_low, wd_v[j]) * gate).astype(jnp.bfloat16)

    gg_v[...] = jnp.zeros_like(gg_v)

    @pl.loop(0, n_h)
    def _(chunk):
        work.arrived(chunk)
        at = pl.multiple_of(chunk * plan.rows, 16)
        gate_in = pltpu.make_async_copy(meta_out.at[chunk], gate_v, t_sem.at[0])
        gate_in.start()
        ins = [
            pltpu.make_async_copy(source.at[:, pl.ds(at, plan.rows), :], held, x_sem.at[i])
            for i, (source, held) in enumerate(((rows_out, x_v), (grads, g_v)))
        ]
        for copy in ins:
            copy.start()
        give.free(chunk)

        @pl.when(chunk > 0)
        def _():
            for j in range(2):
                for copy in outs(chunk - 1, j):
                    copy.wait()

        gate_in.wait()
        for copy in ins:
            copy.wait()
        pl.loop(0, 2 * halves)(lambda index: step(chunk, index))
        for mask in range(1, n_e):
            gg_copy(chunk, mask).start()
        give.send(chunk)
        for j in range(2):
            for copy in outs(chunk, j):
                copy.start()

        @pl.when(chunk + ahead < n_h)
        def _():
            work.chunk(chunk + ahead, lambda at: target_v[at, 0])

    work.finish()
    for j in range(2):
        for copy in outs(n_h - 1, j):
            copy.wait()

    @pl.loop(0, n_h)
    def _(chunk):
        part = gg_v[chunk, 0]
        for mask in range(1, n_e):
            gg_copy(chunk, mask).wait_recv()
            part = part + gg_back[chunk, mask]
        gg_part[chunk] = part

        @pl.when(chunk > 0)
        def _():
            gg_along(chunk).start()

        give.combine(chunk, target_v[chunk, 0])

    give.sent()
    for chunk in range(n_h):
        for mask in range(1, n_e):
            gg_copy(chunk, mask).wait_send()
    sum_gg = gg_part[0]
    for chunk in range(1, n_h):
        gg_along(chunk).wait_recv()
        sum_gg = sum_gg + gg_land[chunk]
    gg_out[...] = sum_gg
    for chunk in range(1, n_h):
        gg_along(chunk).wait_send()
    give.finish()


def run_experts(plan, sent, gates, grads, targets, w_gate, w_up, w_down):
    n_h, n_e, width = plan.n_h, plan.n_e, plan.width
    bf16, f32 = jnp.bfloat16, jnp.float32
    shape = jax.ShapeDtypeStruct
    dma = pltpu.SemaphoreType.DMA
    ring = min(4, n_h)
    d_sems, r_sems = Dispatch.sem_shapes(plan), Return.sem_shapes(plan)
    halves = 2 if plan.rows <= 640 else 4
    return pl.pallas_call(
        functools.partial(expert_body, plan, halves, len(d_sems)),
        in_specs=[ANY] * 7,
        out_specs=[ANY, pl.BlockSpec(memory_space=pltpu.VMEM)] + [ANY] * 9,
        out_shape=[
            shape((LEN, D), f32),
            shape((8, LEN), f32),
            shape((2, plan.total, D), bf16),
            shape((2, plan.total, D), bf16),
            shape((2, plan.total, width), bf16),
            shape((2, plan.total, width), bf16),
            shape((2, plan.total, width), bf16),
            shape((n_h, n_e, 8, LEN), f32),
            shape((n_h, LEN, D), bf16),
            shape((n_h, 2, plan.rows, D), bf16),
            shape((n_h, LEN, D), bf16),
        ],
        scratch_shapes=[
            pltpu.VMEM((2, LEN, D), bf16),
            pltpu.VMEM((n_h, 8, LEN), f32),
            pltpu.VMEM((2, 2, plan.rows, D), bf16),
            pltpu.VMEM((2, D, width), bf16),
            pltpu.VMEM((2, D, width), bf16),
            pltpu.VMEM((2, width, D), bf16),
            pltpu.VMEM((n_h, n_e, 8, LEN), f32),
            pltpu.VMEM((n_e, 8, LEN), f32),
            pltpu.VMEM((2, plan.rows, D), bf16),
            pltpu.VMEM((2, plan.rows, D), bf16),
            pltpu.VMEM((ring, 2, plan.rows, D), bf16),
            pltpu.VMEM((2, plan.rows, D), bf16),
            pltpu.VMEM((2, plan.rows, width), bf16),
            pltpu.VMEM((2, plan.rows, width), bf16),
            pltpu.VMEM((2, plan.rows, width), bf16),
            pltpu.VMEM((n_h, n_e, 8, LEN), f32),
            pltpu.VMEM((n_h, n_e, 8, LEN), f32),
            pltpu.VMEM((n_h, 8, LEN), f32),
            pltpu.VMEM((n_h, 8, LEN), f32),
            pltpu.VMEM((LEN, D), f32),
            dma((3,)),
            dma((1,)),
            dma((2,)),
            dma((4, 2)),
            dma((n_h, n_e)),
            dma((n_h, n_e)),
            dma((n_h,)),
            dma((n_h,)),
        ]
        + d_sems
        + r_sems,
        compiler_params=pltpu.CompilerParams(
            collective_id=2, has_side_effects=True, vmem_limit_bytes=VMEM
        ),
        name="run_experts",
    )(sent, gates, grads, targets, w_gate, w_up, w_down)


def back_body(plan, given, targets, out, back, land, rows_v, stage, target_v, total, t_sem, *sems):
    targets_in = pltpu.make_async_copy(targets, target_v, t_sem.at[0])
    targets_in.start()
    greet(plan)
    give = ReturnHeld(plan, given, back, land, out, stage, rows_v, total, sems)
    for chunk in range(plan.n_h):
        give.send(chunk)
    targets_in.wait()
    pl.loop(0, plan.n_h)(lambda chunk: give.combine(chunk, target_v[chunk, 0]))
    give.sent()
    give.finish()


def bring_back(plan, given, targets):
    n_h, n_e = plan.n_h, plan.n_e
    bf16, f32 = jnp.bfloat16, jnp.float32
    shape = jax.ShapeDtypeStruct
    return pl.pallas_call(
        functools.partial(back_body, plan),
        in_specs=[ANY, ANY],
        out_specs=[ANY] * 3,
        out_shape=[
            shape((LEN, D), f32),
            shape((n_h, 2, plan.rows, D), bf16),
            shape((n_h, LEN, D), bf16),
        ],
        scratch_shapes=[
            pltpu.VMEM((2, LEN, D), bf16),
            pltpu.VMEM((2, 2, plan.rows, D), bf16),
            pltpu.VMEM((n_h, n_e, 8, LEN), f32),
            pltpu.VMEM((LEN, D), f32),
            pltpu.SemaphoreType.DMA((1,)),
        ]
        + Return.sem_shapes(plan),
        compiler_params=pltpu.CompilerParams(
            collective_id=3, has_side_effects=True, vmem_limit_bytes=VMEM
        ),
        name="bring_back",
    )(given, targets)[0]


def per_device(
    n_e,
    n_h,
    tokens,
    gain_one,
    w_query,
    w_key,
    w_value,
    w_out,
    bias_table,
    gain_two,
    w_router,
    w_gate,
    w_up,
    w_down,
    routes,
    cotangent,
):
    experts_all = w_router.shape[1]
    plan = Plan(n_e, n_h, experts_all, w_gate.shape[2])
    both = ("expert", "hidden")

    def small(array):
        return jnp.pad(array.astype(jnp.float32), ((0, 6), (0, 0)))

    targets = small(slot_targets(routes, experts_all, plan.capacity, plan.stride))
    grads_in, targets_all = send_rows(plan, cotangent, targets)
    scaling = HEAD_DIM ** (-0.5)
    bucket_hot = (bucket_ids(LEN)[:, :, None] == jnp.arange(BUCKETS, dtype=jnp.int32)).astype(
        jnp.float32
    )
    inputs = tokens.astype(jnp.float32)
    inv_one = lax.rsqrt(jnp.mean(inputs * inputs, axis=-1, keepdims=True) + eps)
    normed_one = (inputs * inv_one * gain_one).astype(jnp.bfloat16)
    query_rows = jnp.dot(normed_one, w_query, preferred_element_type=jnp.float32).astype(
        jnp.bfloat16
    )
    key_rows = jnp.dot(normed_one, w_key, preferred_element_type=jnp.float32).astype(jnp.bfloat16)
    value_rows = jnp.dot(normed_one, w_value, preferred_element_type=jnp.float32).astype(
        jnp.bfloat16
    )
    query_heads = query_rows.reshape(LEN, HEADS, HEAD_DIM)
    key_heads = key_rows.reshape(LEN, HEADS, HEAD_DIM)
    value_heads = value_rows.reshape(LEN, HEADS, HEAD_DIM)
    bias_rows = jnp.einsum("ijb,bh->hij", bucket_hot, bias_table, precision=precise)

    def score_of():
        raw = jnp.einsum("qhd,khd->hqk", query_heads, key_heads, preferred_element_type=jnp.float32)
        return raw * scaling + bias_rows

    scores = score_of()
    row_peak = jnp.max(scores, axis=-1, keepdims=True)
    exp_terms = jnp.exp(scores - row_peak)
    row_total = jnp.sum(exp_terms, axis=-1, keepdims=True)
    log_total = row_peak + jnp.log(row_total)
    soft_low = (exp_terms / row_total).astype(jnp.bfloat16)
    mixed_rows = jnp.einsum(
        "hqk,khd->qhd", soft_low, value_heads, preferred_element_type=jnp.float32
    )
    mixed_rows = mixed_rows.reshape(LEN, D).astype(jnp.bfloat16)
    hidden = inputs + jnp.dot(mixed_rows, w_out, preferred_element_type=jnp.float32)
    inv_two = lax.rsqrt(jnp.mean(hidden * hidden, axis=-1, keepdims=True) + eps)
    normed_two = hidden * inv_two * gain_two
    sent = normed_two.astype(jnp.bfloat16)
    logits = jnp.dot(normed_two, w_router, precision=precise)
    route_hot = (routes[:, :, None] == jnp.arange(experts_all, dtype=jnp.int32)).astype(jnp.float32)
    chosen = jnp.sum(route_hot * logits[:, None, :], axis=-1)
    gate_values = jax.nn.softmax(chosen, axis=-1)
    grad_sent, grad_gates, rows_in, y_rows, gate_rows, up_rows, act_rows = run_experts(
        plan, sent, small(gate_values.T), grads_in, targets_all, w_gate, w_up, w_down
    )[:7]
    branch = bring_back(plan, y_rows, targets_all)
    grad_gates = grad_gates[:2].T
    block_out = (hidden + branch).astype(jnp.bfloat16)
    down_grad = jnp.einsum("xrf,xrd->xfd", act_rows, grads_in, preferred_element_type=jnp.float32)
    gate_grad = jnp.einsum("xrd,xrf->xdf", rows_in, gate_rows, preferred_element_type=jnp.float32)
    up_grad = jnp.einsum("xrd,xrf->xdf", rows_in, up_rows, preferred_element_type=jnp.float32)
    grad_out = cotangent.astype(jnp.float32)
    grad_chosen = gate_values * (
        grad_gates - jnp.sum(gate_values * grad_gates, axis=-1, keepdims=True)
    )
    grad_logits = jnp.sum(route_hot * grad_chosen[:, :, None], axis=1)
    router_grad = contract_first(normed_two, grad_logits, precise)
    grad_normed_two = contract_last(grad_logits, w_router, precise)
    grad_normed_two = grad_normed_two + grad_sent.astype(jnp.float32)
    gain_two_grad = jnp.sum(grad_normed_two * hidden * inv_two, axis=0)
    scaled_two = grad_normed_two * gain_two
    grad_hidden = (
        grad_out
        + inv_two * scaled_two
        - hidden * inv_two**3 * jnp.mean(scaled_two * hidden, axis=-1, keepdims=True)
    )
    grad_branch = grad_hidden.astype(jnp.bfloat16)
    w_out_grad = contract_first(mixed_rows, grad_branch)
    grad_mixed = (
        contract_last(grad_branch, w_out).astype(jnp.bfloat16).reshape(LEN, HEADS, HEAD_DIM)
    )
    soft_again = jnp.exp(score_of() - log_total)
    soft_again_low = soft_again.astype(jnp.bfloat16)
    grad_value_heads = jnp.einsum(
        "hqk,qhd->khd", soft_again_low, grad_mixed, preferred_element_type=jnp.float32
    )
    grad_value_rows = grad_value_heads.astype(jnp.bfloat16).reshape(LEN, D)
    grad_soft = jnp.einsum(
        "qhd,khd->hqk", grad_mixed, value_heads, preferred_element_type=jnp.float32
    )
    grad_scores = soft_again * (grad_soft - jnp.sum(soft_again * grad_soft, axis=-1, keepdims=True))
    grad_scores = grad_scores.astype(jnp.bfloat16)
    bias_table_grad = jnp.einsum(
        "hij,ijb->bh", grad_scores.astype(jnp.float32), bucket_hot, precision=precise
    )
    grad_query_rows = (
        jnp.einsum("hqk,khd->qhd", grad_scores, key_heads, preferred_element_type=jnp.float32)
        * scaling
    )
    grad_query_rows = grad_query_rows.astype(jnp.bfloat16).reshape(LEN, D)
    grad_key_rows = (
        jnp.einsum("hqk,qhd->khd", grad_scores, query_heads, preferred_element_type=jnp.float32)
        * scaling
    )
    grad_key_rows = grad_key_rows.astype(jnp.bfloat16).reshape(LEN, D)
    query_grad = contract_first(normed_one, grad_query_rows)
    key_grad = contract_first(normed_one, grad_key_rows)
    value_grad = contract_first(normed_one, grad_value_rows)
    grad_normed_one = (
        contract_last(grad_query_rows, w_query)
        + contract_last(grad_key_rows, w_key)
        + contract_last(grad_value_rows, w_value)
    )
    gain_one_grad = jnp.sum(grad_normed_one * inputs * inv_one, axis=0)
    scaled_one = grad_normed_one * gain_one
    tokens_grad = (
        grad_hidden
        + inv_one * scaled_one
        - inputs * inv_one**3 * jnp.mean(scaled_one * inputs, axis=-1, keepdims=True)
    )
    query_grad, key_grad, value_grad, w_out_grad = [
        item.astype(jnp.float32)
        for item in lax.psum(
            [
                item.astype(jnp.bfloat16)
                for item in (query_grad, key_grad, value_grad, w_out_grad)
            ],
            both,
        )
    ]
    bias_table_grad, gain_one_grad, gain_two_grad, router_grad = lax.psum(
        (bias_table_grad, gain_one_grad, gain_two_grad, router_grad), both
    )
    return (
        block_out,
        tokens_grad,
        gain_one_grad,
        query_grad,
        key_grad,
        value_grad,
        w_out_grad,
        bias_table_grad,
        gain_two_grad,
        router_grad,
        gate_grad,
        up_grad,
        down_grad,
    )


def solution(mesh):
    in_specs = (
        P(("expert", "hidden"), None),
        P(),
        P(),
        P(),
        P(),
        P(),
        P(),
        P(),
        P(),
        P("expert", None, "hidden"),
        P("expert", None, "hidden"),
        P("expert", "hidden", None),
        P(("expert", "hidden"), None),
        P(("expert", "hidden"), None),
    )
    out_specs = (
        P(("expert", "hidden"), None),
        P(("expert", "hidden"), None),
        P(),
        P(),
        P(),
        P(),
        P(),
        P(),
        P(),
        P(),
        P("expert", None, "hidden"),
        P("expert", None, "hidden"),
        P("expert", "hidden", None),
    )
    return jax.shard_map(
        functools.partial(per_device, mesh.shape["expert"], mesh.shape["hidden"]),
        mesh=mesh, in_specs=in_specs, out_specs=out_specs, check_vma=False
    )
```

time: 1350 us -> 1130 us (0.84)
  Pallas kernels: 0 us -> 637 us
  waiting for transfers between devices: 695 us -> 171 us
  matrix products: 297 us -> 160 us
  blocking collectives: 126 us -> 41.4 us
  local copies, waits for them, and re-layouts: 140 us -> 56.2 us
  starting transfers between devices: 18.9 us -> 0.08 us
    pallas_call x0 -> x3, Pallas kernels: none -> 637 us  [the longest x1 312 us: run_experts(): pl.pallas_call(functools.partial(expert_body, plan, halves, len(d_sems)),...]
    reduce_scatter x4 -> x0, waiting for transfers between devices: 299 us -> none  [the longest x2 177 us: per_device(): lax.psum_scatter(input_parts.astype(jnp.bfloat16), 'hidden', scatter_dime...]
    all_gather x4 -> x0, waiting for transfers between devices: 226 us -> none  [the longest x2 151 us: per_device(): grad_all = lax.all_gather(arrived, 'hidden', axis=0, tiled=True)]
    dot_general x26 -> x4, matrix products: 174 us -> 43.7 us  [the longest x1 14.6 us: per_device(): jnp.einsum('xrd,xrf->xdf', rows_in, up_rows, preferred_element_type=jnp.f...]
    all_to_all x4 -> x0, blocking collectives: 83.7 us -> none  [the longest x2 42.5 us: per_device(): lax.all_to_all(outgoing, 'expert', split_axis=1, concat_axis=0, tiled=True)]
    reshape x10 -> x0, local copies, waits for them, and re-layouts: 21.3 us -> none  [the longest x2 8.46 us: per_device(): gone_home = lax.all_to_all(returned, 'expert', split_axis=0, concat_axis=...]
    all_to_all x4 -> x0, starting transfers between devices: 18.6 us -> none  [the longest x2 9.5 us: per_device(): lax.all_to_all(returned, 'expert', split_axis=0, concat_axis=1, tiled=True)]
    all_to_all x8 -> x0, local copies, waits for them, and re-layouts: 16.1 us -> none  [the longest x2 7.55 us: per_device(): lax.all_to_all(returned, 'expert', split_axis=0, concat_axis=1, tiled=True)]
  transfers between devices with their start and end apart: 13 -> 2, of which waited for: 8 -> 2; matrix products, arithmetic and copies ran while one was open for 21% -> 8% of each run, Pallas kernels for 0% -> 0%
where the time goes in v1:
time: 1130 us; the launch traced here: 1120 us
  Pallas kernels  637 us (56%)
  waiting for transfers between devices  171 us (15%)
  matrix products  160 us (14%)
  local copies, waits for them, and re-layouts  56.2 us (5%)
  other arithmetic  43.8 us (4%)
  blocking collectives  41.4 us (4%)
  between operations  14.7 us (1%)
    pallas_call x1, Pallas kernels, run_experts(): pl.pallas_call(functools.partial(expert_body, plan, halves, len(d_sems)),...  312 us
    pallas_call x1, Pallas kernels, bring_back(): pl.pallas_call(functools.partial(back_body, plan), in_specs=[ANY, ANY], o...  164 us
    pallas_call x1, Pallas kernels, send_rows(): pl.pallas_call(functools.partial(send_body, plan), in_specs=[ANY, ANY], o...  162 us
    psum x1, waiting for transfers between devices, per_device(): lax.psum((bias_table_grad, gain_one_grad, gain_two_grad, router_grad), both)  114 us
    psum x1, waiting for transfers between devices, per_device(): lax.psum([item.astype(jnp.bfloat16) for item in (query_grad, key_grad, va...  57.4 us
    psum x1, blocking collectives, per_device(): lax.psum((bias_table_grad, gain_one_grad, gain_two_grad, router_grad), both)  41.4 us
  transfers between devices with their start and end apart: 2, of which 2 were waited for; matrix products, arithmetic and copies ran while one was open for 8% of the time, Pallas kernels for 0%

profile of v1, /device:TPU:1, one launch (start us, length us, event | category | flops | bytes accessed | tf_op | source)
XLA Modules:
  0.0 1124.3 jit_solution(2814726051863461884)
XLA Ops:
  11.8 2.9 convolution_convert_fusion.6
  15.4 4.2 convolution_convert_fusion.5
  21.2 4.2 convolution_convert_fusion.7
  27.7 4.6 copy.76.refs_4_
  32.3 4.6 copy.77.refs_5_
  36.9 14.8 %fusion.1 = f32[512,512,16]{1,2,0:T(8,128)} fusion(s32[512,512]{1,0:T(8,128)} %fusion.28, f32[32,16]{0,1:T(8,128)S(1)} %copy-done.35), kind=kOutput, calls=%fused_computation.2 | convolution fusion | flops 1619001344 | bytes 17827840 | tf_op jit(solution)/shard_map/ijb,bh->hij/dot_general | solution.py:857
  51.7 19.3 %copy.72 = f32[512,512,16]{0,1,2:T(8,128)} copy(f32[512,512,16]{1,2,0:T(8,128)} %fusion.1) | data formatting | bytes 33554432 | tf_op jit(solution)/shard_map/ijb,bh->hij/dot_general | solution.py:857
  71.0 10.7 fusion.59
  81.7 8.4 fusion.4
  90.1 7.9 fusion.21
  104.3 161.6 %send_rows.1 = (bf16[2,2560,1024]{2,1,0:T(8,128)(2,1)}, f32[4,8,8,512]{3,2,1,0:T(8,128)}, bf16[4,512,1024]{2,1,0:T(8,128)(2,1)}) custom-call(bf16[512,1024]{1,0:T(8,128)(2,1)} %rows.1, f32[8,512]{1,0:T(8,128)} %pad.8.meta), custom_call_target="tpu_custom_call" | custom-call | tf_op jit(solution)/shard_map/send_rows/pallas_call | solution.py:464
  266.0 311.6 %run_experts.1 = (f32[512,1024]{1,0:T(8,128)}, f32[8,512]{1,0:T(8,128)}, bf16[2,2560,1024]{2,1,0:T(8,128)(2,1)}, bf16[2,2560,1024]{2,1,0:T(8,128)(2,1)}, bf16[2,...) custom-call(bf16[512,1024]{1,0:T(8,128)(2,1)} %fusion.20.refs_0_, ...), custom_call_target="tpu_custom_call" | custom-call | tf_op jit(solution)/shard_map/run_experts/pallas_call | solution.py:716
  579.1 5.8 multiply_reduce_fusion.1
  584.9 164.1 %bring_back.1 = (f32[512,1024]{1,0:T(8,128)}, bf16[4,2,640,1024]{3,2,1,0:T(8,128)(2,1)}, bf16[4,512,1024]{2,1,0:T(8,128)(2,1)}) custom-call(bf16[2,2560,1024]{2,1,0:T(8,128)(2,1)} %get-tuple-element.25.given, f32[4,8,8,512]{3,2,1,0:T(8,128)} %get-tuple-element.24.refs_3_.targets), custom_call_target="tpu_custom_call" | custom-call | tf_op jit(solution)/shard_map/bring_back/pallas_call | solution.py:789
  749.0 4.6 multiply_subtract_fusion
  759.1 9.6 fusion.22
  768.6 13.6 %multiply_reduce_fusion = (f32[16,512]{1,0:T(8,128)S(1)}, f32[16,512,512]{1,2,0:T(8,128)}) fusion(f32[16,512,512]{1,2,0:T(8,128)} %get-tuple-element.51, f32[16,512]{1,0:T(8,128)S(1)} %log_add_fusion, bf16[512,16,64]{0,2,1:T(8,128)(2,1)} %bitcast.90, bf16[512,16,64]{0,2,1:T(8,128)(2,1)} %bitcast.91), kind=kOutput, calls=%fused_computation.5 | convolution fusion | flops 549445632 | bytes 35717120 | tf_op jit(solution)/shard_map/qhd,khd->hqk/dot_general | solution.py:916
  782.7 10.6 multiply_convert_fusion
  793.4 6.5 multiply_convert_fusion.1
  801.8 2.8 convolution_convert_fusion.1
  804.6 2.8 convolution_convert_fusion.3
  807.4 2.8 convolution_convert_fusion.2
  813.8 15.7 %copy.82 = bf16[16,512,512]{2,0,1:T(8,128)(2,1)} copy(bf16[16,512,512]{1,2,0:T(8,128)(2,1)} %multiply_convert_fusion) | data formatting | bytes 16777216 | tf_op jit(solution)/shard_map/convert_element_type | solution.py:920
  829.5 4.5 fusion.60
  836.6 14.4 %fusion.64 = f32[2,704,1024]{2,1,0:T(8,128)} fusion(bf16[2,2560,704]{2,1,0:T(8,128)(2,1)} %get-tuple-element.32, bf16[2,2560,1024]{2,1,0:T(8,128)(2,1)} %get-tuple-element.23.refs_2_), kind=kOutput, calls=%fused_computation.106 | convolution fusion | flops 7381975040 | bytes 23461888 | tf_op jit(solution)/shard_map/xrf,xrd->xfd/dot_general | solution.py:887
  851.0 14.5 %fusion.62 = f32[2,1024,704]{1,2,0:T(8,128)} fusion(bf16[2,2560,1024]{2,1,0:T(8,128)(2,1)} %get-tuple-element.29, bf16[2,2560,704]{2,1,0:T(8,128)(2,1)} %get-tuple-element.30), kind=kOutput, calls=%fused_computation.104 | convolution fusion | flops 7381975040 | bytes 23461888 | tf_op jit(solution)/shard_map/xrd,xrf->xdf/dot_general | solution.py:888
  865.5 14.6 %fusion.63 = f32[2,1024,704]{1,2,0:T(8,128)} fusion(bf16[2,2560,1024]{2,1,0:T(8,128)(2,1)} %get-tuple-element.29, bf16[2,2560,704]{2,1,0:T(8,128)(2,1)} %get-tuple-element.31), kind=kOutput, calls=%fused_computation.105 | convolution fusion | flops 7381975040 | bytes 23461888 | tf_op jit(solution)/shard_map/xrd,xrf->xdf/dot_general | solution.py:889
  880.1 7.5 fusion.27
  891.5 41.4 %all-reduce.2 = (f32[1024]{0:T(1024)}, f32[32,16]{0,1:T(8,128)}, f32[1024]{0:T(1024)}) all-reduce(f32[1024]{0:T(1024)S(1)} %get-tuple-element.35, f32[32,16]{0,1:T(8,128)S(1)} %fusion.27, f32[1024]{0:T(1024)S(1)} %get-tuple-element.33), channel_id=1, replica_groups=mesh['expert'=8,'hidden'=4] {'expert','hidden'}, use_global_device_ids=true, to_apply=%region_14.15 | all-reduce | flops 2560 | bytes 20480 | tf_op jit(solution)/shard_map/psum | solution.py:959
  932.9 57.4 %all-reduce.9.cloned.1.call-done = (bf16[1024,1024]{1,0:T(8,128)(2,1)}, bf16[1024,1024]{1,0:T(8,128)(2,1)}, bf16[1024,1024]{1,0:T(8,128)(2,1)}, bf16[1024,1024]{1,0:T(8,128)(2,1)}) async-done(((bf16[1024,1024]{1,0:T(8,128)(2,1)}, bf16[1024,1024]{1,0:T(8,128)(2,1)}, bf16[1024,1024]{1,0:T(8,128)(2,1)}, bf16[1024,1024]{1,0:T(8,128)(2,1)}), (bf16[1024,1024]{1,0:T(8,128)(2,1)}, bf16[1024,1024]{1,0:T(8,128)(2,1)}, ...) | async-done | bytes 8388624 | tf_op jit(solution)/shard_map/psum | solution.py:951
  990.2 4.2 convert_element_type.216
  1001.9 113.9 %all-reduce.7.cloned.1.call-done = f32[1024,16]{0,1:T(8,128)} async-done(((f32[1024,16]{0,1:T(8,128)}), f32[1024,16]{0,1:T(8,128)}) %all-reduce.7.cloned.1.call-update) | async-done | bytes 65552 | tf_op jit(solution)/shard_map/psum | solution.py:959
  (133 shorter events, 43.8 us)
Async XLA Ops:
  7.2 93.7 %copy-start = (f32[1024,16]{0,1:T(8,128)S(1)}, f32[1024,16]{0,1:T(8,128)}, u32[]{:S(2)}) copy-start(f32[1024,16]{0,1:T(8,128)} %param.22) | copy-start | bytes 196612
  7.2 4.6 copy-start.5
  7.2 3.6 copy-start.33
  7.2 4.6 copy-start.34
  7.2 983.0 %all-reduce.9.cloned.1.call-start = ((), (), s32[]{:S(2)}) async-start(), calls=%async_computation.1 | async-start | bytes 16777216 | tf_op jit(solution)/shard_map/psum | solution.py:951
  15.4 55.6 %copy-start.9 = (bf16[512,1024]{0,1:T(8,128)(2,1)}, bf16[512,1024]{0,1:T(8,128)(2,1)S(1)}, u32[]{:S(2)}) copy-start(bf16[512,1024]{0,1:T(8,128)(2,1)S(1)} %copy.70) | copy-start | bytes 3145732
  21.2 49.9 %copy-start.7 = (bf16[512,1024]{0,1:T(8,128)(2,1)}, bf16[512,1024]{0,1:T(8,128)(2,1)S(1)}, u32[]{:S(2)}) copy-start(bf16[512,1024]{0,1:T(8,128)(2,1)S(1)} %copy.71) | copy-start | bytes 3145732
  32.3 4.6 copy-start.35
  81.7 8.4 copy-start.15
  90.1 7.9 copy-start.23
  99.4 3.6 copy-start.3
  584.9 164.1 %copy-start.14 = (bf16[512,1024]{1,0:T(8,128)(2,1)S(1)}, bf16[512,1024]{1,0:T(8,128)(2,1)}, u32[]{:S(2)}) copy-start(bf16[512,1024]{1,0:T(8,128)(2,1)} %rows.1) | copy-start | bytes 3145732
  749.0 4.6 copy-start.31
  759.0 23.2 %slice-start = ((s8[16777216]{0:T(1024)(128)(4,1)}), s8[4194304]{0:T(1024)(128)(4,1)S(1)}, s32[]{:S(2)}) async-start(s8[16777216]{0:T(1024)(128)(4,1)} %bitcast.83), calls=%async_computation.2 | async-start | bytes 8388608
  759.1 23.2 %slice-start.1 = ((s8[16777216]{0:T(1024)(128)(4,1)}), s8[4194304]{0:T(1024)(128)(4,1)S(1)}, s32[]{:S(2)}) async-start(s8[16777216]{0:T(1024)(128)(4,1)} %bitcast.83), calls=%async_computation.3 | async-start | bytes 8388608
  768.6 13.6 %slice-start.2 = ((s8[16777216]{0:T(1024)(128)(4,1)}), s8[4194304]{0:T(1024)(128)(4,1)S(1)}, s32[]{:S(2)}) async-start(s8[16777216]{0:T(1024)(128)(4,1)} %bitcast.83), calls=%async_computation.4 | async-start | bytes 8388608
  768.6 14.1 %slice-start.3 = ((s8[16777216]{0:T(1024)(128)(4,1)}), s8[4194304]{0:T(1024)(128)(4,1)S(1)}, s32[]{:S(2)}) async-start(s8[16777216]{0:T(1024)(128)(4,1)} %bitcast.83), calls=%async_computation.5 | async-start | bytes 8388608
  793.3 6.5 copy-start.2
  793.3 6.5 copy-start.8
  799.9 7.5 copy-start.28
  801.4 3.2 copy-start.18
  810.2 305.6 %all-reduce.7.cloned.1.call-start = ((), (), s32[]{:S(2)}) async-start(), calls=%async_computation | async-start | bytes 131072 | tf_op jit(solution)/shard_map/psum | solution.py:959
  813.8 15.7 %copy-start.19 = (bf16[16,64,512]{2,1,0:T(8,128)(2,1)S(1)}, bf16[16,64,512]{2,1,0:T(8,128)(2,1)}, u32[]{:S(2)}) copy-start(bf16[16,64,512]{2,1,0:T(8,128)(2,1)} %copy-done.18) | copy-start | bytes 3145732
  829.5 4.5 copy-start.29
  829.5 4.5 copy-start.37
  865.5 14.6 %copy-start.13 = (s32[512,512]{1,0:T(8,128)S(1)}, s32[512,512]{1,0:T(8,128)}, u32[]{:S(2)}) copy-start(s32[512,512]{1,0:T(8,128)} %fusion.28) | copy-start | bytes 3145732
  880.0 7.5 copy-start.17
  880.0 7.5 copy-start.25
  880.0 7.5 copy-start.26
  880.0 7.5 copy-start.27
  990.2 4.2 copy-start.22
  999.4 117.8 %copy-start.1 = (f32[1024,16]{0,1:T(8,128)S(1)}, f32[1024,16]{0,1:T(8,128)}, u32[]{:S(2)}) copy-start(f32[1024,16]{0,1:T(8,128)} %param.22) | copy-start | bytes 196612
  (12 other events, 23.1 us)
Sparse Core Ops, SparseCore 0:
  810.3 179.8 all-reduce.8
  996.4 119.3 all-reduce.6

commit v2 on v1

--- a/solution.py
+++ b/solution.py
@@ -21,15 +21,6 @@
 eps = 1e-06
 precise = lax.Precision.HIGHEST
 thresholds = (12, 16, 23, 32, 46, 64, 91)
-
-
-def bucket_ids(length):
-    position = jnp.arange(length, dtype=jnp.int32)
-    offset = position[None, :] - position[:, None]
-    distance = jnp.abs(offset)
-    far_bucket = 8 + sum(((distance >= threshold).astype(jnp.int32) for threshold in thresholds))
-    near_bucket = jnp.where(distance < 8, distance, far_bucket)
-    return near_bucket + 16 * (offset > 0).astype(jnp.int32)
 
 
 def contract_last(matrix_a, matrix_b, mode=None):
@@ -81,6 +72,10 @@
 
     def place(self):
         return lax.axis_index("expert"), lax.axis_index("hidden")
+
+    def source(self, z, chunk):
+        sign = 1 - 2 * lax.div(z, self.n_h // 2)
+        return lax.rem(z + self.n_h + sign * chunk, self.n_h)
 
 
 def across(here, mask):
@@ -149,9 +144,9 @@
         dma = pltpu.SemaphoreType.DMA
         n_h, n_e = plan.n_h, plan.n_e
         return [
+            dma((n_h, 2)),
             dma((n_h,)),
-            dma((n_h,)),
-            dma((n_h,)),
+            dma((n_h, 2)),
             dma((n_h,)),
             dma((2, n_e)),
             dma((n_h, n_e)),
@@ -160,33 +155,61 @@
             dma((3,)),
         ]
 
-    def along_z(self, shift):
+    def hop(self, source, way, own):
         e, z = self.plan.place()
-        peer = (e, lax.rem(z + self.plan.n_h - shift, self.plan.n_h))
+        sems = [
+            (self.z_send.at[source, (way + 1) // 2], self.z_recv.at[source]),
+            (self.zm_send.at[source, (way + 1) // 2], self.zm_recv.at[source]),
+        ]
         return (
+            remote(self.meta_v.at[source], self.meta_v.at[source], *sems[1], (e, z + way)),
             remote(
-                self.meta,
-                self.meta_v.at[shift],
-                self.zm_send.at[shift],
-                self.zm_recv.at[shift],
-                peer,
+                self.rows if own else self.land.at[source],
+                self.land.at[source],
+                *sems[0],
+                (e, z + way),
             ),
-            remote(
-                self.rows,
-                self.land.at[shift],
-                self.z_send.at[shift],
-                self.z_recv.at[shift],
-                peer,
-            ),
-        )
+        )
+
+    def on_the_way(self, distance, act):
+        n_h = self.plan.n_h
+        _, z = self.plan.place()
+
+        @pl.when(z + distance < n_h)
+        def _():
+            act(z + distance, z > 0, -1)
+
+        @pl.when(z >= distance)
+        def _():
+            act(z - distance, z < n_h - 1, 1)
 
     def begin(self):
-        for shift in range(1, self.plan.n_h):
-            for copy in self.along_z(shift):
-                copy.start()
-        copy = pltpu.make_async_copy(self.meta, self.meta_v.at[0], self.local.at[1])
+        _, z = self.plan.place()
+        copy = pltpu.make_async_copy(self.meta, self.meta_v.at[z], self.local.at[1])
         copy.start()
         copy.wait()
+
+        @pl.when(z > 0)
+        def _():
+            for copy in self.hop(z, -1, True):
+                copy.start()
+
+        @pl.when(z < self.plan.n_h - 1)
+        def _():
+            for copy in self.hop(z, 1, True):
+                copy.start()
+
+    def pass_on(self, distance):
+        def act(source, forwarded, way):
+            for copy in self.hop(source, way, False):
+                copy.wait_recv()
+
+            @pl.when(forwarded)
+            def _():
+                for copy in self.hop(source, way, False):
+                    copy.start()
+
+        self.on_the_way(distance, act)
 
     def in_plane(self, chunk, mask):
         plan = self.plan
@@ -204,7 +227,7 @@
     def meta_copy(self, chunk, mask):
         e, z = self.plan.place()
         return remote(
-            self.meta_v.at[chunk],
+            self.meta_v.at[self.plan.source(z, chunk)],
             self.meta_out.at[chunk, mask],
             self.m_send.at[chunk, mask],
             self.m_recv.at[chunk, mask],
@@ -213,8 +236,9 @@
 
     def chunk(self, chunk, target_of):
         plan = self.plan
-        e, _ = plan.place()
+        e, z = plan.place()
         buffer = lax.rem(chunk, 2)
+        source = plan.source(z, chunk)
 
         @pl.when(chunk == 0)
         def _():
@@ -224,10 +248,9 @@
 
         @pl.when(chunk > 0)
         def _():
-            for copy in self.along_z(chunk):
-                copy.wait_recv()
+            self.pass_on(chunk)
             copy = pltpu.make_async_copy(
-                self.land.at[chunk], self.rows_v.at[buffer], self.local.at[0]
+                self.land.at[source], self.rows_v.at[buffer], self.local.at[0]
             )
             copy.start()
             copy.wait()
@@ -235,7 +258,7 @@
         for mask in range(1, plan.n_e):
             self.meta_copy(chunk, mask).start()
         own_meta = pltpu.make_async_copy(
-            self.meta_v.at[chunk], self.meta_out.at[chunk, 0], self.local.at[1]
+            self.meta_v.at[source], self.meta_out.at[chunk, 0], self.local.at[1]
         )
         own_meta.start()
 
@@ -281,9 +304,26 @@
         for chunk in range(max(0, plan.n_h - 2), plan.n_h):
             for mask in range(1, plan.n_e):
                 self.in_plane(chunk, mask).wait_send()
-        for shift in range(1, plan.n_h):
-            for copy in self.along_z(shift):
+        _, z = plan.place()
+
+        @pl.when(z > 0)
+        def _():
+            for copy in self.hop(z, -1, True):
                 copy.wait_send()
+
+        @pl.when(z < plan.n_h - 1)
+        def _():
+            for copy in self.hop(z, 1, True):
+                copy.wait_send()
+
+        def act(source, forwarded, way):
+            @pl.when(forwarded)
+            def _():
+                for copy in self.hop(source, way, False):
+                    copy.wait_send()
+
+        for distance in range(1, plan.n_h):
+            self.on_the_way(distance, act)
         for chunk in range(plan.n_h):
             for mask in range(1, plan.n_e):
                 self.meta_copy(chunk, mask).wait_send()
@@ -340,10 +380,17 @@
         e, z = self.plan.place()
         return remote(
             self.rows_v.at[lax.rem(chunk, 2)],
-            self.land.at[chunk],
+            self.land.at[z],
             self.s_send.at[chunk],
-            self.s_recv.at[chunk],
-            (e, lax.rem(z + chunk, self.plan.n_h)),
+            self.s_recv.at[z],
+            (e, self.plan.source(z, chunk)),
+        )
+
+    def from_z(self, distance):
+        e, z = self.plan.place()
+        other = lax.rem(z + distance, self.plan.n_h)
+        return other, remote(
+            self.rows_v.at[0], self.land.at[other], self.s_send.at[0], self.s_recv.at[other], (e, other)
         )
 
     def combine(self, chunk, target):
@@ -388,14 +435,13 @@
         plan = self.plan
         for chunk in range(max(1, plan.n_h - 2), plan.n_h):
             self.along_z(chunk).wait_send()
-        for chunk in range(1, plan.n_h):
-            self.along_z(chunk).wait_recv()
-            copy = pltpu.make_async_copy(
-                self.land.at[chunk], self.rows_v.at[chunk % 2], self.local.at[0]
-            )
+        for distance in range(1, plan.n_h):
+            other, arrival = self.from_z(distance)
+            arrival.wait_recv()
+            copy = pltpu.make_async_copy(self.land.at[other], self.rows_v.at[0], self.local.at[0])
             copy.start()
             copy.wait()
-            self.total[...] += self.rows_v[chunk % 2].astype(jnp.float32)
+            self.total[...] += self.rows_v[0].astype(jnp.float32)
         copy = pltpu.make_async_copy(self.total, self.out, self.local.at[0])
         copy.start()
         copy.wait()
@@ -453,7 +499,10 @@
     greet(plan)
     work = Dispatch(plan, rows, meta, land, out, meta_out, rows_v, meta_v, stage, sems)
     work.begin()
-    pl.loop(0, plan.n_h)(lambda chunk: work.chunk(chunk, lambda at: meta_v[at]))
+    _, z = plan.place()
+    pl.loop(0, plan.n_h)(
+        lambda chunk: work.chunk(chunk, lambda at: meta_v[plan.source(z, at)])
+    )
     for chunk in range(plan.n_h):
         work.arrived(chunk)
     work.finish()
@@ -570,10 +619,16 @@
     def gg_along(chunk):
         return remote(
             gg_part.at[chunk],
-            gg_land.at[chunk],
+            gg_land.at[z],
             ggs_send.at[chunk],
-            ggs_recv.at[chunk],
-            (e, lax.rem(z + chunk, n_h)),
+            ggs_recv.at[z],
+            (e, plan.source(z, chunk)),
+        )
+
+    def gg_from(distance):
+        other = lax.rem(z + distance, n_h)
+        return other, remote(
+            gg_part.at[0], gg_land.at[other], ggs_send.at[0], ggs_recv.at[other], (e, other)
         )
 
     def outs(chunk, j):
@@ -585,6 +640,7 @@
             )
         ]
 
+    own_last = 1 if n_h <= dx_v.shape[0] else 0
     masks = n_e // halves
     piece = masks * plan.stride
 
@@ -592,8 +648,8 @@
         j, half = lax.div(index, halves), lax.rem(index, halves)
         at = pl.ds(pl.multiple_of(half * piece, 16), piece)
         rows, grads_in = x_v[j, at, :], g_v[j, at, :]
-        gate_pre = dot(rows, wg_v[j])
-        up_pre = dot(rows, wu_v[j])
+        gate_pre = contract_last(rows, wg_v[j])
+        up_pre = contract_last(rows, wu_v[j])
         raw = contract_last(grads_in, wd_v[j])
         slots = lax.broadcasted_iota(jnp.int32, (plan.stride, LEN), 0).astype(
             jnp.float32
@@ -631,7 +687,7 @@
         dup_v[j, at, :] = grad_up
         act_v[j, at, :] = (act * gate).astype(jnp.bfloat16)
         dx_v[lax.rem(chunk, dx_v.shape[0]), j, at, :] = (
-            contract_last(grad_gate, wg_v[j]) + contract_last(grad_up, wu_v[j])
+            dot(grad_gate, wg_v[j]) + dot(grad_up, wu_v[j])
         ).astype(jnp.bfloat16)
         y_v[j, at, :] = (dot(act_low, wd_v[j]) * gate).astype(jnp.bfloat16)
 
@@ -663,7 +719,11 @@
         pl.loop(0, 2 * halves)(lambda index: step(chunk, index))
         for mask in range(1, n_e):
             gg_copy(chunk, mask).start()
-        give.send(chunk)
+
+        @pl.when(chunk >= own_last)
+        def _():
+            give.send(chunk)
+
         for j in range(2):
             for copy in outs(chunk, j):
                 copy.start()
@@ -672,13 +732,16 @@
         def _():
             work.chunk(chunk + ahead, lambda at: target_v[at, 0])
 
+    if own_last:
+        give.send(0)
     work.finish()
     for j in range(2):
         for copy in outs(n_h - 1, j):
             copy.wait()
 
     @pl.loop(0, n_h)
-    def _(chunk):
+    def _(turn):
+        chunk = lax.rem(turn + own_last, n_h)
         part = gg_v[chunk, 0]
         for mask in range(1, n_e):
             gg_copy(chunk, mask).wait_recv()
@@ -696,9 +759,10 @@
         for mask in range(1, n_e):
             gg_copy(chunk, mask).wait_send()
     sum_gg = gg_part[0]
-    for chunk in range(1, n_h):
-        gg_along(chunk).wait_recv()
-        sum_gg = sum_gg + gg_land[chunk]
+    for distance in range(1, n_h):
+        other, arrival = gg_from(distance)
+        arrival.wait_recv()
+        sum_gg = sum_gg + gg_land[other]
     gg_out[...] = sum_gg
     for chunk in range(1, n_h):
         gg_along(chunk).wait_send()
@@ -734,8 +798,8 @@
             pltpu.VMEM((2, LEN, D), bf16),
             pltpu.VMEM((n_h, 8, LEN), f32),
             pltpu.VMEM((2, 2, plan.rows, D), bf16),
-            pltpu.VMEM((2, D, width), bf16),
-            pltpu.VMEM((2, D, width), bf16),
+            pltpu.VMEM((2, width, D), bf16),
+            pltpu.VMEM((2, width, D), bf16),
             pltpu.VMEM((2, width, D), bf16),
             pltpu.VMEM((n_h, n_e, 8, LEN), f32),
             pltpu.VMEM((n_e, 8, LEN), f32),
@@ -766,7 +830,7 @@
             collective_id=2, has_side_effects=True, vmem_limit_bytes=VMEM
         ),
         name="run_experts",
-    )(sent, gates, grads, targets, w_gate, w_up, w_down)
+    )(sent, gates, grads, targets, jnp.swapaxes(w_gate, 1, 2), jnp.swapaxes(w_up, 1, 2), w_down)
 
 
 def back_body(plan, given, targets, out, back, land, rows_v, stage, target_v, total, t_sem, *sems):
@@ -774,10 +838,16 @@
     targets_in.start()
     greet(plan)
     give = ReturnHeld(plan, given, back, land, out, stage, rows_v, total, sems)
-    for chunk in range(plan.n_h):
+    order = [chunk for chunk in range(1, plan.n_h)] + [0]
+    for chunk in order:
         give.send(chunk)
     targets_in.wait()
-    pl.loop(0, plan.n_h)(lambda chunk: give.combine(chunk, target_v[chunk, 0]))
+
+    @pl.loop(0, plan.n_h)
+    def _(turn):
+        chunk = lax.rem(turn + 1, plan.n_h)
+        give.combine(chunk, target_v[chunk, 0])
+
     give.sent()
     give.finish()
 
@@ -810,6 +880,148 @@
     )(given, targets)[0]
 
 
+NEAR = 128
+
+
+def offset_buckets():
+    offset = jnp.arange(4 * NEAR, dtype=jnp.int32) - 2 * NEAR
+    distance = jnp.abs(offset)
+    far_bucket = 8 + sum(((distance >= threshold).astype(jnp.int32) for threshold in thresholds))
+    bucket = jnp.where(distance < 8, distance, far_bucket) + 16 * (offset > 0).astype(jnp.int32)
+    return (bucket[:, None] == jnp.arange(BUCKETS, dtype=jnp.int32)).astype(jnp.float32)
+
+
+def bias_tiles(line):
+    return pltpu.roll(
+        jnp.broadcast_to(line, (NEAR, 4 * NEAR)), 0, 1, stride=1, stride_axis=0
+    )
+
+
+def mix_head(query, key, value, line, soft_ref, head):
+    tiles = bias_tiles(line)
+    blocks = LEN // NEAR
+    outs = []
+    for i in range(blocks):
+        raw = contract_last(query[i * NEAR : (i + 1) * NEAR], key) * (HEAD_DIM**-0.5)
+        parts = []
+        for j in range(blocks):
+            part = raw[:, j * NEAR : (j + 1) * NEAR]
+            if abs(j - i) <= 1:
+                parts.append(part + tiles[:, (j - i + 2) * NEAR : (j - i + 3) * NEAR])
+            else:
+                edge = 1 if j < i else 4 * NEAR - 1
+                parts.append(part + line[:, edge : edge + 1])
+        scores = jnp.concatenate(parts, axis=1)
+        terms = jnp.exp(scores - jnp.max(scores, axis=1, keepdims=True))
+        soft = (terms * (1.0 / jnp.sum(terms, axis=1, keepdims=True))).astype(jnp.bfloat16)
+        soft_ref[head, i * NEAR : (i + 1) * NEAR, :] = soft
+        outs.append(dot(soft, value))
+    return jnp.concatenate(outs, axis=0).astype(jnp.bfloat16)
+
+
+def mix_body(query_ref, key_ref, value_ref, line_ref, soft_ref, mixed_ref):
+    for head in range(2):
+        at = slice(head * HEAD_DIM, (head + 1) * HEAD_DIM)
+        mixed_ref[:, at] = mix_head(
+            query_ref[:, at],
+            key_ref[:, at],
+            value_ref[:, at],
+            line_ref[0, head : head + 1, :],
+            soft_ref,
+            head,
+        )
+
+
+def mix(query, key, value, lines):
+    pair = pl.BlockSpec((LEN, 2 * HEAD_DIM), lambda i: (0, i))
+    return pl.pallas_call(
+        mix_body,
+        grid=(HEADS // 2,),
+        in_specs=[pair, pair, pair, pl.BlockSpec((1, 2, 4 * NEAR), lambda i: (i, 0, 0))],
+        out_specs=[pl.BlockSpec((2, LEN, LEN), lambda i: (i, 0, 0)), pair],
+        out_shape=[
+            jax.ShapeDtypeStruct((HEADS, LEN, LEN), jnp.bfloat16),
+            jax.ShapeDtypeStruct((LEN, D), jnp.bfloat16),
+        ],
+        compiler_params=pltpu.CompilerParams(vmem_limit_bytes=VMEM),
+        name="mix",
+    )(query, key, value, lines.reshape(HEADS // 2, 2, 4 * NEAR))
+
+
+def unmix_head(query, key, value, grad_mixed, soft_ref, grads_v, head):
+    blocks = LEN // NEAR
+    near = [jnp.zeros((NEAR, NEAR), jnp.float32) for _ in range(3)]
+    below = jnp.zeros((NEAR, NEAR), jnp.float32)
+    above = jnp.zeros((NEAR, NEAR), jnp.float32)
+    grad_query = []
+    for i in range(blocks):
+        at = slice(i * NEAR, (i + 1) * NEAR)
+        soft = soft_ref[head, at, :].astype(jnp.float32)
+        grad_soft = contract_last(grad_mixed[at], value)
+        product = soft * grad_soft
+        grad = product - soft * jnp.sum(product, axis=1, keepdims=True)
+        low = grad.astype(jnp.bfloat16)
+        grads_v[at, :] = low
+        grad_query.append(dot(low, key))
+        wide = low.astype(jnp.float32)
+        for j in range(blocks):
+            part = wide[:, j * NEAR : (j + 1) * NEAR]
+            if abs(j - i) <= 1:
+                near[j - i + 1] = near[j - i + 1] + part
+            elif j < i:
+                below = below + part
+            else:
+                above = above + part
+    band = jnp.concatenate([jnp.zeros((NEAR, NEAR), jnp.float32)] + near, axis=1)
+    eight = band[0:8]
+    for i in range(8, NEAR, 8):
+        eight = eight + pltpu.roll(band[i : i + 8], 4 * NEAR - i, 1)
+    row = lax.broadcasted_iota(jnp.int32, (8, 4 * NEAR), 0)
+    for bit in (1, 2, 4):
+        eight = jnp.where(lax.rem(lax.div(row, bit), 2) == 1, pltpu.roll(eight, 4 * NEAR - bit, 1), eight)
+    line = jnp.sum(eight, axis=0, keepdims=True)
+    column = lax.broadcasted_iota(jnp.int32, (1, 4 * NEAR), 1)
+    line = line + jnp.where(column == 1, jnp.sum(below), 0.0)
+    line = line + jnp.where(column == 4 * NEAR - 1, jnp.sum(above), 0.0)
+    scaling = HEAD_DIM**-0.5
+    grad_query = (jnp.concatenate(grad_query, axis=0) * scaling).astype(jnp.bfloat16)
+    grad_key = (contract_first(grads_v[...], query) * scaling).astype(jnp.bfloat16)
+    grad_value = contract_first(soft_ref[head], grad_mixed).astype(jnp.bfloat16)
+    return grad_query, grad_key, grad_value, line
+
+
+def unmix_body(
+    query_ref, key_ref, value_ref, grad_ref, soft_ref, dq_ref, dk_ref, dv_ref, line_ref, grads_v
+):
+    for head in range(2):
+        at = slice(head * HEAD_DIM, (head + 1) * HEAD_DIM)
+        dq_ref[:, at], dk_ref[:, at], dv_ref[:, at], line_ref[0, head : head + 1, :] = unmix_head(
+            query_ref[:, at],
+            key_ref[:, at],
+            value_ref[:, at],
+            grad_ref[:, at],
+            soft_ref,
+            grads_v,
+            head,
+        )
+
+
+def unmix(query, key, value, grad_mixed, soft):
+    pair = pl.BlockSpec((LEN, 2 * HEAD_DIM), lambda i: (0, i))
+    rows = jax.ShapeDtypeStruct((LEN, D), jnp.bfloat16)
+    out = pl.pallas_call(
+        unmix_body,
+        grid=(HEADS // 2,),
+        in_specs=[pair] * 4 + [pl.BlockSpec((2, LEN, LEN), lambda i: (i, 0, 0))],
+        out_specs=[pair] * 3 + [pl.BlockSpec((1, 2, 4 * NEAR), lambda i: (i, 0, 0))],
+        out_shape=[rows] * 3 + [jax.ShapeDtypeStruct((HEADS // 2, 2, 4 * NEAR), jnp.float32)],
+        scratch_shapes=[pltpu.VMEM((LEN, LEN), jnp.bfloat16)],
+        compiler_params=pltpu.CompilerParams(vmem_limit_bytes=VMEM),
+        name="unmix",
+    )(query, key, value, grad_mixed, soft)
+    return out[0], out[1], out[2], out[3].reshape(HEADS, 4 * NEAR)
+
+
 def per_device(
     n_e,
     n_h,
@@ -833,44 +1045,20 @@
     both = ("expert", "hidden")
 
     def small(array):
-        return jnp.pad(array.astype(jnp.float32), ((0, 6), (0, 0)))
+        return jnp.pad(array.astype(jnp.float32), ((0, 8 - array.shape[0]), (0, 0)))
 
     targets = small(slot_targets(routes, experts_all, plan.capacity, plan.stride))
     grads_in, targets_all = send_rows(plan, cotangent, targets)
-    scaling = HEAD_DIM ** (-0.5)
-    bucket_hot = (bucket_ids(LEN)[:, :, None] == jnp.arange(BUCKETS, dtype=jnp.int32)).astype(
-        jnp.float32
-    )
+    hot_bucket = offset_buckets()
     inputs = tokens.astype(jnp.float32)
     inv_one = lax.rsqrt(jnp.mean(inputs * inputs, axis=-1, keepdims=True) + eps)
     normed_one = (inputs * inv_one * gain_one).astype(jnp.bfloat16)
-    query_rows = jnp.dot(normed_one, w_query, preferred_element_type=jnp.float32).astype(
-        jnp.bfloat16
-    )
-    key_rows = jnp.dot(normed_one, w_key, preferred_element_type=jnp.float32).astype(jnp.bfloat16)
-    value_rows = jnp.dot(normed_one, w_value, preferred_element_type=jnp.float32).astype(
-        jnp.bfloat16
-    )
-    query_heads = query_rows.reshape(LEN, HEADS, HEAD_DIM)
-    key_heads = key_rows.reshape(LEN, HEADS, HEAD_DIM)
-    value_heads = value_rows.reshape(LEN, HEADS, HEAD_DIM)
-    bias_rows = jnp.einsum("ijb,bh->hij", bucket_hot, bias_table, precision=precise)
-
-    def score_of():
-        raw = jnp.einsum("qhd,khd->hqk", query_heads, key_heads, preferred_element_type=jnp.float32)
-        return raw * scaling + bias_rows
-
-    scores = score_of()
-    row_peak = jnp.max(scores, axis=-1, keepdims=True)
-    exp_terms = jnp.exp(scores - row_peak)
-    row_total = jnp.sum(exp_terms, axis=-1, keepdims=True)
-    log_total = row_peak + jnp.log(row_total)
-    soft_low = (exp_terms / row_total).astype(jnp.bfloat16)
-    mixed_rows = jnp.einsum(
-        "hqk,khd->qhd", soft_low, value_heads, preferred_element_type=jnp.float32
-    )
-    mixed_rows = mixed_rows.reshape(LEN, D).astype(jnp.bfloat16)
-    hidden = inputs + jnp.dot(mixed_rows, w_out, preferred_element_type=jnp.float32)
+    query_rows = dot(normed_one, w_query).astype(jnp.bfloat16)
+    key_rows = dot(normed_one, w_key).astype(jnp.bfloat16)
+    value_rows = dot(normed_one, w_value).astype(jnp.bfloat16)
+    lines = jnp.dot(hot_bucket, bias_table, precision=precise).T
+    soft, mixed_rows = mix(query_rows, key_rows, value_rows, lines)
+    hidden = inputs + dot(mixed_rows, w_out)
     inv_two = lax.rsqrt(jnp.mean(hidden * hidden, axis=-1, keepdims=True) + eps)
     normed_two = hidden * inv_two * gain_two
     sent = normed_two.astype(jnp.bfloat16)
@@ -881,20 +1069,14 @@
     grad_sent, grad_gates, rows_in, y_rows, gate_rows, up_rows, act_rows = run_experts(
         plan, sent, small(gate_values.T), grads_in, targets_all, w_gate, w_up, w_down
     )[:7]
-    branch = bring_back(plan, y_rows, targets_all)
     grad_gates = grad_gates[:2].T
-    block_out = (hidden + branch).astype(jnp.bfloat16)
-    down_grad = jnp.einsum("xrf,xrd->xfd", act_rows, grads_in, preferred_element_type=jnp.float32)
-    gate_grad = jnp.einsum("xrd,xrf->xdf", rows_in, gate_rows, preferred_element_type=jnp.float32)
-    up_grad = jnp.einsum("xrd,xrf->xdf", rows_in, up_rows, preferred_element_type=jnp.float32)
     grad_out = cotangent.astype(jnp.float32)
     grad_chosen = gate_values * (
         grad_gates - jnp.sum(gate_values * grad_gates, axis=-1, keepdims=True)
     )
     grad_logits = jnp.sum(route_hot * grad_chosen[:, :, None], axis=1)
-    router_grad = contract_first(normed_two, grad_logits, precise)
-    grad_normed_two = contract_last(grad_logits, w_router, precise)
-    grad_normed_two = grad_normed_two + grad_sent.astype(jnp.float32)
+    router_grad = contract_first(grad_logits, normed_two, precise)
+    grad_normed_two = contract_last(grad_logits, w_router, precise) + grad_sent
     gain_two_grad = jnp.sum(grad_normed_two * hidden * inv_two, axis=0)
     scaled_two = grad_normed_two * gain_two
     grad_hidden = (
@@ -904,40 +1086,18 @@
     )
     grad_branch = grad_hidden.astype(jnp.bfloat16)
     w_out_grad = contract_first(mixed_rows, grad_branch)
-    grad_mixed = (
-        contract_last(grad_branch, w_out).astype(jnp.bfloat16).reshape(LEN, HEADS, HEAD_DIM)
-    )
-    soft_again = jnp.exp(score_of() - log_total)
-    soft_again_low = soft_again.astype(jnp.bfloat16)
-    grad_value_heads = jnp.einsum(
-        "hqk,qhd->khd", soft_again_low, grad_mixed, preferred_element_type=jnp.float32
-    )
-    grad_value_rows = grad_value_heads.astype(jnp.bfloat16).reshape(LEN, D)
-    grad_soft = jnp.einsum(
-        "qhd,khd->hqk", grad_mixed, value_heads, preferred_element_type=jnp.float32
-    )
-    grad_scores = soft_again * (grad_soft - jnp.sum(soft_again * grad_soft, axis=-1, keepdims=True))
-    grad_scores = grad_scores.astype(jnp.bfloat16)
-    bias_table_grad = jnp.einsum(
-        "hij,ijb->bh", grad_scores.astype(jnp.float32), bucket_hot, precision=precise
-    )
-    grad_query_rows = (
-        jnp.einsum("hqk,khd->qhd", grad_scores, key_heads, preferred_element_type=jnp.float32)
-        * scaling
-    )
-    grad_query_rows = grad_query_rows.astype(jnp.bfloat16).reshape(LEN, D)
-    grad_key_rows = (
-        jnp.einsum("hqk,qhd->khd", grad_scores, query_heads, preferred_element_type=jnp.float32)
-        * scaling
-    )
-    grad_key_rows = grad_key_rows.astype(jnp.bfloat16).reshape(LEN, D)
-    query_grad = contract_first(normed_one, grad_query_rows)
-    key_grad = contract_first(normed_one, grad_key_rows)
-    value_grad = contract_first(normed_one, grad_value_rows)
+    grad_mixed = contract_last(grad_branch, w_out).astype(jnp.bfloat16)
+    grad_query, grad_key, grad_value, grad_lines = unmix(
+        query_rows, key_rows, value_rows, grad_mixed, soft
+    )
+    bias_table_grad = jnp.dot(grad_lines, hot_bucket, precision=precise).T
+    query_grad = contract_first(normed_one, grad_query)
+    key_grad = contract_first(normed_one, grad_key)
+    value_grad = contract_first(normed_one, grad_value)
     grad_normed_one = (
-        contract_last(grad_query_rows, w_query)
-        + contract_last(grad_key_rows, w_key)
-        + contract_last(grad_value_rows, w_value)
+        contract_last(grad_query, w_query)
+        + contract_last(grad_key, w_key)
+        + contract_last(grad_value, w_value)
     )
     gain_one_grad = jnp.sum(grad_normed_one * inputs * inv_one, axis=0)
     scaled_one = grad_normed_one * gain_one
@@ -946,30 +1106,30 @@
         + inv_one * scaled_one
         - inputs * inv_one**3 * jnp.mean(scaled_one * inputs, axis=-1, keepdims=True)
     )
-    query_grad, key_grad, value_grad, w_out_grad = [
-        item.astype(jnp.float32)
-        for item in lax.psum(
-            [
-                item.astype(jnp.bfloat16)
-                for item in (query_grad, key_grad, value_grad, w_out_grad)
-            ],
-            both,
-        )
+    last = jnp.pad(bias_table_grad.reshape(1, BUCKETS * HEADS), ((0, 0), (0, D - BUCKETS * HEADS)))
+    few = jnp.concatenate([router_grad, gain_one_grad[None], gain_two_grad[None], last], axis=0)
+    few = jnp.pad(few, ((0, -few.shape[0] % 16), (0, 0)))
+    low = [
+        item.astype(jnp.bfloat16) for item in (query_grad, key_grad, value_grad, w_out_grad, few)
     ]
-    bias_table_grad, gain_one_grad, gain_two_grad, router_grad = lax.psum(
-        (bias_table_grad, gain_one_grad, gain_two_grad, router_grad), both
-    )
+    low, gate_rows, up_rows, act_rows, y_rows = lax.optimization_barrier(
+        (low, gate_rows, up_rows, act_rows, y_rows)
+    )
+    summed = [item.astype(jnp.float32) for item in lax.psum(low, both)]
+    few = summed[4]
+    branch = bring_back(plan, y_rows, targets_all)
+    block_out = (hidden + branch).astype(jnp.bfloat16)
+    down_grad = jnp.einsum("xrf,xrd->xfd", act_rows, grads_in, preferred_element_type=jnp.float32)
+    gate_grad = jnp.einsum("xrd,xrf->xdf", rows_in, gate_rows, preferred_element_type=jnp.float32)
+    up_grad = jnp.einsum("xrd,xrf->xdf", rows_in, up_rows, preferred_element_type=jnp.float32)
     return (
         block_out,
         tokens_grad,
-        gain_one_grad,
-        query_grad,
-        key_grad,
-        value_grad,
-        w_out_grad,
-        bias_table_grad,
-        gain_two_grad,
-        router_grad,
+        few[experts_all],
+        *summed[:4],
+        few[experts_all + 2, : BUCKETS * HEADS].reshape(BUCKETS, HEADS),
+        few[experts_all + 1],
+        few[:experts_all].T,
         gate_grad,
         up_grad,
         down_grad,

time: 1130 us -> 832 us (0.74)
  waiting for transfers between devices: 171 us -> 17.4 us
  matrix products: 160 us -> 91.2 us
  local copies, waits for them, and re-layouts: 56.2 us -> 7.73 us
  blocking collectives: 41.4 us -> 0 us
  Pallas kernels: 637 us -> 673 us
  other arithmetic: 43.8 us -> 22.4 us
    psum x2 -> x1, waiting for transfers between devices: 171 us -> 17.3 us  [per_device(): summed = [item.astype(jnp.float32) for item in lax.psum(low, both)]]
    dot_general x12 -> x6, matrix products: 84.7 us -> 13.1 us  [the longest x4 11.8 us: dot(): return jnp.dot(matrix_a, matrix_b, preferred_element_type=jnp.float32)]
    pallas_call x0 -> x2, Pallas kernels: none -> 55.5 us  [the longest x1 28.7 us: unmix(): pl.pallas_call(unmix_body, grid=(HEADS // 2,), in_specs=[pair] * 4 + [pl....]
    psum x1 -> x0, blocking collectives: 41.4 us -> none  [per_device(): lax.psum((bias_table_grad, gain_one_grad, gain_two_grad, router_grad), both)]
    pallas_call x1, Pallas kernels: 164 us -> 198 us  [bring_back(): pl.pallas_call(functools.partial(back_body, plan), in_specs=[ANY, ANY], o...]
    pallas_call x1, Pallas kernels: 162 us -> 129 us  [send_rows(): pl.pallas_call(functools.partial(send_body, plan), in_specs=[ANY, ANY], o...]
    pallas_call x1, Pallas kernels: 312 us -> 291 us  [run_experts(): pl.pallas_call(functools.partial(expert_body, plan, halves, len(d_sems)),...]
    convert_element_type x5 -> x0, local copies, waits for them, and re-layouts: 20.7 us -> none  [the longest x1 15.7 us: per_device(): grad_scores = grad_scores.astype(jnp.bfloat16)]
  transfers between devices with their start and end apart: 2 -> 1, of which waited for: 2 -> 1; matrix products, arithmetic and copies ran while one was open for 8% -> 6% of each run, Pallas kernels for 0% -> 24%
where the time goes in v2:
time: 832 us; the launch traced here: 826 us
  Pallas kernels  673 us (81%)
  matrix products  91.2 us (11%)
  other arithmetic  22.4 us (3%)
  waiting for transfers between devices  17.4 us (2%)
  between operations  14.9 us (2%)
    pallas_call x1, Pallas kernels, run_experts(): pl.pallas_call(functools.partial(expert_body, plan, halves, len(d_sems)),...  291 us
    pallas_call x1, Pallas kernels, bring_back(): pl.pallas_call(functools.partial(back_body, plan), in_specs=[ANY, ANY], o...  198 us
    pallas_call x1, Pallas kernels, send_rows(): pl.pallas_call(functools.partial(send_body, plan), in_specs=[ANY, ANY], o...  129 us
    pallas_call x1, Pallas kernels, unmix(): pl.pallas_call(unmix_body, grid=(HEADS // 2,), in_specs=[pair] * 4 + [pl....  28.7 us
    pallas_call x1, Pallas kernels, mix(): pl.pallas_call(mix_body, grid=(HEADS // 2,), in_specs=[pair, pair, pair,...  26.8 us
    psum x1, waiting for transfers between devices, per_device(): summed = [item.astype(jnp.float32) for item in lax.psum(low, both)]  17.3 us
  transfers between devices with their start and end apart: 1, of which 1 were waited for; matrix products, arithmetic and copies ran while one was open for 6% of the time, Pallas kernels for 24%

profile of v2, /device:TPU:1, one launch (start us, length us, event | category | flops | bytes accessed | tf_op | source)
XLA Modules:
  0.0 826.5 jit_solution(10895505100809597948)
XLA Ops:
  7.4 1.6 fusion
  12.3 4.0 convolution_convert_fusion.6.key_ref
  16.3 2.3 convolution_convert_fusion.5.value_ref
  18.6 2.3 convolution_convert_fusion.7.query_ref
  20.9 26.8 %mix.1 = (bf16[16,512,512]{2,1,0:T(8,128)(2,1)}, bf16[512,1024]{1,0:T(8,128)(2,1)}) custom-call(bf16[512,1024]{1,0:T(8,128)(2,1)} %convolution_convert_fusion.7.query_ref, bf16[512,1024]{1,0:T(8,128)(2,1)} %convolution_convert_fusion.6.key_ref, bf16[512,1024]{1,0:T(8,128)(2,1)} %convolution_convert_fusion.5.value_ref, f32[8,2,512]{2,1,0:T(2,128)} %reshape.122.line_ref), custom_call_target="tpu_custom_call" | custom-call | tf_op jit(solution)/shard_map/mix/pallas_call | solution.py:937
  47.7 3.3 multiply_reduce_fusion.2
  51.0 1.5 fusion.9.refs_0_
  52.5 2.0 fusion.10
  55.9 129.0 %send_rows.1 = (bf16[2,2560,1024]{2,1,0:T(8,128)(2,1)}, f32[4,8,8,512]{3,2,1,0:T(8,128)}, bf16[4,512,1024]{2,1,0:T(8,128)(2,1)}) custom-call(bf16[512,1024]{1,0:T(8,128)(2,1)} %rows.1, f32[8,512]{1,0:T(8,128)} %pad.18.meta), custom_call_target="tpu_custom_call" | custom-call | tf_op jit(solution)/shard_map/send_rows/pallas_call | solution.py:513
  184.9 290.7 %run_experts.1 = (f32[512,1024]{1,0:T(8,128)}, f32[8,512]{1,0:T(8,128)}, bf16[2,2560,1024]{2,1,0:T(8,128)(2,1)}, bf16[2,2560,1024]{2,1,0:T(8,128)(2,1)}, bf16[2,...) custom-call(bf16[512,1024]{1,0:T(8,128)(2,1)} %fusion.9.refs_0_, ...), custom_call_target="tpu_custom_call" | custom-call | tf_op jit(solution)/shard_map/run_experts/pallas_call | solution.py:780
  477.3 2.9 fusion.12
  480.2 4.1 multiply_reduce_fusion
  485.6 2.7 convolution_convert_fusion
  488.2 2.3 convolution_convert_fusion.4.grad_ref
  490.5 28.7 %unmix.1 = (bf16[512,1024]{1,0:T(8,128)(2,1)}, bf16[512,1024]{1,0:T(8,128)(2,1)}, bf16[512,1024]{1,0:T(8,128)(2,1)}, f32[8,2,512]{2,1,0:T(2,128)}) custom-call(bf16[512,1024]{1,0:T(8,128)(2,1)} %convolution_convert_fusion.7.query_ref, bf16[512,1024]{1,0:T(8,128)(2,1)} %convolution_convert_fusion.6.key_ref, ...), custom_call_target="tpu_custom_call" | custom-call | tf_op jit(solution)/shard_map/unmix/pallas_call | solution.py:1012
  519.3 3.3 fusion.49
  522.6 2.7 convolution_convert_fusion.3
  525.3 2.6 fusion.50
  527.9 2.7 convolution_convert_fusion.2
  531.2 4.1 convolution_convert_fusion.1
  535.3 3.1 fusion.7
  539.1 197.6 %bring_back.1 = (f32[512,1024]{1,0:T(8,128)}, bf16[4,2,640,1024]{3,2,1,0:T(8,128)(2,1)}, bf16[4,512,1024]{2,1,0:T(8,128)(2,1)}) custom-call(bf16[2,2560,1024]{2,1,0:T(8,128)(2,1)} %get-tuple-element.52.given, f32[4,8,8,512]{3,2,1,0:T(8,128)} %get-tuple-element.40.refs_3_.targets), custom_call_target="tpu_custom_call" | custom-call | tf_op jit(solution)/shard_map/bring_back/pallas_call | solution.py:859
  736.7 15.1 %fusion.51 = f32[2,1024,704]{1,2,0:T(8,128)} fusion(bf16[2,2560,1024]{2,1,0:T(8,128)(2,1)} %get-tuple-element.59, bf16[2,2560,704]{2,1,0:T(8,128)(2,1)} %get-tuple-element.60), kind=kOutput, calls=%fused_computation.92 | convolution fusion | flops 7381975040 | bytes 23461888 | tf_op jit(solution)/shard_map/xrd,xrf->xdf/dot_general | solution.py:1123
  751.9 4.5 fusion.6
  756.3 15.2 %fusion.53 = f32[2,704,1024]{2,1,0:T(8,128)} fusion(bf16[2,2560,704]{2,1,0:T(8,128)(2,1)} %get-tuple-element.62, bf16[2,2560,1024]{2,1,0:T(8,128)(2,1)} %get-tuple-element.39.refs_2_), kind=kOutput, calls=%fused_computation.94 | convolution fusion | flops 7381975040 | bytes 23461888 | tf_op jit(solution)/shard_map/xrf,xrd->xfd/dot_general | solution.py:1122
  771.6 14.9 %fusion.52 = f32[2,1024,704]{1,2,0:T(8,128)} fusion(bf16[2,2560,1024]{2,1,0:T(8,128)(2,1)} %get-tuple-element.59, bf16[2,2560,704]{2,1,0:T(8,128)(2,1)} %get-tuple-element.61), kind=kOutput, calls=%fused_computation.93 | convolution fusion | flops 7381975040 | bytes 23461888 | tf_op jit(solution)/shard_map/xrd,xrf->xdf/dot_general | solution.py:1124
  786.5 17.3 %all-reduce.7.cloned.1.call-done = (bf16[32,1024]{1,0:T(8,128)(2,1)}, bf16[1024,1024]{1,0:T(8,128)(2,1)}, bf16[1024,1024]{1,0:T(8,128)(2,1)}, bf16[1024,1024]{1,0:T(8,128)(2,1)}, bf16[1024,1024]{1,0:T(8,128)(2,1)}) async-done(((bf16[32,1024]{1,0:T(8,128)(2,1)}, bf16[1024,1024]{1,0:T(8,128)(2,1)}, bf16[1024,1024]{1,0:T(8,128)(2,1)}, bf16[1024,1024]{1,0:T(8,128)(2,1)}, bf16[1024,1024]{1,0:T(8,128)(2,1)}), ...) | async-done | bytes 8454160 | tf_op jit(solution)/shard_map/psum | solution.py:1118
  803.8 1.4 fusion.48
  807.5 4.2 convert_element_type.179
  811.7 2.5 convert_element_type.180
  814.2 2.5 convert_element_type.181
  816.7 2.5 convert_element_type.182
  (94 shorter events, 11.2 us)
Async XLA Ops:
  7.2 45.3 %copy-start = (f32[1024,16]{0,1:T(8,128)S(1)}, f32[1024,16]{0,1:T(8,128)}, u32[]{:S(2)}) copy-start(f32[1024,16]{0,1:T(8,128)} %param.22) | copy-start | bytes 196612
  7.2 5.1 copy-start.5
  7.2 5.1 copy-start.19
  7.2 796.6 %all-reduce.7.cloned.1.call-start = ((), (), s32[]{:S(2)}) async-start(), calls=%async_computation | async-start | bytes 16908288 | tf_op jit(solution)/shard_map/psum | solution.py:1118
  12.3 4.0 copy-start.9
  16.3 2.3 copy-start.21
  47.7 3.3 copy-start.16
  51.0 3.6 copy-start.2
  51.0 3.6 copy-start.17
  475.6 4.6 copy-start.3
  480.2 4.1 copy-start.8
  484.3 1.2 copy-start.23
  485.6 2.7 copy-start.6
  485.6 2.7 copy-start.20
  519.3 3.3 copy-start.25
  522.6 2.7 copy-start.22
  522.6 2.7 copy-start.24
  527.9 2.7 copy-start.18
  531.1 4.2 copy-start.10
  531.1 4.1 copy-start.14
  531.2 4.1 copy-start.15
  736.7 15.2 %copy-start.4 = (f32[512,1024]{1,0:T(8,128)S(1)}, f32[512,1024]{1,0:T(8,128)}, u32[]{:S(2)}) copy-start(f32[512,1024]{1,0:T(8,128)} %copy-done.2) | copy-start | bytes 6291460
  736.7 15.2 %copy-start.7 = (f32[512,1024]{1,0:T(8,128)S(1)}, f32[512,1024]{1,0:T(8,128)}, u32[]{:S(2)}) copy-start(f32[512,1024]{1,0:T(8,128)} %copy-done.6) | copy-start | bytes 6291460
  807.5 4.2 copy-start.13
  811.7 2.5 copy-start.12
  814.2 2.5 copy-start.11
  816.7 2.5 copy-start.1
Sparse Core Ops, SparseCore 0:
  539.2 264.5 all-reduce.6

commit v3 on v2

v3 whole, which is shorter than its diff:
```python
import functools

import jax
import jax.numpy as jnp
from jax import lax
from jax.experimental import pallas as pl
from jax.experimental.pallas import tpu as pltpu
from jax.sharding import PartitionSpec as P

D = 1024
HEADS = 16
HEAD_DIM = 64
BUCKETS = 32
LEN = 512
MICRO = 2
MB_TOK = 256
VMEM = 62 * 1024 * 1024
MESH = pl.DeviceIdType.MESH


eps = 1e-06
precise = lax.Precision.HIGHEST
thresholds = (12, 16, 23, 32, 46, 64, 91)


def contract_last(matrix_a, matrix_b, mode=None):
    return lax.dot_general(
        matrix_a,
        matrix_b,
        (((1,), (1,)), ((), ())),
        precision=mode,
        preferred_element_type=jnp.float32,
    )


def contract_first(matrix_a, matrix_b, mode=None):
    return lax.dot_general(
        matrix_a,
        matrix_b,
        (((0,), (0,)), ((), ())),
        precision=mode,
        preferred_element_type=jnp.float32,
    )


def dot(matrix_a, matrix_b):
    return jnp.dot(matrix_a, matrix_b, preferred_element_type=jnp.float32)


def slot_targets(routes, experts_all, capacity, stride):
    pairs = 2 * MB_TOK
    flat = routes.reshape(-1, pairs)
    hits = (flat[:, :, None] == jnp.arange(experts_all, dtype=jnp.int32)).astype(jnp.bfloat16)
    lower = (
        jnp.arange(pairs, dtype=jnp.int32)[:, None] > jnp.arange(pairs, dtype=jnp.int32)[None, :]
    ).astype(jnp.bfloat16)
    earlier = jnp.einsum("pq,bqe->bpe", lower, hits, preferred_element_type=jnp.float32)
    rank = jnp.sum(earlier * hits.astype(jnp.float32), axis=-1).astype(jnp.int32)
    block = jnp.arange(flat.shape[0], dtype=jnp.int32)[:, None]
    target = flat * stride + block * capacity + rank
    return target.reshape(-1, 2).T


NEAR = 128


def offset_buckets():
    offset = jnp.arange(4 * NEAR, dtype=jnp.int32) - 2 * NEAR
    distance = jnp.abs(offset)
    far_bucket = 8 + sum(((distance >= threshold).astype(jnp.int32) for threshold in thresholds))
    bucket = jnp.where(distance < 8, distance, far_bucket) + 16 * (offset > 0).astype(jnp.int32)
    return (bucket[:, None] == jnp.arange(BUCKETS, dtype=jnp.int32)).astype(jnp.float32)


def bias_tiles(line):
    return pltpu.roll(
        jnp.broadcast_to(line, (NEAR, 4 * NEAR)), 0, 1, stride=1, stride_axis=0
    )


def mix_head(query, key, value, line, soft_ref, head):
    tiles = bias_tiles(line)
    blocks = LEN // NEAR
    outs = []
    for i in range(blocks):
        raw = contract_last(query[i * NEAR : (i + 1) * NEAR], key) * (HEAD_DIM**-0.5)
        parts = []
        for j in range(blocks):
            part = raw[:, j * NEAR : (j + 1) * NEAR]
            if abs(j - i) <= 1:
                parts.append(part + tiles[:, (j - i + 2) * NEAR : (j - i + 3) * NEAR])
            else:
                edge = 1 if j < i else 4 * NEAR - 1
                parts.append(part + line[:, edge : edge + 1])
        scores = jnp.concatenate(parts, axis=1)
        terms = jnp.exp(scores - jnp.max(scores, axis=1, keepdims=True))
        soft = (terms * (1.0 / jnp.sum(terms, axis=1, keepdims=True))).astype(jnp.bfloat16)
        soft_ref[head, i * NEAR : (i + 1) * NEAR, :] = soft
        outs.append(dot(soft, value))
    return jnp.concatenate(outs, axis=0).astype(jnp.bfloat16)


def unmix_head(query, key, value, grad_mixed, soft_ref, grads_v, head):
    blocks = LEN // NEAR
    near = [jnp.zeros((NEAR, NEAR), jnp.float32) for _ in range(3)]
    below = jnp.zeros((NEAR, NEAR), jnp.float32)
    above = jnp.zeros((NEAR, NEAR), jnp.float32)
    grad_query = []
    for i in range(blocks):
        at = slice(i * NEAR, (i + 1) * NEAR)
        soft = soft_ref[head, at, :].astype(jnp.float32)
        grad_soft = contract_last(grad_mixed[at], value)
        product = soft * grad_soft
        grad = product - soft * jnp.sum(product, axis=1, keepdims=True)
        low = grad.astype(jnp.bfloat16)
        grads_v[at, :] = low
        grad_query.append(dot(low, key))
        wide = low.astype(jnp.float32)
        for j in range(blocks):
            part = wide[:, j * NEAR : (j + 1) * NEAR]
            if abs(j - i) <= 1:
                near[j - i + 1] = near[j - i + 1] + part
            elif j < i:
                below = below + part
            else:
                above = above + part
    band = jnp.concatenate([jnp.zeros((NEAR, NEAR), jnp.float32)] + near, axis=1)
    eight = band[0:8]
    for i in range(8, NEAR, 8):
        eight = eight + pltpu.roll(band[i : i + 8], 4 * NEAR - i, 1)
    row = lax.broadcasted_iota(jnp.int32, (8, 4 * NEAR), 0)
    for bit in (1, 2, 4):
        eight = jnp.where(lax.rem(lax.div(row, bit), 2) == 1, pltpu.roll(eight, 4 * NEAR - bit, 1), eight)
    line = jnp.sum(eight, axis=0, keepdims=True)
    column = lax.broadcasted_iota(jnp.int32, (1, 4 * NEAR), 1)
    line = line + jnp.where(column == 1, jnp.sum(below), 0.0)
    line = line + jnp.where(column == 4 * NEAR - 1, jnp.sum(above), 0.0)
    scaling = HEAD_DIM**-0.5
    grad_query = (jnp.concatenate(grad_query, axis=0) * scaling).astype(jnp.bfloat16)
    grad_key = (contract_first(grads_v[...], query) * scaling).astype(jnp.bfloat16)
    grad_value = contract_first(soft_ref[head], grad_mixed).astype(jnp.bfloat16)
    return grad_query, grad_key, grad_value, line


def unmix_body(
    query_ref, key_ref, value_ref, grad_ref, soft_ref, dq_ref, dk_ref, dv_ref, line_ref, grads_v
):
    for head in range(2):
        at = slice(head * HEAD_DIM, (head + 1) * HEAD_DIM)
        dq_ref[:, at], dk_ref[:, at], dv_ref[:, at], line_ref[0, head : head + 1, :] = unmix_head(
            query_ref[:, at],
            key_ref[:, at],
            value_ref[:, at],
            grad_ref[:, at],
            soft_ref,
            grads_v,
            head,
        )


def unmix(query, key, value, grad_mixed, soft):
    pair = pl.BlockSpec((LEN, 2 * HEAD_DIM), lambda i: (0, i))
    rows = jax.ShapeDtypeStruct((LEN, D), jnp.bfloat16)
    out = pl.pallas_call(
        unmix_body,
        grid=(HEADS // 2,),
        in_specs=[pair] * 4 + [pl.BlockSpec((2, LEN, LEN), lambda i: (i, 0, 0))],
        out_specs=[pair] * 3 + [pl.BlockSpec((1, 2, 4 * NEAR), lambda i: (i, 0, 0))],
        out_shape=[rows] * 3 + [jax.ShapeDtypeStruct((HEADS // 2, 2, 4 * NEAR), jnp.float32)],
        scratch_shapes=[pltpu.VMEM((LEN, LEN), jnp.bfloat16)],
        compiler_params=pltpu.CompilerParams(vmem_limit_bytes=VMEM),
        name="unmix",
    )(query, key, value, grad_mixed, soft)
    return out[0], out[1], out[2], out[3].reshape(HEADS, 4 * NEAR)


class Plan:
    def __init__(self, n_e, n_h, experts_all, width):
        self.n_e, self.n_h, self.width = n_e, n_h, width
        self.capacity = 10 * MB_TOK // (4 * experts_all)
        self.stride = -(-MICRO * self.capacity // 16) * 16
        self.span = 2 * self.stride
        self.rows = n_e * self.stride
        self.total = n_h * self.rows

    def place(self):
        return lax.axis_index("expert"), lax.axis_index("hidden")

    def source(self, z, chunk):
        sign = 1 - 2 * lax.div(z, self.n_h // 2)
        return lax.rem(z + self.n_h + sign * chunk, self.n_h)


def across(here, mask):
    there, bit = here, 1
    while bit <= mask:
        if mask & bit:
            there = there + bit * (1 - 2 * lax.rem(lax.div(here, bit), 2))
        bit *= 2
    return there


def remote(src, dst, send_sem, recv_sem, device):
    return pltpu.make_async_remote_copy(
        src_ref=src,
        dst_ref=dst,
        send_sem=send_sem,
        recv_sem=recv_sem,
        device_id=device,
        device_id_type=MESH,
    )


def greet(plan):
    e, z = plan.place()
    barrier = pltpu.get_barrier_semaphore()
    for mask in range(1, plan.n_e):
        pl.semaphore_signal(barrier, inc=1, device_id=(across(e, mask), z), device_id_type=MESH)
    for shift in range(1, plan.n_h):
        pl.semaphore_signal(
            barrier, inc=1, device_id=(e, lax.rem(z + shift, plan.n_h)), device_id_type=MESH
        )
    pl.semaphore_wait(barrier, plan.n_e + plan.n_h - 2)


def slot_hits(plan, base, target):
    slots = lax.broadcasted_iota(jnp.int32, (plan.stride, LEN), 0).astype(jnp.float32) + base
    return jnp.where((slots == target[0:1, :]) | (slots == target[1:2, :]), 1.0, 0.0).astype(
        jnp.bfloat16
    )


def slot_base(plan, device, j):
    return (device * plan.span + j * plan.stride).astype(jnp.float32)


class Dispatch:
    def __init__(self, plan, rows, meta, land, out, meta_out, rows_v, meta_v, stage, sems):
        self.plan = plan
        self.rows, self.meta, self.land = rows, meta, land
        self.out, self.meta_out = out, meta_out
        self.rows_v, self.meta_v, self.stage = rows_v, meta_v, stage
        (
            self.z_send,
            self.z_recv,
            self.zm_send,
            self.zm_recv,
            self.a_send,
            self.a_recv,
            self.m_send,
            self.m_recv,
            self.local,
        ) = sems

    @staticmethod
    def sem_shapes(plan):
        dma = pltpu.SemaphoreType.DMA
        n_h, n_e = plan.n_h, plan.n_e
        return [
            dma((n_h, 2)),
            dma((n_h,)),
            dma((n_h, 2)),
            dma((n_h,)),
            dma((2, n_e)),
            dma((n_h, n_e)),
            dma((n_h, n_e)),
            dma((n_h, n_e)),
            dma((3,)),
        ]

    def hop(self, source, way, own):
        e, z = self.plan.place()
        sems = [
            (self.z_send.at[source, (way + 1) // 2], self.z_recv.at[source]),
            (self.zm_send.at[source, (way + 1) // 2], self.zm_recv.at[source]),
        ]
        return (
            remote(self.meta_v.at[source], self.meta_v.at[source], *sems[1], (e, z + way)),
            remote(
                self.rows if own else self.land.at[source],
                self.land.at[source],
                *sems[0],
                (e, z + way),
            ),
        )

    def on_the_way(self, distance, act):
        n_h = self.plan.n_h
        _, z = self.plan.place()

        @pl.when(z + distance < n_h)
        def _():
            act(z + distance, z > 0, -1)

        @pl.when(z >= distance)
        def _():
            act(z - distance, z < n_h - 1, 1)

    def begin(self):
        _, z = self.plan.place()
        copy = pltpu.make_async_copy(self.meta, self.meta_v.at[z], self.local.at[1])
        copy.start()
        copy.wait()

        @pl.when(z > 0)
        def _():
            for copy in self.hop(z, -1, True):
                copy.start()

        @pl.when(z < self.plan.n_h - 1)
        def _():
            for copy in self.hop(z, 1, True):
                copy.start()

    def pass_on(self, distance):
        def act(source, forwarded, way):
            for copy in self.hop(source, way, False):
                copy.wait_recv()

            @pl.when(forwarded)
            def _():
                for copy in self.hop(source, way, False):
                    copy.start()

        self.on_the_way(distance, act)

    def in_plane(self, chunk, mask):
        plan = self.plan
        e, z = plan.place()
        buffer = lax.rem(chunk, 2)
        at = pl.multiple_of((chunk * plan.n_e + mask) * plan.stride, 16)
        return remote(
            self.stage.at[buffer, :, pl.ds(mask * plan.stride, plan.stride), :],
            self.out.at[:, pl.ds(at, plan.stride), :],
            self.a_send.at[buffer, mask],
            self.a_recv.at[chunk, mask],
            (across(e, mask), z),
        )

    def meta_copy(self, chunk, mask):
        e, z = self.plan.place()
        return remote(
            self.meta_v.at[self.plan.source(z, chunk)],
            self.meta_out.at[chunk, mask],
            self.m_send.at[chunk, mask],
            self.m_recv.at[chunk, mask],
            (across(e, mask), z),
        )

    def chunk(self, chunk, target_of):
        plan = self.plan
        e, z = plan.place()
        buffer = lax.rem(chunk, 2)
        source = plan.source(z, chunk)

        @pl.when(chunk == 0)
        def _():
            copy = pltpu.make_async_copy(self.rows, self.rows_v.at[buffer], self.local.at[0])
            copy.start()
            copy.wait()

        @pl.when(chunk > 0)
        def _():
            self.pass_on(chunk)
            copy = pltpu.make_async_copy(
                self.land.at[source], self.rows_v.at[buffer], self.local.at[0]
            )
            copy.start()
            copy.wait()

        for mask in range(1, plan.n_e):
            self.meta_copy(chunk, mask).start()
        own_meta = pltpu.make_async_copy(
            self.meta_v.at[source], self.meta_out.at[chunk, 0], self.local.at[1]
        )
        own_meta.start()

        @pl.when(chunk >= 2)
        def _():
            for mask in range(1, plan.n_e):
                self.in_plane(chunk - 2, mask).wait_send()

        target = target_of(chunk)
        group = min(4, plan.n_e)
        for start in range(0, plan.n_e, group):
            for j in range(2):
                hot = jnp.concatenate(
                    [
                        slot_hits(plan, slot_base(plan, across(e, start + i), j), target)
                        for i in range(group)
                    ],
                    axis=0,
                )
                picked = dot(hot, self.rows_v[buffer]).astype(jnp.bfloat16)
                self.stage[
                    buffer, j, start * plan.stride : (start + group) * plan.stride, :
                ] = picked
            for mask in range(max(start, 1), start + group):
                self.in_plane(chunk, mask).start()
        at = pl.multiple_of(chunk * plan.rows, 16)
        own = pltpu.make_async_copy(
            self.stage.at[buffer, :, pl.ds(0, plan.stride), :],
            self.out.at[:, pl.ds(at, plan.stride), :],
            self.local.at[2],
        )
        own.start()
        own.wait()
        own_meta.wait()

    def arrived(self, chunk):
        for mask in range(1, self.plan.n_e):
            self.meta_copy(chunk, mask).wait_recv()
            self.in_plane(chunk, mask).wait_recv()

    def finish(self):
        plan = self.plan
        for chunk in range(max(0, plan.n_h - 2), plan.n_h):
            for mask in range(1, plan.n_e):
                self.in_plane(chunk, mask).wait_send()
        _, z = plan.place()

        @pl.when(z > 0)
        def _():
            for copy in self.hop(z, -1, True):
                copy.wait_send()

        @pl.when(z < plan.n_h - 1)
        def _():
            for copy in self.hop(z, 1, True):
                copy.wait_send()

        def act(source, forwarded, way):
            @pl.when(forwarded)
            def _():
                for copy in self.hop(source, way, False):
                    copy.wait_send()

        for distance in range(1, plan.n_h):
            self.on_the_way(distance, act)
        for chunk in range(plan.n_h):
            for mask in range(1, plan.n_e):
                self.meta_copy(chunk, mask).wait_send()


def same(index, other, count):
    return 1 - lax.div(lax.rem(index - other + count, count) + count - 1, count)


class Return:
    own_first = True

    def __init__(self, plan, back, land, out, stage, rows_v, sum_v, total, sems):
        self.plan = plan
        self.back, self.land, self.out = back, land, out
        self.stage, self.rows_v, self.sum_v, self.total = stage, rows_v, sum_v, total
        (self.b_send, self.b_recv, self.s_send, self.s_recv, self.local, self.own) = sems

    @staticmethod
    def sem_shapes(plan):
        dma = pltpu.SemaphoreType.DMA
        n_h, n_e = plan.n_h, plan.n_e
        return [
            dma((n_h, n_e)),
            dma((n_h, n_e)),
            dma((n_h,)),
            dma((2, n_h)),
            dma((2,)),
            dma((n_h,)),
        ]

    def goal(self, turn):
        n_h = self.plan.n_h
        _, z = self.plan.place()
        found = 0
        for here in range(n_h):
            others = [there for there in range(n_h) if there != here]
            others.sort(key=lambda d: n_h - 1 - d + here if d > here else d + n_h - 1 - here)
            order = [here] + others if self.own_first else others + [here]
            for when, there in enumerate(order):
                found = found + there * same(z, here, n_h) * same(turn, when, n_h)
        return found

    def chunk_of(self, goal):
        n_h = self.plan.n_h
        _, z = self.plan.place()
        sign = 1 - 2 * lax.div(z, n_h // 2)
        return lax.rem(sign * (goal - z) + n_h, n_h)

    def source(self, chunk, mask):
        raise NotImplementedError

    def in_plane(self, chunk, mask):
        plan = self.plan
        e, z = plan.place()
        return remote(
            self.source(chunk, mask),
            self.back.at[chunk, :, pl.ds(mask * plan.stride, plan.stride), :],
            self.b_send.at[chunk, mask],
            self.b_recv.at[chunk, mask],
            (across(e, mask), z),
        )

    def own_copy(self, chunk):
        plan = self.plan
        return pltpu.make_async_copy(
            self.source(chunk, 0),
            self.back.at[chunk, :, pl.ds(0, plan.stride), :],
            self.own.at[chunk],
        )

    def send(self, chunk):
        for mask in range(1, self.plan.n_e):
            self.in_plane(chunk, mask).start()
        self.own_copy(chunk).start()

    def hop(self, turn, goal, way):
        e, z = self.plan.place()
        side = (1 - way) // 2
        return remote(
            self.rows_v.at[lax.rem(turn, 2)],
            self.land.at[side, goal],
            self.s_send.at[turn],
            self.s_recv.at[side, goal],
            (e, z + way),
        )

    def each_way(self, goal, act):
        _, z = self.plan.place()

        @pl.when(goal > z)
        def _():
            act(1, z > 0)

        @pl.when(goal < z)
        def _():
            act(-1, z < self.plan.n_h - 1)

    def take(self, goal, way):
        side = (1 - way) // 2
        e, z = self.plan.place()
        remote(
            self.rows_v.at[0],
            self.land.at[side, goal],
            self.s_send.at[0],
            self.s_recv.at[side, goal],
            (e, z - way),
        ).wait_recv()
        copy = pltpu.make_async_copy(self.land.at[side, goal], self.sum_v, self.local.at[1])
        copy.start()
        copy.wait()
        return self.sum_v[...].astype(jnp.float32)

    def wait_hop(self, turn):
        goal = self.goal(turn)

        def act(way, _):
            self.hop(turn, goal, way).wait_send()

        self.each_way(goal, act)

    def fetched(self, chunk, buffer):
        return pltpu.make_async_copy(self.back.at[chunk], self.stage.at[buffer], self.local.at[0])

    def fetch(self, goal, chunk, buffer):
        for mask in range(1, self.plan.n_e):
            self.in_plane(chunk, mask).wait_recv()
        self.own_copy(chunk).wait()
        self.fetched(chunk, buffer).start()

    def combine(self, turn, target_of):
        plan = self.plan
        e, z = plan.place()
        goal = self.goal(turn)
        chunk = self.chunk_of(goal)
        target = target_of(chunk)
        buffer = lax.rem(turn, 2)
        self.fetch(goal, chunk, buffer)
        hot = [
            jnp.concatenate(
                [
                    slot_hits(plan, slot_base(plan, across(e, mask), j), target)
                    for mask in range(plan.n_e)
                ],
                axis=0,
            )
            for j in range(2)
        ]
        self.fetched(chunk, buffer).wait()

        @pl.when(turn >= 2)
        def _():
            self.wait_hop(turn - 2)

        part = contract_first(hot[0], self.stage[buffer, 0]) + contract_first(
            hot[1], self.stage[buffer, 1]
        )

        @pl.when(goal == z)
        def _():
            self.total[...] = part

        @pl.when(goal != z)
        def _():
            self.rows_v[buffer] = part.astype(jnp.bfloat16)

        def act(way, more):
            @pl.when(more)
            def _():
                so_far = self.take(goal, way)
                self.rows_v[buffer] = (self.rows_v[buffer].astype(jnp.float32) + so_far).astype(
                    jnp.bfloat16
                )

            self.hop(turn, goal, way).start()

        self.each_way(goal, act)

    def finish(self):
        plan = self.plan
        _, z = plan.place()
        for turn in range(plan.n_h - 2, plan.n_h):
            self.wait_hop(turn)

        @pl.when(z > 0)
        def _():
            self.total[...] += self.take(z, 1)

        @pl.when(z < plan.n_h - 1)
        def _():
            self.total[...] += self.take(z, -1)

        copy = pltpu.make_async_copy(self.total, self.out, self.local.at[0])
        copy.start()
        copy.wait()


class ReturnHeld(Return):
    own_first = False

    def __init__(self, plan, given, early, *rest):
        super().__init__(plan, *rest)
        self.given, self.early = given, early

    def fetch(self, goal, chunk, buffer):
        _, z = self.plan.place()

        @pl.when(goal != z)
        def _():
            Return.fetch(self, goal, chunk, buffer)

        @pl.when(goal == z)
        def _():
            pltpu.make_async_copy(self.early, self.stage.at[buffer], self.local.at[0]).start()

    def source(self, chunk, mask):
        plan = self.plan
        at = pl.multiple_of((chunk * plan.n_e + mask) * plan.stride, 16)
        return self.given.at[:, pl.ds(at, plan.stride), :]

    def sent(self):
        for chunk in range(1, self.plan.n_h):
            for mask in range(1, self.plan.n_e):
                self.in_plane(chunk, mask).wait_send()


class ReturnMade(Return):
    def __init__(self, plan, made, *rest):
        super().__init__(plan, *rest)
        self.made = made
        self.ring = made.shape[0]

    def source(self, chunk, mask):
        plan = self.plan
        return self.made.at[
            lax.rem(chunk, self.ring), :, pl.ds(mask * plan.stride, plan.stride), :
        ]

    def free(self, chunk):
        if self.plan.n_h > self.ring:

            @pl.when(chunk >= self.ring)
            def _():
                self.wait_sent(chunk - self.ring)
                self.own_copy(chunk - self.ring).wait()

    def wait_sent(self, chunk):
        for mask in range(1, self.plan.n_e):
            self.in_plane(chunk, mask).wait_send()

    def sent(self):
        for chunk in range(max(0, self.plan.n_h - self.ring), self.plan.n_h):
            self.wait_sent(chunk)


ANY = pl.BlockSpec(memory_space=pl.ANY)


def send_body(
    plan,
    n_d,
    rows,
    meta,
    query,
    key,
    value,
    lines,
    out,
    meta_out,
    land,
    soft_out,
    mixed_out,
    rows_v,
    meta_v,
    stage,
    query_v,
    key_v,
    value_v,
    soft_v,
    mixed_v,
    in_sem,
    soft_sem,
    mixed_sem,
    *sems,
):
    loads = [
        pltpu.make_async_copy(given, held, in_sem.at[i])
        for i, (given, held) in enumerate(((query, query_v), (key, key_v), (value, value_v)))
    ]
    for load in loads:
        load.start()
    greet(plan)
    work = Dispatch(plan, rows, meta, land, out, meta_out, rows_v, meta_v, stage, sems)
    work.begin()
    _, z = plan.place()
    for load in loads:
        load.wait()

    def soft_copy(pair):
        buffer = lax.rem(pair, 2)
        return pltpu.make_async_copy(
            soft_v.at[buffer], soft_out.at[pl.ds(2 * pair, 2)], soft_sem.at[buffer]
        )

    def mix_pair(pair):
        lanes = pl.ds(pl.multiple_of(pair * 2 * HEAD_DIM, 2 * HEAD_DIM), 2 * HEAD_DIM)
        both = [held[:, lanes] for held in (query_v, key_v, value_v)]

        @pl.when(pair >= 2)
        def _():
            soft_copy(pair - 2).wait()

        heads = []
        for head in range(2):
            at = slice(head * HEAD_DIM, (head + 1) * HEAD_DIM)
            heads.append(
                mix_head(
                    *[item[:, at] for item in both],
                    lines[pair, head : head + 1, :],
                    soft_v.at[lax.rem(pair, 2)],
                    head,
                )
            )
        mixed_v[:, lanes] = jnp.concatenate(heads, axis=1)
        soft_copy(pair).start()

    pairs = HEADS // 2
    each = -(-pairs // plan.n_h)

    @pl.loop(0, plan.n_h)
    def _(chunk):
        work.chunk(chunk, lambda at: meta_v[plan.source(z, at)])
        pl.loop(0, each)(lambda i: mix_pair(chunk * each + i))

    mixed_copy = pltpu.make_async_copy(mixed_v, mixed_out, mixed_sem.at[0])
    mixed_copy.start()
    soft_copy(pairs - 2).wait()
    soft_copy(pairs - 1).wait()
    mixed_copy.wait()
    for chunk in range(plan.n_h):
        work.arrived(chunk)
    work.finish()


def send_rows(plan, rows, meta, query, key, value, lines):
    n_h, n_e = plan.n_h, plan.n_e
    bf16, f32 = jnp.bfloat16, jnp.float32
    shape = jax.ShapeDtypeStruct
    sems = Dispatch.sem_shapes(plan)
    out = pl.pallas_call(
        functools.partial(send_body, plan, len(sems)),
        in_specs=[ANY] * 5 + [pl.BlockSpec(memory_space=pltpu.VMEM)],
        out_specs=[ANY] * 5,
        out_shape=[
            shape((2, plan.total, D), bf16),
            shape((n_h, n_e, 8, LEN), f32),
            shape((n_h, LEN, D), bf16),
            shape((HEADS, LEN, LEN), bf16),
            shape((LEN, D), bf16),
        ],
        scratch_shapes=[
            pltpu.VMEM((2, LEN, D), bf16),
            pltpu.VMEM((n_h, 8, LEN), f32),
            pltpu.VMEM((2, 2, plan.rows, D), bf16),
            pltpu.VMEM((LEN, D), bf16),
            pltpu.VMEM((LEN, D), bf16),
            pltpu.VMEM((LEN, D), bf16),
            pltpu.VMEM((2, 2, LEN, LEN), bf16),
            pltpu.VMEM((LEN, D), bf16),
            pltpu.SemaphoreType.DMA((3,)),
            pltpu.SemaphoreType.DMA((2,)),
            pltpu.SemaphoreType.DMA((1,)),
        ]
        + sems,
        compiler_params=pltpu.CompilerParams(
            collective_id=1, has_side_effects=True, vmem_limit_bytes=VMEM
        ),
        name="send_rows",
    )(rows, meta, query, key, value, lines.reshape(HEADS // 2, 2, 4 * NEAR))
    return out[0], out[1], out[3], out[4]


def expert_body(plan, halves, n_d, *refs):
    (
        sent,
        gates,
        grads,
        targets,
        w_gate,
        w_up,
        w_down,
        total_out,
        gg_out,
        rows_out,
        y_out,
        dgate_out,
        dup_out,
        act_out,
        meta_out,
        land,
        back,
        land_back,
        early,
        rows_v,
        meta_v,
        stage,
        wg_v,
        wu_v,
        wd_v,
        target_v,
        gate_v,
        x_v,
        g_v,
        dx_v,
        y_v,
        dgate_v,
        dup_v,
        act_v,
        gg_v,
        gg_back,
        gg_part,
        gg_land,
        sum_v,
        total,
        w_sem,
        t_sem,
        x_sem,
        o_sem,
        gg_send,
        gg_recv,
        ggs_send,
        ggs_recv,
        e_send,
        e_recv,
        *sems,
    ) = refs
    n_e, n_h = plan.n_e, plan.n_h
    e, z = plan.place()
    loads = [
        pltpu.make_async_copy(source, held, w_sem.at[i])
        for i, (source, held) in enumerate(((w_gate, wg_v), (w_up, wu_v), (w_down, wd_v)))
    ]
    for load in loads:
        load.start()
    targets_in = pltpu.make_async_copy(targets, target_v, t_sem.at[0])
    targets_in.start()
    greet(plan)
    work = Dispatch(
        plan, sent, gates, land, rows_out, meta_out, rows_v, meta_v, stage, sems[:n_d]
    )
    give = ReturnMade(
        plan, dx_v, back, land_back, total_out, stage, rows_v, sum_v, total, sems[n_d:]
    )
    work.begin()
    targets_in.wait()
    ahead = min(3, n_h)
    pl.loop(0, ahead)(lambda chunk: work.chunk(chunk, lambda at: target_v[at, 0]))
    for load in loads:
        load.wait()

    def gg_copy(chunk, mask):
        return remote(
            gg_v.at[chunk, mask],
            gg_back.at[chunk, mask],
            gg_send.at[chunk, mask],
            gg_recv.at[chunk, mask],
            (across(e, mask), z),
        )

    def gg_along(chunk):
        return remote(
            gg_part.at[chunk],
            gg_land.at[z],
            ggs_send.at[chunk],
            ggs_recv.at[z],
            (e, plan.source(z, chunk)),
        )

    def gg_from(distance):
        other = lax.rem(z + distance, n_h)
        return other, remote(
            gg_part.at[0], gg_land.at[other], ggs_send.at[0], ggs_recv.at[other], (e, other)
        )

    def outs(chunk, j):
        at = pl.multiple_of(chunk * plan.rows, 16)
        return [
            pltpu.make_async_copy(held.at[j], out.at[j, pl.ds(at, plan.rows), :], o_sem.at[i, j])
            for i, (held, out) in enumerate(
                ((y_v, y_out), (dgate_v, dgate_out), (dup_v, dup_out), (act_v, act_out))
            )
        ]

    all_held = n_h <= dx_v.shape[0]
    masks = n_e // halves
    piece = masks * plan.stride

    def step(chunk, index):
        j, half = lax.div(index, halves), lax.rem(index, halves)
        at = pl.ds(pl.multiple_of(half * piece, 16), piece)
        rows, grads_in = x_v[j, at, :], g_v[j, at, :]
        gate_pre = contract_last(rows, wg_v[j])
        up_pre = contract_last(rows, wu_v[j])
        raw = contract_last(grads_in, wd_v[j])
        slots = lax.broadcasted_iota(jnp.int32, (plan.stride, LEN), 0).astype(
            jnp.float32
        ) + slot_base(plan, e, j)
        columns = []
        for i in range(masks):
            mask = half * masks + i
            aim, weight = target_v[chunk, mask], gate_v[mask]
            hit = jnp.where(slots == aim[0:1, :], weight[0:1, :], 0.0)
            hit = hit + jnp.where(slots == aim[1:2, :], weight[1:2, :], 0.0)
            columns.append(jnp.sum(hit, axis=1, keepdims=True))
        gate = jnp.concatenate(columns, axis=0)
        square = gate_pre * gate_pre
        tanh = jnp.tanh(0.7978845608028654 * gate_pre * (1.0 + 0.044715 * square))
        side = 0.5 * (1.0 + tanh)
        gelu = gate_pre * side
        slope = side + 0.5 * gate_pre * (1.0 - tanh * tanh) * (
            0.7978845608028654 * (1.0 + 0.134145 * square)
        )
        act = gelu * up_pre
        act_low = act.astype(jnp.bfloat16)
        dots = jnp.sum(act_low.astype(jnp.float32) * raw, axis=1, keepdims=True)
        for i in range(masks):
            mask = half * masks + i
            aim, part = target_v[chunk, mask], dots[i * plan.stride : (i + 1) * plan.stride]
            for k in range(2):
                line = jnp.sum(
                    jnp.where(slots == aim[k : k + 1, :], part, 0.0), axis=0, keepdims=True
                )
                gg_v[chunk, mask, k : k + 1, :] += line
        grad_act = gate * raw
        grad_gate = (grad_act * up_pre * slope).astype(jnp.bfloat16)
        grad_up = (grad_act * gelu).astype(jnp.bfloat16)
        dgate_v[j, at, :] = grad_gate
        dup_v[j, at, :] = grad_up
        act_v[j, at, :] = (act * gate).astype(jnp.bfloat16)
        dx_v[lax.rem(chunk, dx_v.shape[0]), j, at, :] = (
            dot(grad_gate, wg_v[j]) + dot(grad_up, wu_v[j])
        ).astype(jnp.bfloat16)
        y_v[j, at, :] = (dot(act_low, wd_v[j]) * gate).astype(jnp.bfloat16)

    gg_v[...] = jnp.zeros_like(gg_v)

    @pl.loop(0, n_h)
    def _(chunk):
        work.arrived(chunk)
        at = pl.multiple_of(chunk * plan.rows, 16)
        gate_in = pltpu.make_async_copy(meta_out.at[chunk], gate_v, t_sem.at[0])
        gate_in.start()
        ins = [
            pltpu.make_async_copy(source.at[:, pl.ds(at, plan.rows), :], held, x_sem.at[i])
            for i, (source, held) in enumerate(((rows_out, x_v), (grads, g_v)))
        ]
        for copy in ins:
            copy.start()
        give.free(chunk)

        @pl.when(chunk > 0)
        def _():
            for j in range(2):
                for copy in outs(chunk - 1, j):
                    copy.wait()

        gate_in.wait()
        for copy in ins:
            copy.wait()
        pl.loop(0, 2 * halves)(lambda index: step(chunk, index))
        for j in range(2):
            for copy in outs(chunk, j):
                copy.start()

        @pl.when(chunk + ahead < n_h)
        def _():
            work.chunk(chunk + ahead, lambda at: target_v[at, 0])

        for mask in range(1, n_e):
            gg_copy(chunk, mask).start()

        @pl.when((chunk < 1) | (not all_held))
        def _():
            give.send(chunk)

    def early_copy(mask):
        at = pl.ds(mask * plan.stride, plan.stride)
        if mask == 0:
            return pltpu.make_async_copy(y_out.at[:, at, :], early.at[:, at, :], e_send.at[0])
        return remote(
            y_out.at[:, at, :],
            early.at[:, at, :],
            e_send.at[mask],
            e_recv.at[mask],
            (across(e, mask), z),
        )

    if all_held:
        pl.loop(1, n_h)(lambda turn: give.send(give.chunk_of(give.goal(turn))))
    for mask in range(n_e):
        early_copy(mask).start()
    work.finish()
    for j in range(2):
        for copy in outs(n_h - 1, j):
            copy.wait()

    @pl.loop(0, n_h)
    def _(turn):
        chunk = give.chunk_of(give.goal(turn))
        part = gg_v[chunk, 0]
        for mask in range(1, n_e):
            gg_copy(chunk, mask).wait_recv()
            part = part + gg_back[chunk, mask]
        gg_part[chunk] = part

        @pl.when(chunk > 0)
        def _():
            gg_along(chunk).start()

        give.combine(turn, lambda at: target_v[at, 0])

    give.sent()
    early_copy(0).wait()
    for mask in range(1, n_e):
        early_copy(mask).wait()
    for chunk in range(n_h):
        for mask in range(1, n_e):
            gg_copy(chunk, mask).wait_send()
    sum_gg = gg_part[0]
    for distance in range(1, n_h):
        other, arrival = gg_from(distance)
        arrival.wait_recv()
        sum_gg = sum_gg + gg_land[other]
    gg_out[...] = sum_gg
    for chunk in range(1, n_h):
        gg_along(chunk).wait_send()
    give.finish()


def run_experts(plan, sent, gates, grads, targets, w_gate, w_up, w_down):
    n_h, n_e, width = plan.n_h, plan.n_e, plan.width
    bf16, f32 = jnp.bfloat16, jnp.float32
    shape = jax.ShapeDtypeStruct
    dma = pltpu.SemaphoreType.DMA
    ring = min(4, n_h)
    d_sems, r_sems = Dispatch.sem_shapes(plan), Return.sem_shapes(plan)
    halves = 2 if plan.rows <= 640 else 4
    return pl.pallas_call(
        functools.partial(expert_body, plan, halves, len(d_sems)),
        in_specs=[ANY] * 7,
        out_specs=[ANY, pl.BlockSpec(memory_space=pltpu.VMEM)] + [ANY] * 10,
        out_shape=[
            shape((LEN, D), f32),
            shape((8, LEN), f32),
            shape((2, plan.total, D), bf16),
            shape((2, plan.total, D), bf16),
            shape((2, plan.total, width), bf16),
            shape((2, plan.total, width), bf16),
            shape((2, plan.total, width), bf16),
            shape((n_h, n_e, 8, LEN), f32),
            shape((n_h, LEN, D), bf16),
            shape((n_h, 2, plan.rows, D), bf16),
            shape((2, n_h, LEN, D), bf16),
            shape((2, plan.rows, D), bf16),
        ],
        scratch_shapes=[
            pltpu.VMEM((2, LEN, D), bf16),
            pltpu.VMEM((n_h, 8, LEN), f32),
            pltpu.VMEM((2, 2, plan.rows, D), bf16),
            pltpu.VMEM((2, width, D), bf16),
            pltpu.VMEM((2, width, D), bf16),
            pltpu.VMEM((2, width, D), bf16),
            pltpu.VMEM((n_h, n_e, 8, LEN), f32),
            pltpu.VMEM((n_e, 8, LEN), f32),
            pltpu.VMEM((2, plan.rows, D), bf16),
            pltpu.VMEM((2, plan.rows, D), bf16),
            pltpu.VMEM((ring, 2, plan.rows, D), bf16),
            pltpu.VMEM((2, plan.rows, D), bf16),
            pltpu.VMEM((2, plan.rows, width), bf16),
            pltpu.VMEM((2, plan.rows, width), bf16),
            pltpu.VMEM((2, plan.rows, width), bf16),
            pltpu.VMEM((n_h, n_e, 8, LEN), f32),
            pltpu.VMEM((n_h, n_e, 8, LEN), f32),
            pltpu.VMEM((n_h, 8, LEN), f32),
            pltpu.VMEM((n_h, 8, LEN), f32),
            pltpu.VMEM((LEN, D), bf16),
            pltpu.VMEM((LEN, D), f32),
            dma((3,)),
            dma((1,)),
            dma((2,)),
            dma((4, 2)),
            dma((n_h, n_e)),
            dma((n_h, n_e)),
            dma((n_h,)),
            dma((n_h,)),
            dma((n_e,)),
            dma((n_e,)),
        ]
        + d_sems
        + r_sems,
        compiler_params=pltpu.CompilerParams(
            collective_id=2, has_side_effects=True, vmem_limit_bytes=VMEM
        ),
        name="run_experts",
    )(sent, gates, grads, targets, jnp.swapaxes(w_gate, 1, 2), jnp.swapaxes(w_up, 1, 2), w_down)


def back_body(
    plan, given, early, targets, out, back, land, rows_v, stage, target_v, sum_v, total, t_sem, *sems
):
    targets_in = pltpu.make_async_copy(targets, target_v, t_sem.at[0])
    targets_in.start()
    greet(plan)
    give = ReturnHeld(plan, given, early, back, land, out, stage, rows_v, sum_v, total, sems)
    pl.loop(0, plan.n_h - 1)(lambda turn: give.send(give.chunk_of(give.goal(turn))))
    targets_in.wait()
    pl.loop(0, plan.n_h)(lambda turn: give.combine(turn, lambda at: target_v[at, 0]))
    give.sent()
    give.finish()


def bring_back(plan, given, early, targets):
    n_h, n_e = plan.n_h, plan.n_e
    bf16, f32 = jnp.bfloat16, jnp.float32
    shape = jax.ShapeDtypeStruct
    return pl.pallas_call(
        functools.partial(back_body, plan),
        in_specs=[ANY] * 3,
        out_specs=[ANY] * 3,
        out_shape=[
            shape((LEN, D), f32),
            shape((n_h, 2, plan.rows, D), bf16),
            shape((2, n_h, LEN, D), bf16),
        ],
        scratch_shapes=[
            pltpu.VMEM((2, LEN, D), bf16),
            pltpu.VMEM((2, 2, plan.rows, D), bf16),
            pltpu.VMEM((n_h, n_e, 8, LEN), f32),
            pltpu.VMEM((LEN, D), bf16),
            pltpu.VMEM((LEN, D), f32),
            pltpu.SemaphoreType.DMA((1,)),
        ]
        + Return.sem_shapes(plan),
        compiler_params=pltpu.CompilerParams(
            collective_id=3, has_side_effects=True, vmem_limit_bytes=VMEM
        ),
        name="bring_back",
    )(given, early, targets)[0]


def per_device(
    n_e,
    n_h,
    tokens,
    gain_one,
    w_query,
    w_key,
    w_value,
    w_out,
    bias_table,
    gain_two,
    w_router,
    w_gate,
    w_up,
    w_down,
    routes,
    cotangent,
):
    experts_all = w_router.shape[1]
    plan = Plan(n_e, n_h, experts_all, w_gate.shape[2])
    both = ("expert", "hidden")

    def small(array):
        return jnp.pad(array.astype(jnp.float32), ((0, 8 - array.shape[0]), (0, 0)))

    targets = small(slot_targets(routes, experts_all, plan.capacity, plan.stride))
    hot_bucket = offset_buckets()
    inputs = tokens.astype(jnp.float32)
    inv_one = lax.rsqrt(jnp.mean(inputs * inputs, axis=-1, keepdims=True) + eps)
    normed_one = (inputs * inv_one * gain_one).astype(jnp.bfloat16)
    query_rows = dot(normed_one, w_query).astype(jnp.bfloat16)
    key_rows = dot(normed_one, w_key).astype(jnp.bfloat16)
    value_rows = dot(normed_one, w_value).astype(jnp.bfloat16)
    lines = jnp.dot(hot_bucket, bias_table, precision=precise).T
    grads_in, targets_all, soft, mixed_rows = send_rows(
        plan, cotangent, targets, query_rows, key_rows, value_rows, lines
    )
    hidden = inputs + dot(mixed_rows, w_out)
    inv_two = lax.rsqrt(jnp.mean(hidden * hidden, axis=-1, keepdims=True) + eps)
    normed_two = hidden * inv_two * gain_two
    sent = normed_two.astype(jnp.bfloat16)
    logits = jnp.dot(normed_two, w_router, precision=precise)
    route_hot = (routes[:, :, None] == jnp.arange(experts_all, dtype=jnp.int32)).astype(jnp.float32)
    chosen = jnp.sum(route_hot * logits[:, None, :], axis=-1)
    gate_values = jax.nn.softmax(chosen, axis=-1)
    made = run_experts(
        plan, sent, small(gate_values.T), grads_in, targets_all, w_gate, w_up, w_down
    )
    grad_sent, grad_gates, rows_in, y_rows, gate_rows, up_rows, act_rows = made[:7]
    y_early = made[-1]
    grad_gates = grad_gates[:2].T
    grad_out = cotangent.astype(jnp.float32)
    grad_chosen = gate_values * (
        grad_gates - jnp.sum(gate_values * grad_gates, axis=-1, keepdims=True)
    )
    grad_logits = jnp.sum(route_hot * grad_chosen[:, :, None], axis=1)
    router_grad = contract_first(grad_logits, normed_two, precise)
    grad_normed_two = contract_last(grad_logits, w_router, precise) + grad_sent
    gain_two_grad = jnp.sum(grad_normed_two * hidden * inv_two, axis=0)
    scaled_two = grad_normed_two * gain_two
    grad_hidden = (
        grad_out
        + inv_two * scaled_two
        - hidden * inv_two**3 * jnp.mean(scaled_two * hidden, axis=-1, keepdims=True)
    )
    grad_branch = grad_hidden.astype(jnp.bfloat16)
    w_out_grad = contract_first(mixed_rows, grad_branch)
    grad_mixed = contract_last(grad_branch, w_out).astype(jnp.bfloat16)
    grad_query, grad_key, grad_value, grad_lines = unmix(
        query_rows, key_rows, value_rows, grad_mixed, soft
    )
    bias_table_grad = jnp.dot(grad_lines, hot_bucket, precision=precise).T
    query_grad = contract_first(normed_one, grad_query)
    key_grad = contract_first(normed_one, grad_key)
    value_grad = contract_first(normed_one, grad_value)
    grad_normed_one = (
        contract_last(grad_query, w_query)
        + contract_last(grad_key, w_key)
        + contract_last(grad_value, w_value)
    )
    gain_one_grad = jnp.sum(grad_normed_one * inputs * inv_one, axis=0)
    scaled_one = grad_normed_one * gain_one
    tokens_grad = (
        grad_hidden
        + inv_one * scaled_one
        - inputs * inv_one**3 * jnp.mean(scaled_one * inputs, axis=-1, keepdims=True)
    )
    last = jnp.pad(bias_table_grad.reshape(1, BUCKETS * HEADS), ((0, 0), (0, D - BUCKETS * HEADS)))
    few = jnp.concatenate([router_grad, gain_one_grad[None], gain_two_grad[None], last], axis=0)
    few = jnp.pad(few, ((0, -few.shape[0] % 16), (0, 0)))
    low = [
        item.astype(jnp.bfloat16) for item in (query_grad, key_grad, value_grad, w_out_grad, few)
    ]
    low, gate_rows, up_rows, act_rows, y_rows = lax.optimization_barrier(
        (low, gate_rows, up_rows, act_rows, y_rows)
    )
    summed = [item.astype(jnp.float32) for item in lax.psum(low, both)]
    few = summed[4]
    branch = bring_back(plan, y_rows, y_early, targets_all)
    block_out = (hidden + branch).astype(jnp.bfloat16)
    down_grad = jnp.einsum("xrf,xrd->xfd", act_rows, grads_in, preferred_element_type=jnp.float32)
    gate_grad = jnp.einsum("xrd,xrf->xdf", rows_in, gate_rows, preferred_element_type=jnp.float32)
    up_grad = jnp.einsum("xrd,xrf->xdf", rows_in, up_rows, preferred_element_type=jnp.float32)
    return (
        block_out,
        tokens_grad,
        few[experts_all],
        *summed[:4],
        few[experts_all + 2, : BUCKETS * HEADS].reshape(BUCKETS, HEADS),
        few[experts_all + 1],
        few[:experts_all].T,
        gate_grad,
        up_grad,
        down_grad,
    )


def solution(mesh):
    in_specs = (
        P(("expert", "hidden"), None),
        P(),
        P(),
        P(),
        P(),
        P(),
        P(),
        P(),
        P(),
        P("expert", None, "hidden"),
        P("expert", None, "hidden"),
        P("expert", "hidden", None),
        P(("expert", "hidden"), None),
        P(("expert", "hidden"), None),
    )
    out_specs = (
        P(("expert", "hidden"), None),
        P(("expert", "hidden"), None),
        P(),
        P(),
        P(),
        P(),
        P(),
        P(),
        P(),
        P(),
        P("expert", None, "hidden"),
        P("expert", None, "hidden"),
        P("expert", "hidden", None),
    )
    return jax.shard_map(
        functools.partial(per_device, mesh.shape["expert"], mesh.shape["hidden"]),
        mesh=mesh, in_specs=in_specs, out_specs=out_specs, check_vma=False
    )
```

time: 832 us -> 736 us (0.88)
  Pallas kernels: 673 us -> 583 us
    pallas_call x3 -> x2, Pallas kernels: 353 us -> 276 us  [the longest x1 146 us: bring_back(): pl.pallas_call(functools.partial(back_body, plan), in_specs=[ANY] * 3, ou...]
    pallas_call x1, Pallas kernels: 291 us -> 278 us  [run_experts(): pl.pallas_call(functools.partial(expert_body, plan, halves, len(d_sems)),...]
  transfers between devices with their start and end apart: 1 -> 1, of which waited for: 1 -> 1; matrix products, arithmetic and copies ran while one was open for 6% -> 7% of each run, Pallas kernels for 24% -> 20%
where the time goes in v3:
time: 736 us; the launch traced here: 730 us
  Pallas kernels  583 us (79%)
  matrix products  90 us (12%)
  other arithmetic  24.3 us (3%)
  between operations  14.5 us (2%)
  waiting for transfers between devices  11.2 us (2%)
  local copies, waits for them, and re-layouts  7.69 us (1%)
    pallas_call x1, Pallas kernels, run_experts(): pl.pallas_call(functools.partial(expert_body, plan, halves, len(d_sems)),...  278 us
    pallas_call x1, Pallas kernels, bring_back(): pl.pallas_call(functools.partial(back_body, plan), in_specs=[ANY] * 3, ou...  146 us
    pallas_call x1, Pallas kernels, send_rows(): pl.pallas_call(functools.partial(send_body, plan, len(sems)), in_specs=[A...  130 us
    pallas_call x1, Pallas kernels, unmix(): pl.pallas_call(unmix_body, grid=(HEADS // 2,), in_specs=[pair] * 4 + [pl....  28.8 us
    dot_general x5, matrix products, contract_last(): lax.dot_general(matrix_a, matrix_b, (((1,), (1,)), ((), ())), precision=m...  15.4 us
    dot_general x5, matrix products, contract_first(): lax.dot_general(matrix_a, matrix_b, (((0,), (0,)), ((), ())), precision=m...  15 us
    dot_general x1, matrix products, per_device(): jnp.einsum('xrf,xrd->xfd', act_rows, grads_in, preferred_element_type=jnp...  14.9 us
    dot_general x1, matrix products, per_device(): jnp.einsum('xrd,xrf->xdf', rows_in, gate_rows, preferred_element_type=jnp...  14.8 us
  transfers between devices with their start and end apart: 1, of which 1 were waited for; matrix products, arithmetic and copies ran while one was open for 7% of the time, Pallas kernels for 20%

profile of v3, /device:TPU:1, one launch (start us, length us, event | category | flops | bytes accessed | tf_op | source)
XLA Modules:
  0.0 730.3 jit_solution(9301279402937365056)
XLA Ops:
  7.4 1.6 fusion
  9.0 1.0 convolution_bitcast_fusion.1
  12.3 4.0 convolution_convert_fusion.6.key.key_ref
  16.3 2.3 convolution_convert_fusion.5.value.value_ref
  18.6 2.3 convolution_convert_fusion.7.query.query_ref
  21.5 130.2 %send_rows.1 = (bf16[2,2560,1024]{2,1,0:T(8,128)(2,1)}, f32[4,8,8,512]{3,2,1,0:T(8,128)}, bf16[4,512,1024]{2,1,0:T(8,128)(2,1)}, bf16[16,512,512]{2,1,0:T(8,128)(2,1)}, bf16[512,1024]{1,0:T(8,128)(2,1)}) custom-call(bf16[512,1024]{1,0:T(8,128)(2,1)} %rows.1, f32[8,512]{1,0:T(8,128)} %pad.17.meta, ...), custom_call_target="tpu_custom_call" | custom-call | tf_op jit(solution)/shard_map/send_rows/pallas_call | solution.py:789
  151.8 3.3 multiply_reduce_fusion.2
  155.1 1.4 fusion.9.refs_0_
  156.5 2.0 fusion.10
  159.3 277.7 %run_experts.1 = (f32[512,1024]{1,0:T(8,128)}, f32[8,512]{1,0:T(8,128)}, bf16[2,2560,1024]{2,1,0:T(8,128)(2,1)}, bf16[2,2560,1024]{2,1,0:T(8,128)(2,1)}, bf16[2,...) custom-call(bf16[512,1024]{1,0:T(8,128)(2,1)} %fusion.9.refs_0_, ...), custom_call_target="tpu_custom_call" | custom-call | tf_op jit(solution)/shard_map/run_experts/pallas_call | solution.py:1087
  438.7 2.9 fusion.12
  441.6 4.1 multiply_reduce_fusion
  447.0 2.6 convolution_convert_fusion
  449.6 2.3 convolution_convert_fusion.4.grad_ref
  451.9 28.8 %unmix.1 = (bf16[512,1024]{1,0:T(8,128)(2,1)}, bf16[512,1024]{1,0:T(8,128)(2,1)}, bf16[512,1024]{1,0:T(8,128)(2,1)}, f32[8,2,512]{2,1,0:T(2,128)}) custom-call(bf16[512,1024]{1,0:T(8,128)(2,1)} %convolution_convert_fusion.7.query.query_ref, bf16[512,1024]{1,0:T(8,128)(2,1)} %convolution_convert_fusion.6.key.key_ref, ...), custom_call_target="tpu_custom_call" | custom-call | tf_op jit(solution)/shard_map/unmix/pallas_call | solution.py:164
  480.7 3.3 fusion.49
  484.0 2.7 convolution_convert_fusion.3
  486.8 2.6 fusion.50
  489.4 2.7 convolution_convert_fusion.2
  492.6 4.1 convolution_convert_fusion.1
  496.7 3.1 fusion.7
  500.5 14.8 %fusion.51 = f32[2,1024,704]{1,2,0:T(8,128)} fusion(bf16[2,2560,1024]{2,1,0:T(8,128)(2,1)} %get-tuple-element.61, bf16[2,2560,704]{2,1,0:T(8,128)(2,1)} %get-tuple-element.62), kind=kOutput, calls=%fused_computation.92 | convolution fusion | flops 7381975040 | bytes 23461888 | tf_op jit(solution)/shard_map/xrd,xrf->xdf/dot_general | solution.py:1291
  515.3 145.7 %bring_back.1 = (f32[512,1024]{1,0:T(8,128)}, bf16[4,2,640,1024]{3,2,1,0:T(8,128)(2,1)}, bf16[2,4,512,1024]{3,2,1,0:T(8,128)(2,1)}) custom-call(bf16[2,2560,1024]{2,1,0:T(8,128)(2,1)} %get-tuple-element.53.given, bf16[2,640,1024]{2,1,0:T(8,128)(2,1)} %get-tuple-element.54.early, f32[4,8,8,512]{3,2,1,0:T(8,128)} %get-tuple-element.41.refs_3_.targets), custom_call_target="tpu_custom_call" | custom-call | tf_op jit(solution)/shard_map/bring_back/pallas_call | solution.py:1165
  661.0 6.4 fusion.6
  667.4 14.9 %fusion.53 = f32[2,704,1024]{2,1,0:T(8,128)} fusion(bf16[2,2560,704]{2,1,0:T(8,128)(2,1)} %get-tuple-element.64, bf16[2,2560,1024]{2,1,0:T(8,128)(2,1)} %get-tuple-element.40.refs_2_), kind=kOutput, calls=%fused_computation.94 | convolution fusion | flops 7381975040 | bytes 23461888 | tf_op jit(solution)/shard_map/xrf,xrd->xfd/dot_general | solution.py:1290
  682.3 14.5 %fusion.52 = f32[2,1024,704]{1,2,0:T(8,128)} fusion(bf16[2,2560,1024]{2,1,0:T(8,128)(2,1)} %get-tuple-element.61, bf16[2,2560,704]{2,1,0:T(8,128)(2,1)} %get-tuple-element.63), kind=kOutput, calls=%fused_computation.93 | convolution fusion | flops 7381975040 | bytes 23461888 | tf_op jit(solution)/shard_map/xrd,xrf->xdf/dot_general | solution.py:1292
  696.8 11.2 %all-reduce.7.cloned.1.call-done = (bf16[32,1024]{1,0:T(8,128)(2,1)}, bf16[1024,1024]{1,0:T(8,128)(2,1)}, bf16[1024,1024]{1,0:T(8,128)(2,1)}, bf16[1024,1024]{1,0:T(8,128)(2,1)}, bf16[1024,1024]{1,0:T(8,128)(2,1)}) async-done(((bf16[32,1024]{1,0:T(8,128)(2,1)}, bf16[1024,1024]{1,0:T(8,128)(2,1)}, bf16[1024,1024]{1,0:T(8,128)(2,1)}, bf16[1024,1024]{1,0:T(8,128)(2,1)}, bf16[1024,1024]{1,0:T(8,128)(2,1)}), ...) | async-done | bytes 8454160 | tf_op jit(solution)/shard_map/psum | solution.py:1286
  708.0 1.4 fusion.48
  711.6 4.2 convert_element_type.179
  715.9 2.5 convert_element_type.180
  718.3 2.5 convert_element_type.181
  720.8 2.5 convert_element_type.182
  (89 shorter events, 10.1 us)
Async XLA Ops:
  7.2 149.3 %copy-start = (f32[1024,16]{0,1:T(8,128)S(1)}, f32[1024,16]{0,1:T(8,128)}, u32[]{:S(2)}) copy-start(f32[1024,16]{0,1:T(8,128)} %param.22) | copy-start | bytes 196612
  7.2 5.1 copy-start.4
  7.2 5.1 copy-start.17
  7.2 700.8 %all-reduce.7.cloned.1.call-start = ((), (), s32[]{:S(2)}) async-start(), calls=%async_computation | async-start | bytes 16908288 | tf_op jit(solution)/shard_map/psum | solution.py:1286
  12.3 4.0 copy-start.7
  16.3 2.3 copy-start.19
  18.6 2.3 copy-start.15
  151.8 3.3 copy-start.14
  155.0 3.5 copy-start.2
  437.0 4.6 copy-start.3
  441.6 4.1 copy-start.6
  445.7 1.2 copy-start.21
  447.0 2.6 copy-start.5
  447.0 2.6 copy-start.18
  480.7 3.3 copy-start.23
  484.0 2.7 copy-start.20
  484.0 2.7 copy-start.22
  489.4 2.7 copy-start.16
  492.6 4.1 copy-start.8
  492.6 4.1 copy-start.12
  492.6 4.1 copy-start.13
  711.6 4.2 copy-start.11
  715.9 2.5 copy-start.10
  718.3 2.5 copy-start.9
  720.8 2.5 copy-start.1
Sparse Core Ops, SparseCore 0:
  500.6 207.3 all-reduce.6

commit v4 on v3

--- a/solution.py
+++ b/solution.py
@@ -45,6 +45,10 @@
 
 def dot(matrix_a, matrix_b):
     return jnp.dot(matrix_a, matrix_b, preferred_element_type=jnp.float32)
+
+
+def dot_high(matrix_a, matrix_b):
+    return jnp.dot(matrix_a, matrix_b, precision=precise, preferred_element_type=jnp.float32)
 
 
 def slot_targets(routes, experts_all, capacity, stride):
@@ -142,38 +146,6 @@
     return grad_query, grad_key, grad_value, line
 
 
-def unmix_body(
-    query_ref, key_ref, value_ref, grad_ref, soft_ref, dq_ref, dk_ref, dv_ref, line_ref, grads_v
-):
-    for head in range(2):
-        at = slice(head * HEAD_DIM, (head + 1) * HEAD_DIM)
-        dq_ref[:, at], dk_ref[:, at], dv_ref[:, at], line_ref[0, head : head + 1, :] = unmix_head(
-            query_ref[:, at],
-            key_ref[:, at],
-            value_ref[:, at],
-            grad_ref[:, at],
-            soft_ref,
-            grads_v,
-            head,
-        )
-
-
-def unmix(query, key, value, grad_mixed, soft):
-    pair = pl.BlockSpec((LEN, 2 * HEAD_DIM), lambda i: (0, i))
-    rows = jax.ShapeDtypeStruct((LEN, D), jnp.bfloat16)
-    out = pl.pallas_call(
-        unmix_body,
-        grid=(HEADS // 2,),
-        in_specs=[pair] * 4 + [pl.BlockSpec((2, LEN, LEN), lambda i: (i, 0, 0))],
-        out_specs=[pair] * 3 + [pl.BlockSpec((1, 2, 4 * NEAR), lambda i: (i, 0, 0))],
-        out_shape=[rows] * 3 + [jax.ShapeDtypeStruct((HEADS // 2, 2, 4 * NEAR), jnp.float32)],
-        scratch_shapes=[pltpu.VMEM((LEN, LEN), jnp.bfloat16)],
-        compiler_params=pltpu.CompilerParams(vmem_limit_bytes=VMEM),
-        name="unmix",
-    )(query, key, value, grad_mixed, soft)
-    return out[0], out[1], out[2], out[3].reshape(HEADS, 4 * NEAR)
-
-
 class Plan:
     def __init__(self, n_e, n_h, experts_all, width):
         self.n_e, self.n_h, self.width = n_e, n_h, width
@@ -182,9 +154,15 @@
         self.span = 2 * self.stride
         self.rows = n_e * self.stride
         self.total = n_h * self.rows
+        self.relayed = n_e - 1 if (n_e, n_h) == (8, 4) else n_e
+        self.summed = (n_e, n_h) == (8, 4)
 
     def place(self):
         return lax.axis_index("expert"), lax.axis_index("hidden")
+
+    def chunk(self, z, source):
+        sign = 1 - 2 * lax.div(z, self.n_h // 2)
+        return lax.rem(sign * (source - z) + self.n_h, self.n_h)
 
     def source(self, z, chunk):
         sign = 1 - 2 * lax.div(z, self.n_h // 2)
@@ -249,6 +227,8 @@
             self.a_recv,
             self.m_send,
             self.m_recv,
+            self.r_send,
+            self.r_recv,
             self.local,
         ) = sems
 
@@ -265,6 +245,8 @@
             dma((n_h, n_e)),
             dma((n_h, n_e)),
             dma((n_h, n_e)),
+            dma((n_h, 2)),
+            dma((n_h,)),
             dma((3,)),
         ]
 
@@ -347,6 +329,64 @@
             (across(e, mask), z),
         )
 
+    def relay_copy(self, source, way):
+        plan = self.plan
+        e, z = plan.place()
+
+        def at(place):
+            chunk = plan.chunk(place, source)
+            return pl.ds(
+                pl.multiple_of((chunk * plan.n_e + plan.relayed) * plan.stride, 16), plan.stride
+            )
+
+        return remote(
+            self.out.at[:, at(z), :],
+            self.out.at[:, at(z + way), :],
+            self.r_send.at[source, (way + 1) // 2],
+            self.r_recv.at[source],
+            (e, z + way),
+        )
+
+    def relay(self, distance):
+        plan = self.plan
+        if plan.relayed == plan.n_e:
+            return
+        _, z = plan.place()
+
+        @pl.when(distance == 0)
+        def _():
+            self.in_plane(0, plan.relayed).wait_recv()
+
+            @pl.when(z > 0)
+            def _():
+                self.relay_copy(z, -1).start()
+
+            @pl.when(z < plan.n_h - 1)
+            def _():
+                self.relay_copy(z, 1).start()
+
+        def act(source, forwarded, way):
+            chunk = plan.chunk(z, source)
+            at = pl.ds(
+                pl.multiple_of((chunk * plan.n_e + plan.relayed) * plan.stride, 16), plan.stride
+            )
+            e, _ = plan.place()
+            remote(
+                self.out.at[:, at, :],
+                self.out.at[:, at, :],
+                self.r_send.at[source, 0],
+                self.r_recv.at[source],
+                (e, z - way),
+            ).wait_recv()
+
+            @pl.when(forwarded)
+            def _():
+                self.relay_copy(source, way).start()
+
+        @pl.when(distance > 0)
+        def _():
+            self.on_the_way(distance, act)
+
     def chunk(self, chunk, target_of):
         plan = self.plan
         e, z = plan.place()
@@ -377,12 +417,11 @@
 
         @pl.when(chunk >= 2)
         def _():
-            for mask in range(1, plan.n_e):
-                self.in_plane(chunk - 2, mask).wait_send()
+            self.wait_sent(chunk - 2)
 
         target = target_of(chunk)
         group = min(4, plan.n_e)
-        for start in range(0, plan.n_e, group):
+        for start in range(plan.n_e - group, -1, -group):
             for j in range(2):
                 hot = jnp.concatenate(
                     [
@@ -395,7 +434,13 @@
                 self.stage[
                     buffer, j, start * plan.stride : (start + group) * plan.stride, :
                 ] = picked
-            for mask in range(max(start, 1), start + group):
+            if start <= plan.relayed < start + group:
+
+                @pl.when(chunk == 0)
+                def _():
+                    self.in_plane(chunk, plan.relayed).start()
+
+            for mask in range(max(start, 1), min(start + group, plan.relayed)):
                 self.in_plane(chunk, mask).start()
         at = pl.multiple_of(chunk * plan.rows, 16)
         own = pltpu.make_async_copy(
@@ -407,16 +452,27 @@
         own.wait()
         own_meta.wait()
 
-    def arrived(self, chunk):
+    def wait_sent(self, chunk):
+        for mask in range(1, self.plan.relayed):
+            self.in_plane(chunk, mask).wait_send()
+        if self.plan.relayed < self.plan.n_e:
+
+            @pl.when(chunk == 0)
+            def _():
+                self.in_plane(chunk, self.plan.relayed).wait_send()
+
+    def told(self, chunk):
         for mask in range(1, self.plan.n_e):
             self.meta_copy(chunk, mask).wait_recv()
+
+    def arrived(self, chunk):
+        for mask in range(1, self.plan.relayed):
             self.in_plane(chunk, mask).wait_recv()
 
     def finish(self):
         plan = self.plan
         for chunk in range(max(0, plan.n_h - 2), plan.n_h):
-            for mask in range(1, plan.n_e):
-                self.in_plane(chunk, mask).wait_send()
+            self.wait_sent(chunk)
         _, z = plan.place()
 
         @pl.when(z > 0)
@@ -440,6 +496,23 @@
         for chunk in range(plan.n_h):
             for mask in range(1, plan.n_e):
                 self.meta_copy(chunk, mask).wait_send()
+        if plan.relayed < plan.n_e:
+
+            @pl.when(z > 0)
+            def _():
+                self.relay_copy(z, -1).wait_send()
+
+            @pl.when(z < plan.n_h - 1)
+            def _():
+                self.relay_copy(z, 1).wait_send()
+
+            def passed(source, forwarded, way):
+                @pl.when(forwarded)
+                def _():
+                    self.relay_copy(source, way).wait_send()
+
+            for distance in range(1, plan.n_h):
+                self.on_the_way(distance, passed)
 
 
 def same(index, other, count):
@@ -481,10 +554,8 @@
         return found
 
     def chunk_of(self, goal):
-        n_h = self.plan.n_h
         _, z = self.plan.place()
-        sign = 1 - 2 * lax.div(z, n_h // 2)
-        return lax.rem(sign * (goal - z) + n_h, n_h)
+        return self.plan.chunk(z, goal)
 
     def source(self, chunk, mask):
         raise NotImplementedError
@@ -695,45 +766,93 @@
 ANY = pl.BlockSpec(memory_space=pl.ANY)
 
 
-def send_body(
-    plan,
-    n_d,
-    rows,
-    meta,
-    query,
-    key,
-    value,
-    lines,
-    out,
-    meta_out,
-    land,
-    soft_out,
-    mixed_out,
-    rows_v,
-    meta_v,
-    stage,
-    query_v,
-    key_v,
-    value_v,
-    soft_v,
-    mixed_v,
-    in_sem,
-    soft_sem,
-    mixed_sem,
-    *sems,
-):
+def inverse_root(rows):
+    return lax.rsqrt(jnp.mean(rows * rows, axis=1, keepdims=True) + eps)
+
+
+def attend_body(plan, *refs):
+    (
+        grads,
+        targets,
+        tokens,
+        w_query,
+        w_key,
+        w_value,
+        w_out,
+        lines,
+        gains,
+        w_router,
+        routes,
+        grads_out,
+        targets_out,
+        land,
+        soft_out,
+        mixed_out,
+        normed_out,
+        query_out,
+        key_out,
+        value_out,
+        hidden_out,
+        sent_out,
+        gates_out,
+        roots_out,
+        rows_v,
+        meta_v,
+        stage,
+        tokens_v,
+        weights_v,
+        normed_v,
+        heads_v,
+        soft_v,
+        mixed_v,
+        hidden_v,
+        in_sem,
+        soft_sem,
+        out_sem,
+        *sems,
+    ) = refs
     loads = [
         pltpu.make_async_copy(given, held, in_sem.at[i])
-        for i, (given, held) in enumerate(((query, query_v), (key, key_v), (value, value_v)))
+        for i, (given, held) in enumerate(
+            [(tokens, tokens_v)]
+            + [
+                (weight, weights_v.at[k])
+                for k, weight in enumerate((w_query, w_key, w_value, w_out))
+            ]
+        )
     ]
     for load in loads:
         load.start()
     greet(plan)
-    work = Dispatch(plan, rows, meta, land, out, meta_out, rows_v, meta_v, stage, sems)
+    work = Dispatch(plan, grads, targets, land, grads_out, targets_out, rows_v, meta_v, stage, sems)
     work.begin()
     _, z = plan.place()
-    for load in loads:
-        load.wait()
+    stores = [
+        pltpu.make_async_copy(held, out, out_sem.at[i])
+        for i, (held, out) in enumerate(
+            (
+                (normed_v, normed_out),
+                (heads_v.at[0], query_out),
+                (heads_v.at[1], key_out),
+                (heads_v.at[2], value_out),
+                (mixed_v, mixed_out),
+                (hidden_v, hidden_out),
+                (normed_v, sent_out),
+            )
+        )
+    ]
+
+    def project():
+        for load in loads:
+            load.wait()
+        rows = tokens_v[...].astype(jnp.float32)
+        root = inverse_root(rows)
+        roots_out[:, 0:128] = jnp.broadcast_to(root, (LEN, 128))
+        normed_v[...] = (rows * root * gains[0:1, :]).astype(jnp.bfloat16)
+        for k in range(3):
+            heads_v[k] = dot(normed_v[...], weights_v[k]).astype(jnp.bfloat16)
+        for store in stores[:4]:
+            store.start()
 
     def soft_copy(pair):
         buffer = lax.rem(pair, 2)
@@ -743,7 +862,7 @@
 
     def mix_pair(pair):
         lanes = pl.ds(pl.multiple_of(pair * 2 * HEAD_DIM, 2 * HEAD_DIM), 2 * HEAD_DIM)
-        both = [held[:, lanes] for held in (query_v, key_v, value_v)]
+        both = [heads_v[k, :, lanes] for k in range(3)]
 
         @pl.when(pair >= 2)
         def _():
@@ -763,60 +882,125 @@
         mixed_v[:, lanes] = jnp.concatenate(heads, axis=1)
         soft_copy(pair).start()
 
+    def route():
+        stores[4].start()
+        hidden = tokens_v[...].astype(jnp.float32) + dot(mixed_v[...], weights_v[3])
+        hidden_v[...] = hidden
+        stores[5].start()
+        root = inverse_root(hidden)
+        roots_out[:, 128:256] = jnp.broadcast_to(root, (LEN, 128))
+        normed = hidden * root * gains[1:2, :]
+        stores[0].wait()
+        normed_v[...] = normed.astype(jnp.bfloat16)
+        stores[6].start()
+        logits = contract_last(w_router[...], normed, precise)
+        experts = lax.broadcasted_iota(jnp.int32, logits.shape, 0).astype(jnp.float32)
+        chosen = [
+            jnp.sum(jnp.where(experts == routes[k : k + 1, :], logits, 0.0), axis=0, keepdims=True)
+            for k in range(2)
+        ]
+        peak = jnp.maximum(chosen[0], chosen[1])
+        terms = [jnp.exp(item - peak) for item in chosen]
+        for k in range(2):
+            gates_out[k : k + 1, :] = terms[k] / (terms[0] + terms[1])
+        gates_out[2:8, :] = jnp.zeros((6, LEN), jnp.float32)
+
     pairs = HEADS // 2
-    each = -(-pairs // plan.n_h)
+    each = -(-pairs // (plan.n_h - 1))
 
     @pl.loop(0, plan.n_h)
     def _(chunk):
         work.chunk(chunk, lambda at: meta_v[plan.source(z, at)])
-        pl.loop(0, each)(lambda i: mix_pair(chunk * each + i))
-
-    mixed_copy = pltpu.make_async_copy(mixed_v, mixed_out, mixed_sem.at[0])
-    mixed_copy.start()
+        pl.when(chunk == 0)(project)
+        work.relay(chunk)
+
+        @pl.loop(0, each)
+        def _(i):
+            pair = chunk * each + i
+            pl.when(pair < pairs)(lambda: mix_pair(pair))
+
     soft_copy(pairs - 2).wait()
     soft_copy(pairs - 1).wait()
-    mixed_copy.wait()
+    route()
+    for store in stores[1:]:
+        store.wait()
     for chunk in range(plan.n_h):
+        work.told(chunk)
         work.arrived(chunk)
     work.finish()
 
 
-def send_rows(plan, rows, meta, query, key, value, lines):
+def attend(
+    plan,
+    grads,
+    targets,
+    tokens,
+    w_query,
+    w_key,
+    w_value,
+    w_out,
+    lines,
+    gains,
+    w_router,
+    routes,
+):
     n_h, n_e = plan.n_h, plan.n_e
     bf16, f32 = jnp.bfloat16, jnp.float32
     shape = jax.ShapeDtypeStruct
-    sems = Dispatch.sem_shapes(plan)
-    out = pl.pallas_call(
-        functools.partial(send_body, plan, len(sems)),
-        in_specs=[ANY] * 5 + [pl.BlockSpec(memory_space=pltpu.VMEM)],
-        out_specs=[ANY] * 5,
+    vmem = pl.BlockSpec(memory_space=pltpu.VMEM)
+    rows = shape((LEN, D), bf16)
+    return pl.pallas_call(
+        functools.partial(attend_body, plan),
+        in_specs=[ANY] * 7 + [vmem] * 4,
+        out_specs=[ANY] * 11 + [vmem] * 2,
         out_shape=[
             shape((2, plan.total, D), bf16),
             shape((n_h, n_e, 8, LEN), f32),
             shape((n_h, LEN, D), bf16),
             shape((HEADS, LEN, LEN), bf16),
-            shape((LEN, D), bf16),
+            rows,
+            rows,
+            rows,
+            rows,
+            rows,
+            shape((LEN, D), f32),
+            rows,
+            shape((8, LEN), f32),
+            shape((LEN, 256), f32),
         ],
         scratch_shapes=[
             pltpu.VMEM((2, LEN, D), bf16),
             pltpu.VMEM((n_h, 8, LEN), f32),
             pltpu.VMEM((2, 2, plan.rows, D), bf16),
             pltpu.VMEM((LEN, D), bf16),
+            pltpu.VMEM((4, D, D), bf16),
             pltpu.VMEM((LEN, D), bf16),
-            pltpu.VMEM((LEN, D), bf16),
+            pltpu.VMEM((3, LEN, D), bf16),
             pltpu.VMEM((2, 2, LEN, LEN), bf16),
             pltpu.VMEM((LEN, D), bf16),
-            pltpu.SemaphoreType.DMA((3,)),
+            pltpu.VMEM((LEN, D), f32),
+            pltpu.SemaphoreType.DMA((5,)),
             pltpu.SemaphoreType.DMA((2,)),
-            pltpu.SemaphoreType.DMA((1,)),
+            pltpu.SemaphoreType.DMA((7,)),
         ]
-        + sems,
+        + Dispatch.sem_shapes(plan),
         compiler_params=pltpu.CompilerParams(
             collective_id=1, has_side_effects=True, vmem_limit_bytes=VMEM
         ),
-        name="send_rows",
-    )(rows, meta, query, key, value, lines.reshape(HEADS // 2, 2, 4 * NEAR))
-    return out[0], out[1], out[3], out[4]
+        name="attend",
+    )(
+        grads,
+        targets,
+        tokens,
+        w_query,
+        w_key,
+        w_value,
+        w_out,
+        lines.reshape(HEADS // 2, 2, 4 * NEAR),
+        gains,
+        w_router,
+        routes,
+    )
 
 
 def expert_body(plan, halves, n_d, *refs):
@@ -859,6 +1043,8 @@
         gg_back,
         gg_part,
         gg_land,
+        column_v,
+        dots_v,
         sum_v,
         total,
         w_sem,
@@ -893,7 +1079,12 @@
     work.begin()
     targets_in.wait()
     ahead = min(3, n_h)
-    pl.loop(0, ahead)(lambda chunk: work.chunk(chunk, lambda at: target_v[at, 0]))
+
+    @pl.loop(0, ahead)
+    def _(chunk):
+        work.chunk(chunk, lambda at: target_v[at, 0])
+        work.relay(chunk)
+
     for load in loads:
         load.wait()
 
@@ -934,42 +1125,49 @@
     masks = n_e // halves
     piece = masks * plan.stride
 
+    def own_slots(j):
+        slots = lax.broadcasted_iota(jnp.int32, (plan.stride, LEN), 0).astype(jnp.float32)
+        return slots + slot_base(plan, e, j)
+
+    def weigh(chunk, mask):
+        aim, weight = target_v[chunk, mask], gate_v[mask]
+        at = pl.ds(pl.multiple_of(mask * plan.stride, 16), plan.stride)
+        for j in range(2):
+            hit = jnp.where(own_slots(j) == aim[0:1, :], weight[0:1, :], 0.0)
+            hit = hit + jnp.where(own_slots(j) == aim[1:2, :], weight[1:2, :], 0.0)
+            column_v[j, at, :] = jnp.broadcast_to(
+                jnp.sum(hit, axis=1, keepdims=True), (plan.stride, 128)
+            )
+
+    def spread(chunk, mask):
+        aim = target_v[chunk, mask]
+        at = pl.ds(pl.multiple_of(mask * plan.stride, 16), plan.stride)
+        for k in range(2):
+            line = jnp.zeros((1, LEN), jnp.float32)
+            for j in range(2):
+                hit = own_slots(j) == aim[k : k + 1, :]
+                line = line + jnp.sum(
+                    jnp.where(hit, dots_v[j, at, 0:1], 0.0), axis=0, keepdims=True
+                )
+            gg_v[chunk, mask, k : k + 1, :] = line
+
     def step(chunk, index):
         j, half = lax.div(index, halves), lax.rem(index, halves)
         at = pl.ds(pl.multiple_of(half * piece, 16), piece)
-        rows, grads_in = x_v[j, at, :], g_v[j, at, :]
-        gate_pre = contract_last(rows, wg_v[j])
-        up_pre = contract_last(rows, wu_v[j])
-        raw = contract_last(grads_in, wd_v[j])
-        slots = lax.broadcasted_iota(jnp.int32, (plan.stride, LEN), 0).astype(
-            jnp.float32
-        ) + slot_base(plan, e, j)
-        columns = []
-        for i in range(masks):
-            mask = half * masks + i
-            aim, weight = target_v[chunk, mask], gate_v[mask]
-            hit = jnp.where(slots == aim[0:1, :], weight[0:1, :], 0.0)
-            hit = hit + jnp.where(slots == aim[1:2, :], weight[1:2, :], 0.0)
-            columns.append(jnp.sum(hit, axis=1, keepdims=True))
-        gate = jnp.concatenate(columns, axis=0)
+        gate_pre = contract_last(x_v[j, at, :], wg_v[j])
+        up_pre = contract_last(x_v[j, at, :], wu_v[j])
+        raw = contract_last(g_v[j, at, :], wd_v[j])
+        gate = column_v[j, at, 0:1]
         square = gate_pre * gate_pre
-        tanh = jnp.tanh(0.7978845608028654 * gate_pre * (1.0 + 0.044715 * square))
-        side = 0.5 * (1.0 + tanh)
+        tanh = jnp.tanh(gate_pre * (0.7978845608028654 + 0.035677408136300125 * square))
+        side = 0.5 + 0.5 * tanh
         gelu = gate_pre * side
-        slope = side + 0.5 * gate_pre * (1.0 - tanh * tanh) * (
-            0.7978845608028654 * (1.0 + 0.134145 * square)
-        )
+        slope = side + gelu * (1.0 - side) * (1.5957691216057308 + 0.21406444881780075 * square)
         act = gelu * up_pre
         act_low = act.astype(jnp.bfloat16)
-        dots = jnp.sum(act_low.astype(jnp.float32) * raw, axis=1, keepdims=True)
-        for i in range(masks):
-            mask = half * masks + i
-            aim, part = target_v[chunk, mask], dots[i * plan.stride : (i + 1) * plan.stride]
-            for k in range(2):
-                line = jnp.sum(
-                    jnp.where(slots == aim[k : k + 1, :], part, 0.0), axis=0, keepdims=True
-                )
-                gg_v[chunk, mask, k : k + 1, :] += line
+        dots_v[j, at, :] = jnp.broadcast_to(
+            jnp.sum(act_low.astype(jnp.float32) * raw, axis=1, keepdims=True), (piece, 128)
+        )
         grad_act = gate * raw
         grad_gate = (grad_act * up_pre * slope).astype(jnp.bfloat16)
         grad_up = (grad_act * gelu).astype(jnp.bfloat16)
@@ -985,16 +1183,17 @@
 
     @pl.loop(0, n_h)
     def _(chunk):
-        work.arrived(chunk)
         at = pl.multiple_of(chunk * plan.rows, 16)
-        gate_in = pltpu.make_async_copy(meta_out.at[chunk], gate_v, t_sem.at[0])
-        gate_in.start()
         ins = [
             pltpu.make_async_copy(source.at[:, pl.ds(at, plan.rows), :], held, x_sem.at[i])
             for i, (source, held) in enumerate(((rows_out, x_v), (grads, g_v)))
         ]
-        for copy in ins:
-            copy.start()
+        ins[1].start()
+        work.told(chunk)
+        gate_in = pltpu.make_async_copy(meta_out.at[chunk], gate_v, t_sem.at[0])
+        gate_in.start()
+        gate_in.wait()
+        pl.loop(0, n_e)(lambda mask: weigh(chunk, mask))
         give.free(chunk)
 
         @pl.when(chunk > 0)
@@ -1003,7 +1202,8 @@
                 for copy in outs(chunk - 1, j):
                     copy.wait()
 
-        gate_in.wait()
+        work.arrived(chunk)
+        ins[0].start()
         for copy in ins:
             copy.wait()
         pl.loop(0, 2 * halves)(lambda index: step(chunk, index))
@@ -1014,13 +1214,15 @@
         @pl.when(chunk + ahead < n_h)
         def _():
             work.chunk(chunk + ahead, lambda at: target_v[at, 0])
-
+            work.relay(chunk + ahead)
+
+        @pl.when((chunk < 1) | (not all_held))
+        def _():
+            give.send(chunk)
+
+        pl.loop(0, n_e)(lambda mask: spread(chunk, mask))
         for mask in range(1, n_e):
             gg_copy(chunk, mask).start()
-
-        @pl.when((chunk < 1) | (not all_held))
-        def _():
-            give.send(chunk)
 
     def early_copy(mask):
         at = pl.ds(mask * plan.stride, plan.stride)
@@ -1122,6 +1324,8 @@
             pltpu.VMEM((n_h, n_e, 8, LEN), f32),
             pltpu.VMEM((n_h, 8, LEN), f32),
             pltpu.VMEM((n_h, 8, LEN), f32),
+            pltpu.VMEM((2, plan.rows, 128), f32),
+            pltpu.VMEM((2, plan.rows, 128), f32),
             pltpu.VMEM((LEN, D), bf16),
             pltpu.VMEM((LEN, D), f32),
             dma((3,)),
@@ -1144,47 +1348,579 @@
     )(sent, gates, grads, targets, jnp.swapaxes(w_gate, 1, 2), jnp.swapaxes(w_up, 1, 2), w_down)
 
 
-def back_body(
-    plan, given, early, targets, out, back, land, rows_v, stage, target_v, sum_v, total, t_sem, *sems
-):
+class Sum:
+    pieces, stages, few = 4, 5, 32
+
+    def __init__(self, plan, held, whole, few_v, few_in, *rest):
+        self.plan = plan
+        self.held, self.whole, self.few_v, self.few_in = held, whole, few_v, few_in
+        self.landed, (self.send, self.recv, self.f_send, self.f_recv) = rest[:5], rest[5:]
+
+    @classmethod
+    def scratch_shapes(cls):
+        dma = pltpu.SemaphoreType.DMA
+        bf16, f32 = jnp.bfloat16, jnp.float32
+        rows = (D // 2, D // 4, D // 8, D // 16, D // 32)
+        return (
+            [
+                pltpu.VMEM((cls.pieces, D, D), bf16),
+                pltpu.VMEM((cls.pieces, D, D), bf16),
+                pltpu.VMEM((cls.stages + 1, cls.few, D), f32),
+                pltpu.VMEM((cls.stages, cls.few, D), f32),
+            ]
+            + [pltpu.VMEM((cls.pieces, count, D), bf16) for count in rows]
+            + [
+                dma((2 * cls.stages, cls.pieces, 2)),
+                dma((2 * cls.stages, cls.pieces, 2)),
+                dma((cls.stages,)),
+                dma((cls.stages,)),
+            ]
+        )
+
+    def partner(self, bit):
+        e, z = self.plan.place()
+        if bit < 3:
+            return (across(e, 1 << bit), z)
+        return (e, across(z, 1 << (bit - 3)))
+
+    def parts(self, stage):
+        e, z = self.plan.place()
+        place = [lax.rem(lax.div(e, 1 << k), 2) for k in range(3)]
+        place += [lax.rem(lax.div(z, 1 << k), 2) for k in range(2)]
+        base, count = place[0] * (D // 2), D // 2
+        if stage == 1:
+            return [(self.partner(0), base, D // 2 - base, count)]
+        out = []
+        for part, order in enumerate(((1, 2, 3, 4), (2, 1, 3, 4))):
+            at, count = base + part * (D // 4), D // 4
+            for bit in order[: stage - 1]:
+                count //= 2
+                keep, give = at + place[bit] * count, at + (1 - place[bit]) * count
+                at = keep
+            out.append((self.partner(bit), keep, give, count))
+        return out
+
+    def copies(self, stage, piece):
+        halving = stage <= self.stages
+        out = []
+        parts = self.parts(stage if halving else 2 * self.stages + 1 - stage)
+        for part, (device, keep, give, count) in enumerate(parts):
+            here = pl.ds(pl.multiple_of(give if halving else keep, 16), count)
+            there = (
+                self.landed[stage - 1].at[piece, part * count : (part + 1) * count, :]
+                if halving
+                else self.whole.at[piece, here, :]
+            )
+            out.append(
+                remote(
+                    (self.held if halving else self.whole).at[piece, here, :],
+                    there,
+                    self.send.at[stage - 1, piece, part],
+                    self.recv.at[stage - 1, piece, part],
+                    device,
+                )
+            )
+        return out
+
+    def few_copy(self, stage):
+        return remote(
+            self.few_v.at[stage - 1],
+            self.few_in.at[stage - 1],
+            self.f_send.at[stage - 1],
+            self.f_recv.at[stage - 1],
+            self.partner(stage - 1),
+        )
+
+    def add(self, stage, piece):
+        for part, (_, keep, _, count) in enumerate(self.parts(stage)):
+            tile = min(count, 64)
+
+            @pl.loop(0, count // tile)
+            def _(i):
+                at = pl.ds(pl.multiple_of(keep + i * tile, 16), tile)
+                come = pl.ds(pl.multiple_of(part * count + i * tile, 16), tile)
+                total = self.held[piece, at, :].astype(jnp.float32) + self.landed[stage - 1][
+                    piece, come, :
+                ].astype(jnp.float32)
+                into = self.whole if stage == self.stages else self.held
+                into[piece, at, :] = total.astype(jnp.bfloat16)
+
+    slots = pieces + 2 * stages
+
+    def slot(self, slot, ready, done):
+        for piece in range(self.pieces):
+            stage = slot - piece + 1
+            if stage == 1:
+                ready(piece)
+            if 2 <= stage <= 2 * self.stages + 1:
+                for copy in self.copies(stage - 1, piece):
+                    copy.wait_recv()
+                if stage - 1 <= self.stages:
+                    self.add(stage - 1, piece)
+            if 1 <= stage <= 2 * self.stages:
+                for copy in self.copies(stage, piece):
+                    copy.start()
+            if stage == 2 * self.stages + 1:
+                done(piece)
+        stage = slot + 1
+        if 2 <= stage <= self.stages + 1:
+            self.few_copy(stage - 1).wait_recv()
+            self.few_v[stage - 1] = self.few_v[stage - 2] + self.few_in[stage - 2]
+        if stage <= self.stages:
+            self.few_copy(stage).start()
+
+    def finish(self):
+        for stage in range(1, 2 * self.stages + 1):
+            for piece in range(self.pieces):
+                for copy in self.copies(stage, piece):
+                    copy.wait_send()
+        for stage in range(1, self.stages + 1):
+            self.few_copy(stage).wait_send()
+
+
+def sum_body(plan, *refs):
+    n_h = plan.n_h
+    dgate, dup, act, rows, grads = refs[:5]
+    refs = refs[5:]
+    if plan.summed:
+        low, few = refs[:2]
+        refs = refs[2:]
+    outs, refs = refs[:3], refs[3:]
+    if plan.summed:
+        sums_out, few_out = refs[:2]
+        refs = refs[2:]
+    left_v, right_v, made_v, p_sem, g_sem = refs[:5]
+    steps = 3 * n_h
+
+    def factors(q, act_on):
+        buffer = lax.rem(q, 2)
+        at = pl.ds(pl.multiple_of(lax.rem(q, n_h) * plan.rows, 16), plan.rows)
+
+        def copies(lefts, rights):
+            for i in range(2):
+                for k, ((source, j), held) in enumerate(((lefts[i], left_v), (rights[i], right_v))):
+                    act_on(
+                        pltpu.make_async_copy(
+                            source.at[j, at, :], held.at[buffer, i], p_sem.at[buffer, 2 * i + k]
+                        )
+                    )
+
+        @pl.when(q < 2 * n_h)
+        def _():
+            j = lax.div(q, n_h)
+            copies(((dgate, j), (dup, j)), ((rows, j), (rows, j)))
+
+        @pl.when(q >= 2 * n_h)
+        def _():
+            copies(((act, 0), (act, 1)), ((grads, 0), (grads, 1)))
+
+    def results(group, act_on):
+        @pl.when(group < 2)
+        def _():
+            for i in range(2):
+                act_on(pltpu.make_async_copy(made_v.at[i], outs[i].at[group], g_sem.at[i]))
+
+        @pl.when(group == 2)
+        def _():
+            for i in range(2):
+                act_on(pltpu.make_async_copy(made_v.at[i], outs[2].at[i], g_sem.at[i]))
+
+    def product(q):
+        buffer, turn, group = lax.rem(q, 2), lax.rem(q, n_h), lax.div(q, n_h)
+        factors(q, lambda copy: copy.wait())
+
+        @pl.when(q + 1 < steps)
+        def _():
+            factors(q + 1, lambda copy: copy.start())
+
+        @pl.when((turn == 0) & (q > 0))
+        def _():
+            results(group - 1, lambda copy: copy.wait())
+
+        @pl.when(turn == 0)
+        def _():
+            made_v[...] = jnp.zeros_like(made_v)
+
+        for i in range(2):
+            made_v[i] += contract_first(left_v[buffer, i], right_v[buffer, i])
+
+        @pl.when(turn == n_h - 1)
+        def _():
+            results(group, lambda copy: copy.start())
+
+    factors(0, lambda copy: copy.start())
+    if plan.summed:
+        load_sem, store_sem = refs[5:7]
+        total = Sum(plan, *refs[7:])
+        loads = [
+            pltpu.make_async_copy(low.at[i], total.held.at[i], load_sem.at[i]) for i in range(4)
+        ]
+        stores = [
+            pltpu.make_async_copy(total.whole.at[i], sums_out.at[i], store_sem.at[i])
+            for i in range(4)
+        ]
+        for load in loads:
+            load.start()
+        total.few_v[0] = few[...]
+        greet(plan)
+        done = 0
+        for slot in range(total.slots):
+            total.slot(slot, lambda i: loads[i].wait(), lambda i: stores[i].start())
+            if slot % 2 == 0 and done < steps:
+                pl.loop(done, min(done + 2, steps))(product)
+                done = min(done + 2, steps)
+        few_out[...] = total.few_v[total.stages]
+        total.finish()
+        for store in stores:
+            store.wait()
+    else:
+        pl.loop(0, steps)(product)
+    results(2, lambda copy: copy.wait())
+
+
+def sum_all(plan, dgate, dup, act, rows, grads, low, few):
+    bf16, f32 = jnp.bfloat16, jnp.float32
+    shape = jax.ShapeDtypeStruct
+    vmem = pl.BlockSpec(memory_space=pltpu.VMEM)
+    dma = pltpu.SemaphoreType.DMA
+    args = [dgate, dup, act, rows, grads]
+    in_specs, out_specs = [ANY] * 5, [ANY] * 3
+    out_shape = [shape((2, plan.width, D), f32)] * 3
+    scratch_shapes = [
+        pltpu.VMEM((2, 2, plan.rows, plan.width), bf16),
+        pltpu.VMEM((2, 2, plan.rows, D), bf16),
+        pltpu.VMEM((2, plan.width, D), f32),
+        dma((2, 4)),
+        dma((2,)),
+    ]
+    params = {"vmem_limit_bytes": VMEM}
+    if plan.summed:
+        args += [low, few]
+        in_specs += [ANY, vmem]
+        out_specs += [ANY, vmem]
+        out_shape += [shape((4, D, D), bf16), shape((Sum.few, D), f32)]
+        scratch_shapes += [dma((4,)), dma((4,))] + Sum.scratch_shapes()
+        params.update(collective_id=4, has_side_effects=True)
+    out = pl.pallas_call(
+        functools.partial(sum_body, plan),
+        in_specs=in_specs,
+        out_specs=out_specs,
+        out_shape=out_shape,
+        scratch_shapes=scratch_shapes,
+        compiler_params=pltpu.CompilerParams(**params),
+        name="sum_all",
+    )(*args)
+    if plan.summed:
+        return out[:3], out[3], out[4]
+    return out[:3], *lax.psum((low, few), ("expert", "hidden"))
+
+
+def unattend_body(plan, n_r, *refs):
+    (
+        given,
+        early,
+        targets,
+        grad_sent,
+        hidden,
+        grad_out,
+        tokens,
+        mixed,
+        normed,
+        query,
+        key,
+        value,
+        soft,
+        w_query,
+        w_key,
+        w_value,
+        w_out,
+        grad_gates,
+        gates,
+        routes,
+        w_router,
+        gains,
+        roots,
+        branch_out,
+        back,
+        land,
+        low_out,
+        tokens_out,
+        few_out,
+        lines_out,
+        rows_v,
+        stage,
+        target_v,
+        sum_v,
+        total,
+        grad_sent_v,
+        hidden_v,
+        grad_out_v,
+        tokens_v,
+        mixed_v,
+        normed_v,
+        heads_v,
+        soft_v,
+        weights_v,
+        grad_hidden_v,
+        branch_v,
+        grad_heads_v,
+        grads_v,
+        low_v,
+        wide_v,
+        t_sem,
+        in_sem,
+        soft_sem,
+        low_sem,
+        out_sem,
+        *sems,
+    ) = refs
+    f32, bf16 = jnp.float32, jnp.bfloat16
+    ins = [
+        (grad_sent, grad_sent_v),
+        (hidden, hidden_v),
+        (grad_out, grad_out_v),
+        (mixed, mixed_v),
+        (w_out, weights_v.at[3]),
+        (query, heads_v.at[0]),
+        (key, heads_v.at[1]),
+        (value, heads_v.at[2]),
+        (normed, normed_v),
+        (w_query, weights_v.at[0]),
+        (w_key, weights_v.at[1]),
+        (w_value, weights_v.at[2]),
+        (tokens, tokens_v),
+    ]
+    loads = [
+        pltpu.make_async_copy(source, held, in_sem.at[i]) for i, (source, held) in enumerate(ins)
+    ]
     targets_in = pltpu.make_async_copy(targets, target_v, t_sem.at[0])
+
+    def soft_copy(pair):
+        buffer = lax.rem(pair, 2)
+        return pltpu.make_async_copy(
+            soft.at[pl.ds(2 * pair, 2)], soft_v.at[buffer], soft_sem.at[buffer]
+        )
+
     targets_in.start()
+    for load in loads:
+        load.start()
+    soft_copy(0).start()
     greet(plan)
-    give = ReturnHeld(plan, given, early, back, land, out, stage, rows_v, sum_v, total, sems)
-    pl.loop(0, plan.n_h - 1)(lambda turn: give.send(give.chunk_of(give.goal(turn))))
+    give = ReturnHeld(plan, given, early, back, land, branch_out, stage, rows_v, sum_v, total, sems)
+    turns = plan.n_h
+    pl.loop(0, turns - 1)(lambda turn: give.send(give.chunk_of(give.goal(turn))))
     targets_in.wait()
-    pl.loop(0, plan.n_h)(lambda turn: give.combine(turn, lambda at: target_v[at, 0]))
+
+    def combine(turn):
+        give.combine(turn, lambda at: target_v[at, 0])
+
+    tile = 64
+
+    def low_copy(i):
+        return pltpu.make_async_copy(low_v.at[i % 2], low_out.at[i], low_sem.at[i % 2])
+
+    for load in loads[:3]:
+        load.wait()
+    few_out[...] = jnp.zeros_like(few_out)
+    mean = gates[0:1, :] * grad_gates[0:1, :] + gates[1:2, :] * grad_gates[1:2, :]
+    experts = w_router.shape[0]
+    numbers = lax.broadcasted_iota(jnp.int32, (experts, LEN), 0).astype(f32)
+    grad_logits = jnp.zeros((experts, LEN), f32)
+    for k in range(2):
+        chosen = gates[k : k + 1, :] * (grad_gates[k : k + 1, :] - mean)
+        grad_logits = grad_logits + jnp.where(numbers == routes[k : k + 1, :], chosen, 0.0)
+    wide_v[...] = contract_first(grad_logits, w_router[...], precise)
+
+    @pl.loop(0, LEN // tile)
+    def _(i):
+        at = pl.ds(pl.multiple_of(i * tile, 16), tile)
+        rows, root = hidden_v[at, :], roots[at, 128:129]
+        grad = wide_v[at, :] + grad_sent_v[at, :]
+        near = rows * root
+        few_out[experts + 1 : experts + 2, :] += jnp.sum(grad * near, axis=0, keepdims=True)
+        scaled = grad * gains[1:2, :]
+        pull = jnp.mean(scaled * rows, axis=1, keepdims=True) * (root * root * root)
+        grad = grad_out_v[at, :].astype(f32) + root * scaled - rows * pull
+        grad_hidden_v[at, :] = grad
+        branch_v[at, :] = grad.astype(bf16)
+        grad_sent_v[at, :] = near * gains[1:2, :]
+
+    few_out[0:experts, :] = dot_high(grad_logits, grad_sent_v[...])
+    for load in loads[3:5]:
+        load.wait()
+    low_v[1] = contract_first(mixed_v[...], branch_v[...]).astype(bf16)
+    low_copy(3).start()
+    mixed_v[...] = contract_last(branch_v[...], weights_v[3]).astype(bf16)
+    for load in loads[5:8]:
+        load.wait()
+
+    def unmix_pair(pair):
+        lanes = pl.ds(pl.multiple_of(pair * 2 * HEAD_DIM, 2 * HEAD_DIM), 2 * HEAD_DIM)
+        soft_copy(pair).wait()
+
+        @pl.when(pair + 1 < HEADS // 2)
+        def _():
+            soft_copy(pair + 1).start()
+
+        both = [heads_v[k, :, lanes] for k in range(3)] + [mixed_v[:, lanes]]
+        found = []
+        for head in range(2):
+            at = slice(head * HEAD_DIM, (head + 1) * HEAD_DIM)
+            found.append(
+                unmix_head(
+                    *[item[:, at] for item in both], soft_v.at[lax.rem(pair, 2)], grads_v, head
+                )
+            )
+        for k in range(3):
+            grad_heads_v[k, :, lanes] = jnp.concatenate([found[0][k], found[1][k]], axis=1)
+        lines_out[pair] = jnp.concatenate([found[0][3], found[1][3]], axis=0)
+
+    pairs = HEADS // 2
+    pl.loop(0, pairs // 2)(unmix_pair)
+    combine(0)
+    pl.loop(pairs // 2, pairs)(unmix_pair)
+    combine(1)
+    for load in loads[8:]:
+        load.wait()
+    for k in range(3):
+        if k == 1:
+            low_copy(3).wait()
+        if k == 2:
+            low_copy(0).wait()
+        low_v[k % 2] = contract_first(normed_v[...], grad_heads_v[k]).astype(bf16)
+        low_copy(k).start()
+    wide_v[...] = (
+        contract_last(grad_heads_v[0], weights_v[0])
+        + contract_last(grad_heads_v[1], weights_v[1])
+        + contract_last(grad_heads_v[2], weights_v[2])
+    )
+
+    @pl.loop(0, LEN // tile)
+    def _(i):
+        at = pl.ds(pl.multiple_of(i * tile, 16), tile)
+        rows, root = tokens_v[at, :].astype(f32), roots[at, 0:1]
+        grad = wide_v[at, :]
+        few_out[experts : experts + 1, :] += jnp.sum(grad * rows * root, axis=0, keepdims=True)
+        scaled = grad * gains[0:1, :]
+        pull = jnp.mean(scaled * rows, axis=1, keepdims=True) * (root * root * root)
+        grad_hidden_v[at, :] = grad_hidden_v[at, :] + root * scaled - rows * pull
+
+    tokens_copy = pltpu.make_async_copy(grad_hidden_v, tokens_out, out_sem.at[0])
+    tokens_copy.start()
+    for turn in range(2, turns):
+        combine(turn)
     give.sent()
     give.finish()
-
-
-def bring_back(plan, given, early, targets):
+    for i in (1, 2):
+        low_copy(i).wait()
+    tokens_copy.wait()
+
+
+def unattend(
+    plan,
+    given,
+    early,
+    targets,
+    grad_sent,
+    hidden,
+    grad_out,
+    tokens,
+    mixed,
+    normed,
+    query,
+    key,
+    value,
+    soft,
+    w_query,
+    w_key,
+    w_value,
+    w_out,
+    grad_gates,
+    gates,
+    routes,
+    w_router,
+    gains,
+    roots,
+):
     n_h, n_e = plan.n_h, plan.n_e
     bf16, f32 = jnp.bfloat16, jnp.float32
     shape = jax.ShapeDtypeStruct
-    return pl.pallas_call(
-        functools.partial(back_body, plan),
-        in_specs=[ANY] * 3,
-        out_specs=[ANY] * 3,
+    vmem = pl.BlockSpec(memory_space=pltpu.VMEM)
+    dma = pltpu.SemaphoreType.DMA
+    sems = Return.sem_shapes(plan)
+    few = -(-(w_router.shape[0] + 3) // Sum.few) * Sum.few
+    rows, wide = pltpu.VMEM((LEN, D), bf16), pltpu.VMEM((LEN, D), f32)
+    out = pl.pallas_call(
+        functools.partial(unattend_body, plan, len(sems)),
+        in_specs=[ANY] * 17 + [vmem] * 6,
+        out_specs=[ANY] * 5 + [vmem] * 2,
         out_shape=[
             shape((LEN, D), f32),
             shape((n_h, 2, plan.rows, D), bf16),
             shape((2, n_h, LEN, D), bf16),
+            shape((4, D, D), bf16),
+            shape((LEN, D), f32),
+            shape((few, D), f32),
+            shape((HEADS // 2, 2, 4 * NEAR), f32),
         ],
         scratch_shapes=[
             pltpu.VMEM((2, LEN, D), bf16),
             pltpu.VMEM((2, 2, plan.rows, D), bf16),
             pltpu.VMEM((n_h, n_e, 8, LEN), f32),
-            pltpu.VMEM((LEN, D), bf16),
-            pltpu.VMEM((LEN, D), f32),
-            pltpu.SemaphoreType.DMA((1,)),
+            rows,
+            wide,
+            wide,
+            wide,
+            rows,
+            rows,
+            rows,
+            rows,
+            pltpu.VMEM((3, LEN, D), bf16),
+            pltpu.VMEM((2, 2, LEN, LEN), bf16),
+            pltpu.VMEM((4, D, D), bf16),
+            wide,
+            rows,
+            pltpu.VMEM((3, LEN, D), bf16),
+            pltpu.VMEM((LEN, LEN), bf16),
+            pltpu.VMEM((2, D, D), bf16),
+            wide,
+            dma((1,)),
+            dma((13,)),
+            dma((2,)),
+            dma((2,)),
+            dma((1,)),
         ]
-        + Return.sem_shapes(plan),
+        + sems,
         compiler_params=pltpu.CompilerParams(
             collective_id=3, has_side_effects=True, vmem_limit_bytes=VMEM
         ),
-        name="bring_back",
-    )(given, early, targets)[0]
+        name="unattend",
+    )(
+        given,
+        early,
+        targets,
+        grad_sent,
+        hidden,
+        grad_out,
+        tokens,
+        mixed,
+        normed,
+        query,
+        key,
+        value,
+        soft,
+        w_query,
+        w_key,
+        w_value,
+        w_out,
+        grad_gates,
+        gates,
+        routes,
+        w_router,
+        gains,
+        roots,
+    )
+    return out[0], out[3], out[4], out[5], out[6].reshape(HEADS, 4 * NEAR)
 
 
 def per_device(
@@ -1213,94 +1949,86 @@
         return jnp.pad(array.astype(jnp.float32), ((0, 8 - array.shape[0]), (0, 0)))
 
     targets = small(slot_targets(routes, experts_all, plan.capacity, plan.stride))
+    gains, route_rows = small(jnp.stack([gain_one, gain_two])), small(routes.T)
     hot_bucket = offset_buckets()
-    inputs = tokens.astype(jnp.float32)
-    inv_one = lax.rsqrt(jnp.mean(inputs * inputs, axis=-1, keepdims=True) + eps)
-    normed_one = (inputs * inv_one * gain_one).astype(jnp.bfloat16)
-    query_rows = dot(normed_one, w_query).astype(jnp.bfloat16)
-    key_rows = dot(normed_one, w_key).astype(jnp.bfloat16)
-    value_rows = dot(normed_one, w_value).astype(jnp.bfloat16)
     lines = jnp.dot(hot_bucket, bias_table, precision=precise).T
-    grads_in, targets_all, soft, mixed_rows = send_rows(
-        plan, cotangent, targets, query_rows, key_rows, value_rows, lines
+    (
+        grads_in,
+        targets_all,
+        _,
+        soft,
+        mixed_rows,
+        normed_one,
+        query_rows,
+        key_rows,
+        value_rows,
+        hidden,
+        sent,
+        gates,
+        roots,
+    ) = attend(
+        plan,
+        cotangent,
+        targets,
+        tokens,
+        w_query,
+        w_key,
+        w_value,
+        w_out,
+        lines,
+        gains,
+        w_router.T,
+        route_rows,
     )
-    hidden = inputs + dot(mixed_rows, w_out)
-    inv_two = lax.rsqrt(jnp.mean(hidden * hidden, axis=-1, keepdims=True) + eps)
-    normed_two = hidden * inv_two * gain_two
-    sent = normed_two.astype(jnp.bfloat16)
-    logits = jnp.dot(normed_two, w_router, precision=precise)
-    route_hot = (routes[:, :, None] == jnp.arange(experts_all, dtype=jnp.int32)).astype(jnp.float32)
-    chosen = jnp.sum(route_hot * logits[:, None, :], axis=-1)
-    gate_values = jax.nn.softmax(chosen, axis=-1)
     made = run_experts(
-        plan, sent, small(gate_values.T), grads_in, targets_all, w_gate, w_up, w_down
+        plan, sent, gates, grads_in, targets_all, w_gate, w_up, w_down
     )
     grad_sent, grad_gates, rows_in, y_rows, gate_rows, up_rows, act_rows = made[:7]
-    y_early = made[-1]
-    grad_gates = grad_gates[:2].T
-    grad_out = cotangent.astype(jnp.float32)
-    grad_chosen = gate_values * (
-        grad_gates - jnp.sum(gate_values * grad_gates, axis=-1, keepdims=True)
+    branch, low, tokens_grad, few, grad_lines = unattend(
+        plan,
+        y_rows,
+        made[-1],
+        targets_all,
+        grad_sent,
+        hidden,
+        cotangent,
+        tokens,
+        mixed_rows,
+        normed_one,
+        query_rows,
+        key_rows,
+        value_rows,
+        soft,
+        w_query,
+        w_key,
+        w_value,
+        w_out,
+        grad_gates,
+        gates,
+        route_rows,
+        w_router.T,
+        gains,
+        roots,
     )
-    grad_logits = jnp.sum(route_hot * grad_chosen[:, :, None], axis=1)
-    router_grad = contract_first(grad_logits, normed_two, precise)
-    grad_normed_two = contract_last(grad_logits, w_router, precise) + grad_sent
-    gain_two_grad = jnp.sum(grad_normed_two * hidden * inv_two, axis=0)
-    scaled_two = grad_normed_two * gain_two
-    grad_hidden = (
-        grad_out
-        + inv_two * scaled_two
-        - hidden * inv_two**3 * jnp.mean(scaled_two * hidden, axis=-1, keepdims=True)
+    block_out = (hidden + branch).astype(jnp.bfloat16)
+    bias_table_grad = jnp.dot(grad_lines, hot_bucket, precision=precise).T
+    last = jnp.pad(bias_table_grad.reshape(1, BUCKETS * HEADS), ((0, 0), (0, D - BUCKETS * HEADS)))
+    few = lax.dynamic_update_slice(few, last, (experts_all + 2, 0))
+    weight_grads, summed, few = sum_all(
+        plan, gate_rows, up_rows, act_rows, rows_in, grads_in, low, few
     )
-    grad_branch = grad_hidden.astype(jnp.bfloat16)
-    w_out_grad = contract_first(mixed_rows, grad_branch)
-    grad_mixed = contract_last(grad_branch, w_out).astype(jnp.bfloat16)
-    grad_query, grad_key, grad_value, grad_lines = unmix(
-        query_rows, key_rows, value_rows, grad_mixed, soft
-    )
-    bias_table_grad = jnp.dot(grad_lines, hot_bucket, precision=precise).T
-    query_grad = contract_first(normed_one, grad_query)
-    key_grad = contract_first(normed_one, grad_key)
-    value_grad = contract_first(normed_one, grad_value)
-    grad_normed_one = (
-        contract_last(grad_query, w_query)
-        + contract_last(grad_key, w_key)
-        + contract_last(grad_value, w_value)
-    )
-    gain_one_grad = jnp.sum(grad_normed_one * inputs * inv_one, axis=0)
-    scaled_one = grad_normed_one * gain_one
-    tokens_grad = (
-        grad_hidden
-        + inv_one * scaled_one
-        - inputs * inv_one**3 * jnp.mean(scaled_one * inputs, axis=-1, keepdims=True)
-    )
-    last = jnp.pad(bias_table_grad.reshape(1, BUCKETS * HEADS), ((0, 0), (0, D - BUCKETS * HEADS)))
-    few = jnp.concatenate([router_grad, gain_one_grad[None], gain_two_grad[None], last], axis=0)
-    few = jnp.pad(few, ((0, -few.shape[0] % 16), (0, 0)))
-    low = [
-        item.astype(jnp.bfloat16) for item in (query_grad, key_grad, value_grad, w_out_grad, few)
-    ]
-    low, gate_rows, up_rows, act_rows, y_rows = lax.optimization_barrier(
-        (low, gate_rows, up_rows, act_rows, y_rows)
-    )
-    summed = [item.astype(jnp.float32) for item in lax.psum(low, both)]
-    few = summed[4]
-    branch = bring_back(plan, y_rows, y_early, targets_all)
-    block_out = (hidden + branch).astype(jnp.bfloat16)
-    down_grad = jnp.einsum("xrf,xrd->xfd", act_rows, grads_in, preferred_element_type=jnp.float32)
-    gate_grad = jnp.einsum("xrd,xrf->xdf", rows_in, gate_rows, preferred_element_type=jnp.float32)
-    up_grad = jnp.einsum("xrd,xrf->xdf", rows_in, up_rows, preferred_element_type=jnp.float32)
+    summed = [summed[i].astype(jnp.float32) for i in range(4)]
     return (
         block_out,
         tokens_grad,
         few[experts_all],
-        *summed[:4],
+        *summed,
         few[experts_all + 2, : BUCKETS * HEADS].reshape(BUCKETS, HEADS),
         few[experts_all + 1],
         few[:experts_all].T,
-        gate_grad,
-        up_grad,
-        down_grad,
+        jnp.swapaxes(weight_grads[0], 1, 2),
+        jnp.swapaxes(weight_grads[1], 1, 2),
+        weight_grads[2],
     )
 
 

time: 736 us -> 700 us (0.951)
  matrix products: 90 us -> 0.95 us
  Pallas kernels: 583 us -> 648 us
  local copies, waits for them, and re-layouts: 7.69 us -> 23.2 us
  between operations: 14.5 us -> 1.21 us
  waiting for transfers between devices: 11.2 us -> 0 us
  other arithmetic: 24.3 us -> 16 us
    dot_general x18 -> x0, matrix products: 88.5 us -> none  [the longest x5 15.4 us: contract_last(): lax.dot_general(matrix_a, matrix_b, (((1,), (1,)), ((), ())), precision=m...]
    pallas_call x3, Pallas kernels: 305 us -> 363 us  [the longest x1 125 us: unattend(): pl.pallas_call(functools.partial(unattend_body, plan, len(sems)), in_spec...]
    unnamed x52 -> x24, local copies, waits for them, and re-layouts: 2.35 us -> 15.6 us
    psum x1 -> x0, waiting for transfers between devices: 11.2 us -> none  [per_device(): summed = [item.astype(jnp.float32) for item in lax.psum(low, both)]]
    pallas_call x1, Pallas kernels: 278 us -> 285 us  [run_experts(): pl.pallas_call(functools.partial(expert_body, plan, halves, len(d_sems)),...]
  transfers between devices with their start and end apart: 1 -> 0, of which waited for: 1 -> 0; matrix products, arithmetic and copies ran while one was open for 7% -> 0% of each run, Pallas kernels for 20% -> 0%
where the time goes in v4:
time: 700 us; the launch traced here: 689 us
  Pallas kernels  648 us (93%)
  local copies, waits for them, and re-layouts  23.2 us (3%)
  other arithmetic  16 us (2%)
    pallas_call x1, Pallas kernels, run_experts(): pl.pallas_call(functools.partial(expert_body, plan, halves, len(d_sems)),...  285 us
    pallas_call x1, Pallas kernels, unattend(): pl.pallas_call(functools.partial(unattend_body, plan, len(sems)), in_spec...  125 us
    pallas_call x1, Pallas kernels, sum_all(): pl.pallas_call(functools.partial(sum_body, plan), in_specs=in_specs, out_...  119 us
    pallas_call x1, Pallas kernels, attend(): pl.pallas_call(functools.partial(attend_body, plan), in_specs=[ANY] * 7 +...  119 us
    unnamed x24, local copies, waits for them, and re-layouts  15.6 us

profile of v4, /device:TPU:1, one launch (start us, length us, event | category | flops | bytes accessed | tf_op | source)
XLA Modules:
  0.0 689.3 jit_solution(11263098717589519992)
XLA Ops:
  0.7 0.1 broadcast_bitcast_fusion
  0.8 1.3 select_maximum_fusion.refs_8_.refs_21_
  2.1 0.3 convolution_bitcast_fusion.1
  2.4 0.7 reshape.85.refs_7_
  3.1 0.8 copy.29
  3.9 0.2 eq.34
  4.1 0.3 fusion.1
  4.4 0.2 convert_element_type.128
  4.6 0.1 copy.30
  4.7 0.8 convert_bitcast_fusion
  5.5 0.6 pad.17.refs_10_.refs_19_
  6.1 0.6 pad.15.refs_1_
  6.7 118.7 %attend.1 = (bf16[2,2560,1024]{2,1,0:T(8,128)(2,1)}, f32[4,8,8,512]{3,2,1,0:T(8,128)}, bf16[4,512,1024]{2,1,0:T(8,128)(2,1)}, bf16[16,512,512]{2,1,0:T(8,128)(2,...) custom-call(bf16[512,1024]{1,0:T(8,128)(2,1)} %refs_5_.3, ...), custom_call_target="tpu_custom_call" | custom-call | tf_op jit(solution)/shard_map/attend/pallas_call | solution.py:952
  125.4 285.2 %run_experts.1 = (f32[512,1024]{1,0:T(8,128)}, f32[8,512]{1,0:T(8,128)}, bf16[2,2560,1024]{2,1,0:T(8,128)(2,1)}, bf16[2,2560,1024]{2,1,0:T(8,128)(2,1)}, bf16[2,...) custom-call(bf16[512,1024]{1,0:T(8,128)(2,1)} %get-tuple-element.44., ...), custom_call_target="tpu_custom_call" | custom-call | tf_op jit(solution)/shard_map/run_experts/pallas_call | solution.py:1289
  410.6 125.1 %unattend.1 = (f32[512,1024]{1,0:T(8,128)}, bf16[4,2,640,1024]{3,2,1,0:T(8,128)(2,1)}, bf16[2,4,512,1024]{3,2,1,0:T(8,128)(2,1)}, bf16[4,1024,1024]{2,1,0:T(8,12...) custom-call(bf16[2,2560,1024]{2,1,0:T(8,128)(2,1)} %get-tuple-element.48.refs_0_, ...), custom_call_target="tpu_custom_call" | custom-call | tf_op jit(solution)/shard_map/unattend/pallas_call | solution.py:1853
  535.7 3.5 add_convert_fusion
  539.2 0.4 fusion.5
  539.6 0.1 reshape.87
  539.7 1.4 dynamic_update_slice.3.refs_6_
  541.1 119.1 %sum_all.1 = (f32[2,704,1024]{2,1,0:T(8,128)}, f32[2,704,1024]{2,1,0:T(8,128)}, f32[2,704,1024]{2,1,0:T(8,128)}, bf16[4,1024,1024]{2,1,0:T(8,128)(2,1)}, f32[32,1024]{1,0:T(8,128)}) custom-call(bf16[2,2560,704]{2,1,0:T(8,128)(2,1)} %get-tuple-element.61.refs_0_, bf16[2,2560,704]{2,1,0:T(8,128)(2,1)} %get-tuple-element.62.refs_1_, ...), custom_call_target="tpu_custom_call" | custom-call | tf_op jit(solution)/shard_map/sum_all/pallas_call | solution.py:1604
  660.1 0.7 slice_reduce_fusion
  660.9 1.4 fusion.21
  662.3 1.5 slice_bitcast_fusion
  663.8 0.1 reshape_squeeze.3
  663.9 0.7 copy.32
  664.5 10.3 %bitcast_convert_fusion = (f32[1024,1024]{1,0:T(8,128)}, f32[1024,1024]{1,0:T(8,128)}, f32[1024,1024]{1,0:T(8,128)}, f32[1024,1024]{1,0:T(8,128)}) fusion(bf16[4,1024,1024]{2,1,0:T(8,128)(2,1)} %get-tuple-element.69), kind=kLoop, calls=%fused_computation | loop fusion | flops 4194304 | bytes 25165824 | tf_op jit(solution)/shard_map/convert_element_type | solution.py:2020
  674.9 3.2 copy.40
  678.0 2.9 copy.41
  681.0 1.8 copy-done.2
  682.8 2.8 copy.42
  685.5 0.8 slice-done.1
  686.3 2.5 copy.43
  (22 shorter events, 0.1 us)
Async XLA Ops:
  0.6 1.5 copy-start
  535.7 3.5 copy-start.3
  663.9 14.2 %slice-start.2 = ((s8[5767168]{0:T(1024)(128)(4,1)}), s8[1572864]{0:T(1024)(128)(4,1)S(1)}, s32[]{:S(2)}) async-start(s8[5767168]{0:T(1024)(128)(4,1)} %bitcast.46), calls=%async_computation.2 | async-start | bytes 3145728
  664.5 13.5 %slice-start.3 = ((s8[5767168]{0:T(1024)(128)(4,1)}), s8[4194304]{0:T(1024)(128)(4,1)S(1)}, s32[]{:S(2)}) async-start(s8[5767168]{0:T(1024)(128)(4,1)} %bitcast.46), calls=%async_computation.3 | async-start | bytes 8388608
  678.0 4.7 copy-start.2
  678.0 7.5 %slice-start = ((s8[5767168]{0:T(1024)(128)(4,1)}), s8[4194304]{0:T(1024)(128)(4,1)S(1)}, s32[]{:S(2)}) async-start(s8[5767168]{0:T(1024)(128)(4,1)} %bitcast.43), calls=%async_computation | async-start | bytes 8388608
  682.7 3.6 slice-start.1
  682.8 6.1 copy-start.1

commit v5 on v4

--- a/solution.py
+++ b/solution.py
@@ -156,6 +156,7 @@
         self.total = n_h * self.rows
         self.relayed = n_e - 1 if (n_e, n_h) == (8, 4) else n_e
         self.summed = (n_e, n_h) == (8, 4)
+        self.direct = n_h == 4
 
     def place(self):
         return lax.axis_index("expert"), lax.axis_index("hidden")
@@ -535,8 +536,8 @@
         return [
             dma((n_h, n_e)),
             dma((n_h, n_e)),
-            dma((n_h,)),
-            dma((2, n_h)),
+            dma((n_h, 2)),
+            dma((3, n_h, 2)),
             dma((2,)),
             dma((n_h,)),
         ]
@@ -546,6 +547,11 @@
         _, z = self.plan.place()
         found = 0
         for here in range(n_h):
+            if self.plan.direct:
+                order = ((2, 3, 1, 0), (3, 0, 2, 1), (0, 3, 1, 2), (1, 0, 2, 3))[here]
+                for when, there in enumerate(order):
+                    found = found + there * same(z, here, n_h) * same(turn, when, n_h)
+                continue
             others = [there for there in range(n_h) if there != here]
             others.sort(key=lambda d: n_h - 1 - d + here if d > here else d + n_h - 1 - here)
             order = [here] + others if self.own_first else others + [here]
@@ -579,53 +585,81 @@
             self.own.at[chunk],
         )
 
-    def send(self, chunk):
-        for mask in range(1, self.plan.n_e):
-            self.in_plane(chunk, mask).start()
-        self.own_copy(chunk).start()
-
-    def hop(self, turn, goal, way):
+    def send(self, chunk, first=0, end=None):
+        for mask in range(first, self.plan.n_e if end is None else end):
+            if mask == 0:
+                self.own_copy(chunk).start()
+            else:
+                self.in_plane(chunk, mask).start()
+
+    def hop(self, turn, goal, way, half, far=False):
         e, z = self.plan.place()
-        side = (1 - way) // 2
+        side = 2 if far else (1 - way) // 2
         return remote(
-            self.rows_v.at[lax.rem(turn, 2)],
-            self.land.at[side, goal],
-            self.s_send.at[turn],
-            self.s_recv.at[side, goal],
-            (e, z + way),
+            self.rows_v.at[lax.rem(turn, 2), half, :],
+            self.land.at[side, goal, half, :],
+            self.s_send.at[turn, half.start // half.size],
+            self.s_recv.at[side, goal, half.start // half.size],
+            (e, goal if far else z + way),
         )
+
+    def each_hop(self, turn, goal, way, half, act):
+        last = self.plan.n_h - 1
+        _, z = self.plan.place()
+        if not self.plan.direct:
+            act(self.hop(turn, goal, way, half))
+            return
+        far = (z == 0) & (goal == last) if way > 0 else (z == last) & (goal == 0)
+
+        @pl.when(far)
+        def _():
+            act(self.hop(turn, goal, way, half, True))
+
+        @pl.when(jnp.logical_not(far))
+        def _():
+            act(self.hop(turn, goal, way, half))
 
     def each_way(self, goal, act):
         _, z = self.plan.place()
+        last = self.plan.n_h - 1
+        below, above = z > 0, z < last
+        if self.plan.direct:
+            below = below & ((z > 1) | (goal < last))
+            above = above & ((z < last - 1) | (goal > 0))
 
         @pl.when(goal > z)
         def _():
-            act(1, z > 0)
+            act(1, below)
 
         @pl.when(goal < z)
         def _():
-            act(-1, z < self.plan.n_h - 1)
-
-    def take(self, goal, way):
-        side = (1 - way) // 2
+            act(-1, above)
+
+    halves = (pl.ds(0, LEN // 2), pl.ds(LEN // 2, LEN // 2))
+
+    def take(self, goal, way, half, far=False):
+        side = 2 if far else (1 - way) // 2
         e, z = self.plan.place()
         remote(
-            self.rows_v.at[0],
-            self.land.at[side, goal],
-            self.s_send.at[0],
-            self.s_recv.at[side, goal],
-            (e, z - way),
+            self.rows_v.at[0, half, :],
+            self.land.at[side, goal, half, :],
+            self.s_send.at[0, half.start // half.size],
+            self.s_recv.at[side, goal, half.start // half.size],
+            (e, self.plan.n_h - 1 - z if far else z - way),
         ).wait_recv()
-        copy = pltpu.make_async_copy(self.land.at[side, goal], self.sum_v, self.local.at[1])
+        copy = pltpu.make_async_copy(
+            self.land.at[side, goal, half, :], self.sum_v.at[half, :], self.local.at[1]
+        )
         copy.start()
         copy.wait()
-        return self.sum_v[...].astype(jnp.float32)
+        return self.sum_v[half, :].astype(jnp.float32)
 
     def wait_hop(self, turn):
         goal = self.goal(turn)
 
         def act(way, _):
-            self.hop(turn, goal, way).wait_send()
+            for half in self.halves:
+                self.each_hop(turn, goal, way, half, lambda copy: copy.wait_send())
 
         self.each_way(goal, act)
 
@@ -675,14 +709,16 @@
             self.rows_v[buffer] = part.astype(jnp.bfloat16)
 
         def act(way, more):
-            @pl.when(more)
-            def _():
-                so_far = self.take(goal, way)
-                self.rows_v[buffer] = (self.rows_v[buffer].astype(jnp.float32) + so_far).astype(
-                    jnp.bfloat16
-                )
-
-            self.hop(turn, goal, way).start()
+            for half in self.halves:
+
+                @pl.when(more)
+                def _():
+                    so_far = self.take(goal, way, half)
+                    self.rows_v[buffer, half, :] = (
+                        self.rows_v[buffer, half, :].astype(jnp.float32) + so_far
+                    ).astype(jnp.bfloat16)
+
+                self.each_hop(turn, goal, way, half, lambda copy: copy.start())
 
         self.each_way(goal, act)
 
@@ -694,11 +730,20 @@
 
         @pl.when(z > 0)
         def _():
-            self.total[...] += self.take(z, 1)
+            for half in self.halves:
+                self.total[half, :] += self.take(z, 1, half)
 
         @pl.when(z < plan.n_h - 1)
         def _():
-            self.total[...] += self.take(z, -1)
+            for half in self.halves:
+                self.total[half, :] += self.take(z, -1, half)
+
+        if plan.direct:
+
+            @pl.when((z == 0) | (z == plan.n_h - 1))
+            def _():
+                for half in self.halves:
+                    self.total[half, :] += self.take(z, 1, half, True)
 
         copy = pltpu.make_async_copy(self.total, self.out, self.local.at[0])
         copy.start()
@@ -708,20 +753,9 @@
 class ReturnHeld(Return):
     own_first = False
 
-    def __init__(self, plan, given, early, *rest):
+    def __init__(self, plan, given, *rest):
         super().__init__(plan, *rest)
-        self.given, self.early = given, early
-
-    def fetch(self, goal, chunk, buffer):
-        _, z = self.plan.place()
-
-        @pl.when(goal != z)
-        def _():
-            Return.fetch(self, goal, chunk, buffer)
-
-        @pl.when(goal == z)
-        def _():
-            pltpu.make_async_copy(self.early, self.stage.at[buffer], self.local.at[0]).start()
+        self.given = given
 
     def source(self, chunk, mask):
         plan = self.plan
@@ -729,7 +763,7 @@
         return self.given.at[:, pl.ds(at, plan.stride), :]
 
     def sent(self):
-        for chunk in range(1, self.plan.n_h):
+        for chunk in range(self.plan.n_h):
             for mask in range(1, self.plan.n_e):
                 self.in_plane(chunk, mask).wait_send()
 
@@ -906,19 +940,22 @@
         gates_out[2:8, :] = jnp.zeros((6, LEN), jnp.float32)
 
     pairs = HEADS // 2
-    each = -(-pairs // (plan.n_h - 1))
+
+    def mixed_by(chunk):
+        n_h, found = plan.n_h, 0
+        for when in range(1, n_h + 1):
+            share = (0, 0, 6, 8, 8)[when] if n_h == 4 else pairs * when // n_h
+            found = found + same(chunk, when, n_h + 1) * share
+        return found
 
     @pl.loop(0, plan.n_h)
     def _(chunk):
         work.chunk(chunk, lambda at: meta_v[plan.source(z, at)])
         pl.when(chunk == 0)(project)
-        work.relay(chunk)
-
-        @pl.loop(0, each)
-        def _(i):
-            pair = chunk * each + i
-            pl.when(pair < pairs)(lambda: mix_pair(pair))
-
+        pl.when(chunk > 0)(lambda: work.relay(chunk - 1))
+        pl.loop(mixed_by(chunk), mixed_by(chunk + 1))(mix_pair)
+
+    work.relay(plan.n_h - 1)
     soft_copy(pairs - 2).wait()
     soft_copy(pairs - 1).wait()
     route()
@@ -1023,7 +1060,6 @@
         land,
         back,
         land_back,
-        early,
         rows_v,
         meta_v,
         stage,
@@ -1055,8 +1091,7 @@
         gg_recv,
         ggs_send,
         ggs_recv,
-        e_send,
-        e_recv,
+        y_sem,
         *sems,
     ) = refs
     n_e, n_h = plan.n_e, plan.n_h
@@ -1083,7 +1118,7 @@
     @pl.loop(0, ahead)
     def _(chunk):
         work.chunk(chunk, lambda at: target_v[at, 0])
-        work.relay(chunk)
+        pl.when(chunk > 0)(lambda: work.relay(chunk - 1))
 
     for load in loads:
         load.wait()
@@ -1117,7 +1152,7 @@
         return [
             pltpu.make_async_copy(held.at[j], out.at[j, pl.ds(at, plan.rows), :], o_sem.at[i, j])
             for i, (held, out) in enumerate(
-                ((y_v, y_out), (dgate_v, dgate_out), (dup_v, dup_out), (act_v, act_out))
+                ((dgate_v, dgate_out), (dup_v, dup_out), (act_v, act_out))
             )
         ]
 
@@ -1147,9 +1182,30 @@
             for j in range(2):
                 hit = own_slots(j) == aim[k : k + 1, :]
                 line = line + jnp.sum(
-                    jnp.where(hit, dots_v[j, at, 0:1], 0.0), axis=0, keepdims=True
+                    jnp.where(hit, dots_v[chunk, j, at, 0:1], 0.0), axis=0, keepdims=True
                 )
             gg_v[chunk, mask, k : k + 1, :] = line
+
+    def y_copy(chunk):
+        at = pl.ds(pl.multiple_of(chunk * plan.rows, 16), plan.rows)
+        return pltpu.make_async_copy(y_v, y_out.at[:, at, :], y_sem.at[1])
+
+    def make_y(chunk):
+        at = pl.ds(pl.multiple_of(chunk * plan.rows, 16), plan.rows)
+        kept = pltpu.make_async_copy(act_out.at[:, at, :], act_v, y_sem.at[0])
+        kept.start()
+
+        @pl.when(chunk > 0)
+        def _():
+            y_copy(chunk - 1).wait()
+
+        kept.wait()
+
+        @pl.loop(0, 2)
+        def _(j):
+            y_v[j] = dot(act_v[j], wd_v[j]).astype(jnp.bfloat16)
+
+        y_copy(chunk).start()
 
     def step(chunk, index):
         j, half = lax.div(index, halves), lax.rem(index, halves)
@@ -1164,9 +1220,8 @@
         gelu = gate_pre * side
         slope = side + gelu * (1.0 - side) * (1.5957691216057308 + 0.21406444881780075 * square)
         act = gelu * up_pre
-        act_low = act.astype(jnp.bfloat16)
-        dots_v[j, at, :] = jnp.broadcast_to(
-            jnp.sum(act_low.astype(jnp.float32) * raw, axis=1, keepdims=True), (piece, 128)
+        dots_v[chunk, j, at, :] = jnp.broadcast_to(
+            jnp.sum(act * raw, axis=1, keepdims=True), (piece, 128)
         )
         grad_act = gate * raw
         grad_gate = (grad_act * up_pre * slope).astype(jnp.bfloat16)
@@ -1177,7 +1232,13 @@
         dx_v[lax.rem(chunk, dx_v.shape[0]), j, at, :] = (
             dot(grad_gate, wg_v[j]) + dot(grad_up, wu_v[j])
         ).astype(jnp.bfloat16)
-        y_v[j, at, :] = (dot(act_low, wd_v[j]) * gate).astype(jnp.bfloat16)
+
+    split = n_e - n_e // 4
+
+    def now(chunk):
+        if plan.direct:
+            return chunk > 1
+        return (chunk < 1) | (not all_held)
 
     gg_v[...] = jnp.zeros_like(gg_v)
 
@@ -1214,36 +1275,30 @@
         @pl.when(chunk + ahead < n_h)
         def _():
             work.chunk(chunk + ahead, lambda at: target_v[at, 0])
-            work.relay(chunk + ahead)
-
-        @pl.when((chunk < 1) | (not all_held))
-        def _():
-            give.send(chunk)
-
+
+        pl.when(chunk + ahead <= n_h)(lambda: work.relay(chunk + ahead - 1))
         pl.loop(0, n_e)(lambda mask: spread(chunk, mask))
         for mask in range(1, n_e):
             gg_copy(chunk, mask).start()
 
-    def early_copy(mask):
-        at = pl.ds(mask * plan.stride, plan.stride)
-        if mask == 0:
-            return pltpu.make_async_copy(y_out.at[:, at, :], early.at[:, at, :], e_send.at[0])
-        return remote(
-            y_out.at[:, at, :],
-            early.at[:, at, :],
-            e_send.at[mask],
-            e_recv.at[mask],
-            (across(e, mask), z),
-        )
-
-    if all_held:
+        @pl.when(now(chunk))
+        def _():
+            give.send(chunk)
+
+        if plan.direct:
+            pl.when(chunk == 0)(lambda: give.send(0, 0, split))
+
+
+    if plan.direct:
+        give.send(1)
+        give.send(0, split, n_e)
+    elif all_held:
         pl.loop(1, n_h)(lambda turn: give.send(give.chunk_of(give.goal(turn))))
-    for mask in range(n_e):
-        early_copy(mask).start()
-    work.finish()
     for j in range(2):
         for copy in outs(n_h - 1, j):
             copy.wait()
+    make_y(0)
+    work.finish()
 
     @pl.loop(0, n_h)
     def _(turn):
@@ -1259,11 +1314,10 @@
             gg_along(chunk).start()
 
         give.combine(turn, lambda at: target_v[at, 0])
-
+        pl.when(turn + 1 < n_h)(lambda: make_y(turn + 1))
+
+    y_copy(n_h - 1).wait()
     give.sent()
-    early_copy(0).wait()
-    for mask in range(1, n_e):
-        early_copy(mask).wait()
     for chunk in range(n_h):
         for mask in range(1, n_e):
             gg_copy(chunk, mask).wait_send()
@@ -1289,7 +1343,7 @@
     return pl.pallas_call(
         functools.partial(expert_body, plan, halves, len(d_sems)),
         in_specs=[ANY] * 7,
-        out_specs=[ANY, pl.BlockSpec(memory_space=pltpu.VMEM)] + [ANY] * 10,
+        out_specs=[ANY, pl.BlockSpec(memory_space=pltpu.VMEM)] + [ANY] * 9,
         out_shape=[
             shape((LEN, D), f32),
             shape((8, LEN), f32),
@@ -1301,8 +1355,7 @@
             shape((n_h, n_e, 8, LEN), f32),
             shape((n_h, LEN, D), bf16),
             shape((n_h, 2, plan.rows, D), bf16),
-            shape((2, n_h, LEN, D), bf16),
-            shape((2, plan.rows, D), bf16),
+            shape((3, n_h, LEN, D), bf16),
         ],
         scratch_shapes=[
             pltpu.VMEM((2, LEN, D), bf16),
@@ -1325,19 +1378,18 @@
             pltpu.VMEM((n_h, 8, LEN), f32),
             pltpu.VMEM((n_h, 8, LEN), f32),
             pltpu.VMEM((2, plan.rows, 128), f32),
-            pltpu.VMEM((2, plan.rows, 128), f32),
+            pltpu.VMEM((n_h, 2, plan.rows, 128), f32),
             pltpu.VMEM((LEN, D), bf16),
             pltpu.VMEM((LEN, D), f32),
             dma((3,)),
             dma((1,)),
             dma((2,)),
-            dma((4, 2)),
+            dma((3, 2)),
             dma((n_h, n_e)),
             dma((n_h, n_e)),
             dma((n_h,)),
             dma((n_h,)),
-            dma((n_e,)),
-            dma((n_e,)),
+            dma((2,)),
         ]
         + d_sems
         + r_sems,
@@ -1618,7 +1670,6 @@
 def unattend_body(plan, n_r, *refs):
     (
         given,
-        early,
         targets,
         grad_sent,
         hidden,
@@ -1706,9 +1757,9 @@
         load.start()
     soft_copy(0).start()
     greet(plan)
-    give = ReturnHeld(plan, given, early, back, land, branch_out, stage, rows_v, sum_v, total, sems)
+    give = ReturnHeld(plan, given, back, land, branch_out, stage, rows_v, sum_v, total, sems)
     turns = plan.n_h
-    pl.loop(0, turns - 1)(lambda turn: give.send(give.chunk_of(give.goal(turn))))
+    pl.loop(0, turns)(lambda turn: give.send(give.chunk_of(give.goal(turn))))
     targets_in.wait()
 
     def combine(turn):
@@ -1776,10 +1827,11 @@
         lines_out[pair] = jnp.concatenate([found[0][3], found[1][3]], axis=0)
 
     pairs = HEADS // 2
+    first, second = turns // 4, turns // 2
     pl.loop(0, pairs // 2)(unmix_pair)
-    combine(0)
+    pl.loop(0, first)(combine)
     pl.loop(pairs // 2, pairs)(unmix_pair)
-    combine(1)
+    pl.loop(first, second)(combine)
     for load in loads[8:]:
         load.wait()
     for k in range(3):
@@ -1807,8 +1859,7 @@
 
     tokens_copy = pltpu.make_async_copy(grad_hidden_v, tokens_out, out_sem.at[0])
     tokens_copy.start()
-    for turn in range(2, turns):
-        combine(turn)
+    pl.loop(second, turns)(combine)
     give.sent()
     give.finish()
     for i in (1, 2):
@@ -1819,7 +1870,6 @@
 def unattend(
     plan,
     given,
-    early,
     targets,
     grad_sent,
     hidden,
@@ -1852,12 +1902,12 @@
     rows, wide = pltpu.VMEM((LEN, D), bf16), pltpu.VMEM((LEN, D), f32)
     out = pl.pallas_call(
         functools.partial(unattend_body, plan, len(sems)),
-        in_specs=[ANY] * 17 + [vmem] * 6,
+        in_specs=[ANY] * 16 + [vmem] * 6,
         out_specs=[ANY] * 5 + [vmem] * 2,
         out_shape=[
             shape((LEN, D), f32),
             shape((n_h, 2, plan.rows, D), bf16),
-            shape((2, n_h, LEN, D), bf16),
+            shape((3, n_h, LEN, D), bf16),
             shape((4, D, D), bf16),
             shape((LEN, D), f32),
             shape((few, D), f32),
@@ -1897,7 +1947,6 @@
         name="unattend",
     )(
         given,
-        early,
         targets,
         grad_sent,
         hidden,
@@ -1987,7 +2036,6 @@
     branch, low, tokens_grad, few, grad_lines = unattend(
         plan,
         y_rows,
-        made[-1],
         targets_all,
         grad_sent,
         hidden,

time: 700 us -> 672 us (0.960)
  Pallas kernels: 648 us -> 621 us
    pallas_call x1, Pallas kernels: 285 us -> 261 us  [run_experts(): pl.pallas_call(functools.partial(expert_body, plan, halves, len(d_sems)),...]
    pallas_call x1, Pallas kernels: 125 us -> 136 us  [unattend(): pl.pallas_call(functools.partial(unattend_body, plan, len(sems)), in_spec...]
    pallas_call x1, Pallas kernels: 119 us -> 110 us  [sum_all(): pl.pallas_call(functools.partial(sum_body, plan), in_specs=in_specs, out_...]
where the time goes in v5:
time: 672 us; the launch traced here: 662 us
  Pallas kernels  621 us (92%)
  local copies, waits for them, and re-layouts  23.2 us (3%)
  other arithmetic  16 us (2%)
    pallas_call x1, Pallas kernels, run_experts(): pl.pallas_call(functools.partial(expert_body, plan, halves, len(d_sems)),...  261 us
    pallas_call x1, Pallas kernels, unattend(): pl.pallas_call(functools.partial(unattend_body, plan, len(sems)), in_spec...  136 us
    pallas_call x1, Pallas kernels, attend(): pl.pallas_call(functools.partial(attend_body, plan), in_specs=[ANY] * 7 +...  113 us
    pallas_call x1, Pallas kernels, sum_all(): pl.pallas_call(functools.partial(sum_body, plan), in_specs=in_specs, out_...  110 us
    unnamed x24, local copies, waits for them, and re-layouts  15.6 us

profile of v5, /device:TPU:1, one launch (start us, length us, event | category | flops | bytes accessed | tf_op | source)
XLA Modules:
  0.0 661.9 jit_solution(17373594561058130205)
XLA Ops:
  0.7 0.1 broadcast_bitcast_fusion
  0.8 1.3 select_maximum_fusion.refs_8_.refs_20_
  2.1 0.3 convolution_bitcast_fusion.1
  2.4 0.7 reshape.85.refs_7_
  3.1 0.8 copy.29
  3.9 0.2 eq.34
  4.1 0.3 fusion.1
  4.4 0.2 convert_element_type.128
  4.6 0.1 copy.30
  4.7 0.8 convert_bitcast_fusion
  5.5 0.6 pad.17.refs_10_.refs_18_
  6.1 0.6 pad.15.refs_1_
  6.7 113.0 %attend.1 = (bf16[2,2560,1024]{2,1,0:T(8,128)(2,1)}, f32[4,8,8,512]{3,2,1,0:T(8,128)}, bf16[4,512,1024]{2,1,0:T(8,128)(2,1)}, bf16[16,512,512]{2,1,0:T(8,128)(2,...) custom-call(bf16[512,1024]{1,0:T(8,128)(2,1)} %refs_4_.3, ...), custom_call_target="tpu_custom_call" | custom-call | tf_op jit(solution)/shard_map/attend/pallas_call | solution.py:989
  119.7 260.7 %run_experts.1 = (f32[512,1024]{1,0:T(8,128)}, f32[8,512]{1,0:T(8,128)}, bf16[2,2560,1024]{2,1,0:T(8,128)(2,1)}, bf16[2,2560,1024]{2,1,0:T(8,128)(2,1)}, bf16[2,...) custom-call(bf16[512,1024]{1,0:T(8,128)(2,1)} %get-tuple-element.43., ...), custom_call_target="tpu_custom_call" | custom-call | tf_op jit(solution)/shard_map/run_experts/pallas_call | solution.py:1343
  380.4 136.4 %unattend.1 = (f32[512,1024]{1,0:T(8,128)}, bf16[4,2,640,1024]{3,2,1,0:T(8,128)(2,1)}, bf16[3,4,512,1024]{3,2,1,0:T(8,128)(2,1)}, bf16[4,1024,1024]{2,1,0:T(8,12...) custom-call(bf16[2,2560,1024]{2,1,0:T(8,128)(2,1)} %get-tuple-element.47.refs_0_, ...), custom_call_target="tpu_custom_call" | custom-call | tf_op jit(solution)/shard_map/unattend/pallas_call | solution.py:1903
  516.9 3.5 add_convert_fusion
  520.4 0.4 fusion.5
  520.8 0.1 reshape.87
  520.9 1.4 dynamic_update_slice.3.refs_6_
  522.3 110.4 %sum_all.1 = (f32[2,704,1024]{2,1,0:T(8,128)}, f32[2,704,1024]{2,1,0:T(8,128)}, f32[2,704,1024]{2,1,0:T(8,128)}, bf16[4,1024,1024]{2,1,0:T(8,128)(2,1)}, f32[32,1024]{1,0:T(8,128)}) custom-call(bf16[2,2560,704]{2,1,0:T(8,128)(2,1)} %get-tuple-element.59.refs_0_, bf16[2,2560,704]{2,1,0:T(8,128)(2,1)} %get-tuple-element.60.refs_1_, ...), custom_call_target="tpu_custom_call" | custom-call | tf_op jit(solution)/shard_map/sum_all/pallas_call | solution.py:1656
  632.7 0.7 slice_reduce_fusion
  633.5 1.4 fusion.21
  634.9 1.5 slice_bitcast_fusion
  636.4 0.1 reshape_squeeze.3
  636.5 0.7 copy.32
  637.1 10.3 %bitcast_convert_fusion = (f32[1024,1024]{1,0:T(8,128)}, f32[1024,1024]{1,0:T(8,128)}, f32[1024,1024]{1,0:T(8,128)}, f32[1024,1024]{1,0:T(8,128)}) fusion(bf16[4,1024,1024]{2,1,0:T(8,128)(2,1)} %get-tuple-element.67), kind=kLoop, calls=%fused_computation | loop fusion | flops 4194304 | bytes 25165824 | tf_op jit(solution)/shard_map/convert_element_type | solution.py:2068
  647.5 3.2 copy.40
  650.6 2.9 copy.41
  653.6 1.8 copy-done.2
  655.4 2.8 copy.42
  658.1 0.8 slice-done.1
  658.9 2.5 copy.43
  (22 shorter events, 0.1 us)
Async XLA Ops:
  0.6 1.5 copy-start
  516.9 3.5 copy-start.3
  636.5 14.2 %slice-start.2 = ((s8[5767168]{0:T(1024)(128)(4,1)}), s8[1572864]{0:T(1024)(128)(4,1)S(1)}, s32[]{:S(2)}) async-start(s8[5767168]{0:T(1024)(128)(4,1)} %bitcast.46), calls=%async_computation.2 | async-start | bytes 3145728
  637.1 13.5 %slice-start.3 = ((s8[5767168]{0:T(1024)(128)(4,1)}), s8[4194304]{0:T(1024)(128)(4,1)S(1)}, s32[]{:S(2)}) async-start(s8[5767168]{0:T(1024)(128)(4,1)} %bitcast.46), calls=%async_computation.3 | async-start | bytes 8388608
  650.6 4.7 copy-start.2
  650.6 7.5 %slice-start = ((s8[5767168]{0:T(1024)(128)(4,1)}), s8[4194304]{0:T(1024)(128)(4,1)S(1)}, s32[]{:S(2)}) async-start(s8[5767168]{0:T(1024)(128)(4,1)} %bitcast.43), calls=%async_computation | async-start | bytes 8388608
  655.3 3.6 slice-start.1
  655.4 6.1 copy-start.1

commit v6 on v5

--- a/solution.py
+++ b/solution.py
@@ -523,11 +523,21 @@
 class Return:
     own_first = True
 
-    def __init__(self, plan, back, land, out, stage, rows_v, sum_v, total, sems):
+    def __init__(self, plan, back, land, out, stage, rows_v, sum_v, total, slots_in, slots_v, sems):
         self.plan = plan
         self.back, self.land, self.out = back, land, out
         self.stage, self.rows_v, self.sum_v, self.total = stage, rows_v, sum_v, total
-        (self.b_send, self.b_recv, self.s_send, self.s_recv, self.local, self.own) = sems
+        self.slots_in, self.slots_v = slots_in, slots_v
+        (
+            self.b_send,
+            self.b_recv,
+            self.s_send,
+            self.s_recv,
+            self.local,
+            self.own,
+            self.r_send,
+            self.r_recv,
+        ) = sems
 
     @staticmethod
     def sem_shapes(plan):
@@ -540,6 +550,15 @@
             dma((3, n_h, 2)),
             dma((2,)),
             dma((n_h,)),
+            dma((n_h,)),
+            dma((n_h,)),
+        ]
+
+    @staticmethod
+    def slot_shapes(plan):
+        return [
+            pltpu.VMEM((plan.n_h, 2, plan.stride, D), jnp.bfloat16),
+            pltpu.VMEM((2, plan.stride, D), jnp.bfloat16),
         ]
 
     def goal(self, turn):
@@ -586,11 +605,69 @@
         )
 
     def send(self, chunk, first=0, end=None):
-        for mask in range(first, self.plan.n_e if end is None else end):
+        for mask in range(first, self.plan.relayed if end is None else end):
             if mask == 0:
                 self.own_copy(chunk).start()
             else:
                 self.in_plane(chunk, mask).start()
+
+    def relay(self, chunk):
+        plan = self.plan
+        e, z = plan.place()
+        return remote(
+            self.source(chunk, plan.relayed),
+            self.slots_in.at[z],
+            self.r_send.at[chunk],
+            self.r_recv.at[z],
+            (e, plan.source(z, chunk)),
+        )
+
+    def relay_sum(self):
+        plan = self.plan
+        if plan.relayed == plan.n_e:
+            return
+        e, z = plan.place()
+        copy = pltpu.make_async_copy(
+            self.source(0, plan.relayed), self.slots_v, self.local.at[0]
+        )
+        copy.start()
+        copy.wait()
+        for j in range(2):
+            total = self.slots_v[j].astype(jnp.float32)
+            for distance in range(1, plan.n_h):
+                other = lax.rem(z + distance, plan.n_h)
+                if j == 0:
+                    remote(
+                        self.slots_v,
+                        self.slots_in.at[other],
+                        self.r_send.at[0],
+                        self.r_recv.at[other],
+                        (e, other),
+                    ).wait_recv()
+                total = total + self.slots_in[other, j].astype(jnp.float32)
+            self.slots_v[j] = total.astype(jnp.bfloat16)
+        self.relayed_copy().start()
+
+    def relayed_copy(self):
+        plan = self.plan
+        e, z = plan.place()
+        return remote(
+            self.slots_v,
+            self.back.at[0, :, pl.ds(plan.relayed * plan.stride, plan.stride), :],
+            self.b_send.at[0, plan.relayed],
+            self.b_recv.at[0, plan.relayed],
+            (across(e, plan.relayed), z),
+        )
+
+    def wait_sent(self, chunk):
+        plan = self.plan
+        for mask in range(1, plan.relayed):
+            self.in_plane(chunk, mask).wait_send()
+        if plan.relayed < plan.n_e:
+            if chunk == 0:
+                self.relayed_copy().wait_send()
+            else:
+                self.relay(chunk).wait_send()
 
     def hop(self, turn, goal, way, half, far=False):
         e, z = self.plan.place()
@@ -664,12 +741,28 @@
         self.each_way(goal, act)
 
     def fetched(self, chunk, buffer):
-        return pltpu.make_async_copy(self.back.at[chunk], self.stage.at[buffer], self.local.at[0])
+        at = pl.ds(0, self.plan.relayed * self.plan.stride)
+        return pltpu.make_async_copy(
+            self.back.at[chunk, :, at, :], self.stage.at[buffer, :, at, :], self.local.at[0]
+        )
 
     def fetch(self, goal, chunk, buffer):
-        for mask in range(1, self.plan.n_e):
+        plan = self.plan
+        for mask in range(1, plan.relayed):
             self.in_plane(chunk, mask).wait_recv()
         self.own_copy(chunk).wait()
+        if plan.relayed < plan.n_e:
+
+            @pl.when(chunk == 0)
+            def _():
+                self.relayed_copy().wait_recv()
+                at = pl.ds(plan.relayed * plan.stride, plan.stride)
+                copy = pltpu.make_async_copy(
+                    self.back.at[0, :, at, :], self.stage.at[buffer, :, at, :], self.local.at[1]
+                )
+                copy.start()
+                copy.wait()
+
         self.fetched(chunk, buffer).start()
 
     def combine(self, turn, target_of):
@@ -684,7 +777,7 @@
             jnp.concatenate(
                 [
                     slot_hits(plan, slot_base(plan, across(e, mask), j), target)
-                    for mask in range(plan.n_e)
+                    for mask in range(plan.relayed)
                 ],
                 axis=0,
             )
@@ -696,13 +789,20 @@
         def _():
             self.wait_hop(turn - 2)
 
-        part = contract_first(hot[0], self.stage[buffer, 0]) + contract_first(
-            hot[1], self.stage[buffer, 1]
+        count = plan.relayed * plan.stride
+        part = contract_first(hot[0], self.stage[buffer, 0, :count, :]) + contract_first(
+            hot[1], self.stage[buffer, 1, :count, :]
         )
 
         @pl.when(goal == z)
         def _():
             self.total[...] = part
+            if plan.relayed < plan.n_e:
+                for j in range(2):
+                    base = slot_base(plan, across(e, plan.relayed), j)
+                    self.total[...] += contract_first(
+                        slot_hits(plan, base, target), self.stage[buffer, j, count:, :]
+                    )
 
         @pl.when(goal != z)
         def _():
@@ -764,8 +864,7 @@
 
     def sent(self):
         for chunk in range(self.plan.n_h):
-            for mask in range(1, self.plan.n_e):
-                self.in_plane(chunk, mask).wait_send()
+            self.wait_sent(chunk)
 
 
 class ReturnMade(Return):
@@ -787,10 +886,6 @@
             def _():
                 self.wait_sent(chunk - self.ring)
                 self.own_copy(chunk - self.ring).wait()
-
-    def wait_sent(self, chunk):
-        for mask in range(1, self.plan.n_e):
-            self.in_plane(chunk, mask).wait_send()
 
     def sent(self):
         for chunk in range(max(0, self.plan.n_h - self.ring), self.plan.n_h):
@@ -1083,6 +1178,8 @@
         dots_v,
         sum_v,
         total,
+        slots_in,
+        slots_v,
         w_sem,
         t_sem,
         x_sem,
@@ -1109,7 +1206,18 @@
         plan, sent, gates, land, rows_out, meta_out, rows_v, meta_v, stage, sems[:n_d]
     )
     give = ReturnMade(
-        plan, dx_v, back, land_back, total_out, stage, rows_v, sum_v, total, sems[n_d:]
+        plan,
+        dx_v,
+        back,
+        land_back,
+        total_out,
+        stage,
+        rows_v,
+        sum_v,
+        total,
+        slots_in,
+        slots_v,
+        sems[n_d:],
     )
     work.begin()
     targets_in.wait()
@@ -1281,6 +1389,9 @@
         for mask in range(1, n_e):
             gg_copy(chunk, mask).start()
 
+        if plan.relayed < n_e:
+            pl.when(chunk > 0)(lambda: give.relay(chunk).start())
+
         @pl.when(now(chunk))
         def _():
             give.send(chunk)
@@ -1291,7 +1402,8 @@
 
     if plan.direct:
         give.send(1)
-        give.send(0, split, n_e)
+        give.send(0, split, plan.relayed)
+        give.relay_sum()
     elif all_held:
         pl.loop(1, n_h)(lambda turn: give.send(give.chunk_of(give.goal(turn))))
     for j in range(2):
@@ -1381,6 +1493,7 @@
             pltpu.VMEM((n_h, 2, plan.rows, 128), f32),
             pltpu.VMEM((LEN, D), bf16),
             pltpu.VMEM((LEN, D), f32),
+            *Return.slot_shapes(plan),
             dma((3,)),
             dma((1,)),
             dma((2,)),
@@ -1703,6 +1816,8 @@
         target_v,
         sum_v,
         total,
+        slots_in,
+        slots_v,
         grad_sent_v,
         hidden_v,
         grad_out_v,
@@ -1757,8 +1872,12 @@
         load.start()
     soft_copy(0).start()
     greet(plan)
-    give = ReturnHeld(plan, given, back, land, branch_out, stage, rows_v, sum_v, total, sems)
+    give = ReturnHeld(
+        plan, given, back, land, branch_out, stage, rows_v, sum_v, total, slots_in, slots_v, sems
+    )
     turns = plan.n_h
+    if plan.relayed < plan.n_e:
+        pl.loop(1, turns)(lambda chunk: give.relay(chunk).start())
     pl.loop(0, turns)(lambda turn: give.send(give.chunk_of(give.goal(turn))))
     targets_in.wait()
 
@@ -1801,6 +1920,7 @@
         load.wait()
     low_v[1] = contract_first(mixed_v[...], branch_v[...]).astype(bf16)
     low_copy(3).start()
+    give.relay_sum()
     mixed_v[...] = contract_last(branch_v[...], weights_v[3]).astype(bf16)
     for load in loads[5:8]:
         load.wait()
@@ -1919,6 +2039,7 @@
             pltpu.VMEM((n_h, n_e, 8, LEN), f32),
             rows,
             wide,
+            *Return.slot_shapes(plan),
             wide,
             wide,
             rows,

time: 672 us -> 651 us (0.969)
  Pallas kernels: 621 us -> 599 us
    pallas_call x1, Pallas kernels: 261 us -> 251 us  [run_experts(): pl.pallas_call(functools.partial(expert_body, plan, halves, len(d_sems)),...]
    pallas_call x1, Pallas kernels: 136 us -> 129 us  [unattend(): pl.pallas_call(functools.partial(unattend_body, plan, len(sems)), in_spec...]
where the time goes in v6:
time: 651 us; the launch traced here: 641 us
  Pallas kernels  599 us (92%)
  local copies, waits for them, and re-layouts  23.2 us (4%)
  other arithmetic  16 us (2%)
    pallas_call x1, Pallas kernels, run_experts(): pl.pallas_call(functools.partial(expert_body, plan, halves, len(d_sems)),...  251 us
    pallas_call x1, Pallas kernels, unattend(): pl.pallas_call(functools.partial(unattend_body, plan, len(sems)), in_spec...  129 us
    pallas_call x1, Pallas kernels, attend(): pl.pallas_call(functools.partial(attend_body, plan), in_specs=[ANY] * 7 +...  113 us
    pallas_call x1, Pallas kernels, sum_all(): pl.pallas_call(functools.partial(sum_body, plan), in_specs=in_specs, out_...  106 us
    unnamed x24, local copies, waits for them, and re-layouts  15.6 us

profile of v6, /device:TPU:1, one launch (start us, length us, event | category | flops | bytes accessed | tf_op | source)
XLA Modules:
  0.0 640.7 jit_solution(649764796419833689)
XLA Ops:
  0.7 0.1 broadcast_bitcast_fusion
  0.8 1.3 select_maximum_fusion.refs_8_.refs_20_
  2.1 0.3 convolution_bitcast_fusion.1
  2.4 0.7 reshape.85.refs_7_
  3.1 0.8 copy.29
  3.9 0.2 eq.34
  4.1 0.3 fusion.1
  4.4 0.2 convert_element_type.128
  4.6 0.1 copy.30
  4.7 0.8 convert_bitcast_fusion
  5.5 0.6 pad.17.refs_10_.refs_18_
  6.1 0.6 pad.15.refs_1_
  6.7 113.0 %attend.1 = (bf16[2,2560,1024]{2,1,0:T(8,128)(2,1)}, f32[4,8,8,512]{3,2,1,0:T(8,128)}, bf16[4,512,1024]{2,1,0:T(8,128)(2,1)}, bf16[16,512,512]{2,1,0:T(8,128)(2,...) custom-call(bf16[512,1024]{1,0:T(8,128)(2,1)} %refs_4_.3, ...), custom_call_target="tpu_custom_call" | custom-call | tf_op jit(solution)/shard_map/attend/pallas_call | solution.py:1084
  119.7 251.0 %run_experts.1 = (f32[512,1024]{1,0:T(8,128)}, f32[8,512]{1,0:T(8,128)}, bf16[2,2560,1024]{2,1,0:T(8,128)(2,1)}, bf16[2,2560,1024]{2,1,0:T(8,128)(2,1)}, bf16[2,...) custom-call(bf16[512,1024]{1,0:T(8,128)(2,1)} %get-tuple-element.43., ...), custom_call_target="tpu_custom_call" | custom-call | tf_op jit(solution)/shard_map/run_experts/pallas_call | solution.py:1455
  370.7 129.2 %unattend.1 = (f32[512,1024]{1,0:T(8,128)}, bf16[4,2,640,1024]{3,2,1,0:T(8,128)(2,1)}, bf16[3,4,512,1024]{3,2,1,0:T(8,128)(2,1)}, bf16[4,1024,1024]{2,1,0:T(8,12...) custom-call(bf16[2,2560,1024]{2,1,0:T(8,128)(2,1)} %get-tuple-element.47.refs_0_, ...), custom_call_target="tpu_custom_call" | custom-call | tf_op jit(solution)/shard_map/unattend/pallas_call | solution.py:2023
  500.0 3.5 add_convert_fusion
  503.5 0.4 fusion.5
  503.9 0.1 reshape.87
  504.0 1.4 dynamic_update_slice.3.refs_6_
  505.4 106.1 %sum_all.1 = (f32[2,704,1024]{2,1,0:T(8,128)}, f32[2,704,1024]{2,1,0:T(8,128)}, f32[2,704,1024]{2,1,0:T(8,128)}, bf16[4,1024,1024]{2,1,0:T(8,128)(2,1)}, f32[32,1024]{1,0:T(8,128)}) custom-call(bf16[2,2560,704]{2,1,0:T(8,128)(2,1)} %get-tuple-element.59.refs_0_, bf16[2,2560,704]{2,1,0:T(8,128)(2,1)} %get-tuple-element.60.refs_1_, ...), custom_call_target="tpu_custom_call" | custom-call | tf_op jit(solution)/shard_map/sum_all/pallas_call | solution.py:1769
  611.5 0.7 slice_reduce_fusion
  612.2 1.4 fusion.21
  613.7 1.5 slice_bitcast_fusion
  615.1 0.1 reshape_squeeze.3
  615.2 0.7 copy.32
  615.9 10.3 %bitcast_convert_fusion = (f32[1024,1024]{1,0:T(8,128)}, f32[1024,1024]{1,0:T(8,128)}, f32[1024,1024]{1,0:T(8,128)}, f32[1024,1024]{1,0:T(8,128)}) fusion(bf16[4,1024,1024]{2,1,0:T(8,128)(2,1)} %get-tuple-element.67), kind=kLoop, calls=%fused_computation | loop fusion | flops 4194304 | bytes 25165824 | tf_op jit(solution)/shard_map/convert_element_type | solution.py:2189
  626.2 3.2 copy.40
  629.4 2.9 copy.41
  632.3 1.8 copy-done.2
  634.1 2.8 copy.42
  636.9 0.8 slice-done.1
  637.7 2.5 copy.43
  (22 shorter events, 0.1 us)
Async XLA Ops:
  0.6 1.5 copy-start
  499.9 3.5 copy-start.3
  615.2 14.2 %slice-start.2 = ((s8[5767168]{0:T(1024)(128)(4,1)}), s8[1572864]{0:T(1024)(128)(4,1)S(1)}, s32[]{:S(2)}) async-start(s8[5767168]{0:T(1024)(128)(4,1)} %bitcast.46), calls=%async_computation.2 | async-start | bytes 3145728
  615.9 13.5 %slice-start.3 = ((s8[5767168]{0:T(1024)(128)(4,1)}), s8[4194304]{0:T(1024)(128)(4,1)S(1)}, s32[]{:S(2)}) async-start(s8[5767168]{0:T(1024)(128)(4,1)} %bitcast.46), calls=%async_computation.3 | async-start | bytes 8388608
  629.4 4.7 copy-start.2
  629.4 7.5 %slice-start = ((s8[5767168]{0:T(1024)(128)(4,1)}), s8[4194304]{0:T(1024)(128)(4,1)S(1)}, s32[]{:S(2)}) async-start(s8[5767168]{0:T(1024)(128)(4,1)} %bitcast.43), calls=%async_computation | async-start | bytes 8388608
  634.1 3.6 slice-start.1
  634.1 6.1 copy-start.1

commit v7 on v6

--- a/solution.py
+++ b/solution.py
@@ -45,10 +45,6 @@
 
 def dot(matrix_a, matrix_b):
     return jnp.dot(matrix_a, matrix_b, preferred_element_type=jnp.float32)
-
-
-def dot_high(matrix_a, matrix_b):
-    return jnp.dot(matrix_a, matrix_b, precision=precise, preferred_element_type=jnp.float32)
 
 
 def slot_targets(routes, experts_all, capacity, stride):
@@ -822,7 +818,7 @@
 
         self.each_way(goal, act)
 
-    def finish(self):
+    def finish(self, base=None):
         plan = self.plan
         _, z = plan.place()
         for turn in range(plan.n_h - 2, plan.n_h):
@@ -845,7 +841,11 @@
                 for half in self.halves:
                     self.total[half, :] += self.take(z, 1, half, True)
 
-        copy = pltpu.make_async_copy(self.total, self.out, self.local.at[0])
+        if base is None:
+            copy = pltpu.make_async_copy(self.total, self.out, self.local.at[0])
+        else:
+            self.rows_v[0] = (self.total[...] + base[...]).astype(jnp.bfloat16)
+            copy = pltpu.make_async_copy(self.rows_v.at[0], self.out, self.local.at[0])
         copy.start()
         copy.wait()
 
@@ -1780,6 +1780,11 @@
     return out[:3], *lax.psum((low, few), ("expert", "hidden"))
 
 
+def two_parts(array):
+    high = array.astype(jnp.bfloat16)
+    return high, (array - high.astype(jnp.float32)).astype(jnp.bfloat16)
+
+
 def unattend_body(plan, n_r, *refs):
     (
         given,
@@ -1899,7 +1904,11 @@
     for k in range(2):
         chosen = gates[k : k + 1, :] * (grad_gates[k : k + 1, :] - mean)
         grad_logits = grad_logits + jnp.where(numbers == routes[k : k + 1, :], chosen, 0.0)
-    wide_v[...] = contract_first(grad_logits, w_router[...], precise)
+    high, rest = two_parts(grad_logits)
+    wide_v[...] = contract_first(
+        jnp.concatenate([high, high, rest], axis=0),
+        jnp.concatenate([*two_parts(w_router[...]), w_router[...].astype(bf16)], axis=0),
+    )
 
     @pl.loop(0, LEN // tile)
     def _(i):
@@ -1915,12 +1924,12 @@
         branch_v[at, :] = grad.astype(bf16)
         grad_sent_v[at, :] = near * gains[1:2, :]
 
-    few_out[0:experts, :] = dot_high(grad_logits, grad_sent_v[...])
+    normed_high, normed_rest = two_parts(grad_sent_v[...])
+    few_out[0:experts, :] = dot(high, normed_high) + dot(rest, normed_high) + dot(high, normed_rest)
     for load in loads[3:5]:
         load.wait()
     low_v[1] = contract_first(mixed_v[...], branch_v[...]).astype(bf16)
     low_copy(3).start()
-    give.relay_sum()
     mixed_v[...] = contract_last(branch_v[...], weights_v[3]).astype(bf16)
     for load in loads[5:8]:
         load.wait()
@@ -1951,6 +1960,7 @@
     pl.loop(0, pairs // 2)(unmix_pair)
     pl.loop(0, first)(combine)
     pl.loop(pairs // 2, pairs)(unmix_pair)
+    give.relay_sum()
     pl.loop(first, second)(combine)
     for load in loads[8:]:
         load.wait()
@@ -1961,6 +1971,7 @@
             low_copy(0).wait()
         low_v[k % 2] = contract_first(normed_v[...], grad_heads_v[k]).astype(bf16)
         low_copy(k).start()
+    pl.loop(second, turns - 1)(combine)
     wide_v[...] = (
         contract_last(grad_heads_v[0], weights_v[0])
         + contract_last(grad_heads_v[1], weights_v[1])
@@ -1979,9 +1990,9 @@
 
     tokens_copy = pltpu.make_async_copy(grad_hidden_v, tokens_out, out_sem.at[0])
     tokens_copy.start()
-    pl.loop(second, turns)(combine)
+    combine(turns - 1)
     give.sent()
-    give.finish()
+    give.finish(hidden_v)
     for i in (1, 2):
         low_copy(i).wait()
     tokens_copy.wait()
@@ -2025,7 +2036,7 @@
         in_specs=[ANY] * 16 + [vmem] * 6,
         out_specs=[ANY] * 5 + [vmem] * 2,
         out_shape=[
-            shape((LEN, D), f32),
+            shape((LEN, D), bf16),
             shape((n_h, 2, plan.rows, D), bf16),
             shape((3, n_h, LEN, D), bf16),
             shape((4, D, D), bf16),
@@ -2154,7 +2165,7 @@
         plan, sent, gates, grads_in, targets_all, w_gate, w_up, w_down
     )
     grad_sent, grad_gates, rows_in, y_rows, gate_rows, up_rows, act_rows = made[:7]
-    branch, low, tokens_grad, few, grad_lines = unattend(
+    block_out, low, tokens_grad, few, grad_lines = unattend(
         plan,
         y_rows,
         targets_all,
@@ -2179,7 +2190,6 @@
         gains,
         roots,
     )
-    block_out = (hidden + branch).astype(jnp.bfloat16)
     bias_table_grad = jnp.dot(grad_lines, hot_bucket, precision=precise).T
     last = jnp.pad(bias_table_grad.reshape(1, BUCKETS * HEADS), ((0, 0), (0, D - BUCKETS * HEADS)))
     few = lax.dynamic_update_slice(few, last, (experts_all + 2, 0))

time: 651 us -> 643 us (0.988)
  Pallas kernels: 599 us -> 592 us
    pallas_call x1, Pallas kernels: 129 us -> 112 us  [unattend(): pl.pallas_call(functools.partial(unattend_body, plan, len(sems)), in_spec...]
    pallas_call x1, Pallas kernels: 106 us -> 116 us  [sum_all(): pl.pallas_call(functools.partial(sum_body, plan), in_specs=in_specs, out_...]
    unnamed x24 -> x23, local copies, waits for them, and re-layouts: 15.6 us -> 17.8 us
where the time goes in v7:
time: 643 us; the launch traced here: 633 us
  Pallas kernels  592 us (92%)
  local copies, waits for them, and re-layouts  26.2 us (4%)
  other arithmetic  12.5 us (2%)
    pallas_call x1, Pallas kernels, run_experts(): pl.pallas_call(functools.partial(expert_body, plan, halves, len(d_sems)),...  251 us
    pallas_call x1, Pallas kernels, sum_all(): pl.pallas_call(functools.partial(sum_body, plan), in_specs=in_specs, out_...  116 us
    pallas_call x1, Pallas kernels, attend(): pl.pallas_call(functools.partial(attend_body, plan), in_specs=[ANY] * 7 +...  113 us
    pallas_call x1, Pallas kernels, unattend(): pl.pallas_call(functools.partial(unattend_body, plan, len(sems)), in_spec...  112 us
    unnamed x23, local copies, waits for them, and re-layouts  17.8 us

profile of v7, /device:TPU:1, one launch (start us, length us, event | category | flops | bytes accessed | tf_op | source)
XLA Modules:
  0.0 633.2 jit_solution(5270859737008441519)
XLA Ops:
  0.8 1.3 select_maximum_fusion.refs_8_.refs_20_
  2.1 0.3 convolution_bitcast_fusion.1
  2.4 0.7 reshape.85.refs_7_
  3.1 0.8 copy.29
  3.9 0.2 eq.34
  4.1 0.3 fusion.1
  4.4 0.2 convert_element_type.125
  4.6 0.1 copy.30
  4.7 0.8 convert_bitcast_fusion
  5.5 0.6 pad.17.refs_10_.refs_18_
  6.1 0.6 pad.15.refs_1_
  6.7 113.0 %attend.1 = (bf16[2,2560,1024]{2,1,0:T(8,128)(2,1)}, f32[4,8,8,512]{3,2,1,0:T(8,128)}, bf16[4,512,1024]{2,1,0:T(8,128)(2,1)}, bf16[16,512,512]{2,1,0:T(8,128)(2,...) custom-call(bf16[512,1024]{1,0:T(8,128)(2,1)} %refs_4_.3, ...), custom_call_target="tpu_custom_call" | custom-call | tf_op jit(solution)/shard_map/attend/pallas_call | solution.py:1084
  119.7 251.0 %run_experts.1 = (f32[512,1024]{1,0:T(8,128)}, f32[8,512]{1,0:T(8,128)}, bf16[2,2560,1024]{2,1,0:T(8,128)(2,1)}, bf16[2,2560,1024]{2,1,0:T(8,128)(2,1)}, bf16[2,...) custom-call(bf16[512,1024]{1,0:T(8,128)(2,1)} %get-tuple-element.42., ...), custom_call_target="tpu_custom_call" | custom-call | tf_op jit(solution)/shard_map/run_experts/pallas_call | solution.py:1455
  370.7 112.3 %unattend.1 = (bf16[512,1024]{1,0:T(8,128)(2,1)}, bf16[4,2,640,1024]{3,2,1,0:T(8,128)(2,1)}, bf16[3,4,512,1024]{3,2,1,0:T(8,128)(2,1)}, bf16[4,1024,1024]{2,1,0:...) custom-call(bf16[2,2560,1024]{2,1,0:T(8,128)(2,1)} %get-tuple-element.46.refs_0_, ...), custom_call_target="tpu_custom_call" | custom-call | tf_op jit(solution)/shard_map/unattend/pallas_call | solution.py:2034
  483.0 0.8 reshape.86
  483.8 0.4 fusion.5
  484.1 0.1 reshape.87
  484.2 1.4 dynamic_update_slice.3.refs_6_
  485.6 116.1 %sum_all.1 = (f32[2,704,1024]{2,1,0:T(8,128)}, f32[2,704,1024]{2,1,0:T(8,128)}, f32[2,704,1024]{2,1,0:T(8,128)}, bf16[4,1024,1024]{2,1,0:T(8,128)(2,1)}, f32[32,1024]{1,0:T(8,128)}) custom-call(bf16[2,2560,704]{2,1,0:T(8,128)(2,1)} %get-tuple-element.59.refs_0_, bf16[2,2560,704]{2,1,0:T(8,128)(2,1)} %get-tuple-element.60.refs_1_, ...), custom_call_target="tpu_custom_call" | custom-call | tf_op jit(solution)/shard_map/sum_all/pallas_call | solution.py:1769
  601.7 0.7 slice_reduce_fusion
  602.5 1.4 fusion.21
  603.9 1.5 slice_bitcast_fusion
  605.4 0.1 reshape_squeeze.3
  605.5 0.7 copy.32
  606.1 10.3 %bitcast_convert_fusion = (f32[1024,1024]{1,0:T(8,128)}, f32[1024,1024]{1,0:T(8,128)}, f32[1024,1024]{1,0:T(8,128)}, f32[1024,1024]{1,0:T(8,128)}) fusion(bf16[4,1024,1024]{2,1,0:T(8,128)(2,1)} %get-tuple-element.67), kind=kLoop, calls=%fused_computation | loop fusion | flops 4194304 | bytes 25165824 | tf_op jit(solution)/shard_map/convert_element_type | solution.py:2199
  616.5 2.3 copy.41
  618.7 3.2 copy.42
  621.9 2.9 copy.43
  624.8 1.8 copy-done.2
  626.6 2.8 copy.44
  629.4 0.8 slice-done.1
  630.2 2.5 copy.45
  (20 shorter events, 0.1 us)
Async XLA Ops:
  0.6 1.5 copy-start
  605.5 16.4 %slice-start.2 = ((s8[5767168]{0:T(1024)(128)(4,1)}), s8[1572864]{0:T(1024)(128)(4,1)S(1)}, s32[]{:S(2)}) async-start(s8[5767168]{0:T(1024)(128)(4,1)} %bitcast.46), calls=%async_computation.2 | async-start | bytes 3145728
  606.1 15.7 %slice-start.3 = ((s8[5767168]{0:T(1024)(128)(4,1)}), s8[4194304]{0:T(1024)(128)(4,1)S(1)}, s32[]{:S(2)}) async-start(s8[5767168]{0:T(1024)(128)(4,1)} %bitcast.46), calls=%async_computation.3 | async-start | bytes 8388608
  621.9 4.7 copy-start.2
  621.9 7.5 %slice-start = ((s8[5767168]{0:T(1024)(128)(4,1)}), s8[4194304]{0:T(1024)(128)(4,1)S(1)}, s32[]{:S(2)}) async-start(s8[5767168]{0:T(1024)(128)(4,1)} %bitcast.43), calls=%async_computation | async-start | bytes 8388608
  626.6 3.6 slice-start.1
  626.6 6.1 copy-start.1
